TPU v7x, 32 devices: a whole 2x2x4 slice. The times are simulated.
32 devices in a mesh: dp: 4 (over y, x), shard: 8 (over z, core).
Axes of the slice: x: 2, y: 2, z: 4, core: 2. Of those that a mesh axis runs over, the one named last changes fastest.
Arguments:
- training_inputs: bfloat16 [4096, 8192], P(('dp', 'shard')), may hold values from -6 to 6
- training_cotangents: bfloat16 [4096, 8192], P(('dp', 'shard')), may hold values from -6 to 6
- validation_inputs: bfloat16 [1024, 8192], P(('dp', 'shard')), may hold values from -6 to 6
- validation_cotangents: bfloat16 [1024, 8192], P(('dp', 'shard')), may hold values from -6 to 6
- adapter_down: bfloat16 [8192, 64], replicated, may hold values from -0.0625 to 0.0625
- adapter_up: bfloat16 [64, 8192], replicated, may hold values from -0.0625 to 0.0625
- adam_first_moment: bfloat16 [8, 128, 1024], P('shard'), may hold values from -6 to 6
- adam_second_moment: bfloat16 [8, 128, 1024], P('shard'), may hold values from 0.019897461 to 20
- slot_block_index: int32 [8], replicated, may hold values from 0 to 7, each once
- example_lengths: int32 [4, 8, 8], P('dp', 'shard'), may hold values from 1 to 64, 128 in all within a row
- projection_rows: float32 [128, 64], replicated, may hold values from -0.5 to 0.5
- projection_columns: float32 [8192, 128], replicated, may hold values from -0.0625 to 0.0625
Outputs:
- train_dirs: float32 [4, 8, 8, 8192], P('dp', 'shard')
- val_dir: float32 [8192], replicated
- scores: float32 [4, 8, 8], P('dp', 'shard')
Inputs may be any that keep to these rules, and one draw needn't show every extreme that they name: slot_block_index holds every block number once. `example_lengths`: each device's 8 lengths sum to 128; on every device the longest example has exactly 64 tokens.
All inputs are finite; a program needn't handle non-finite values.
Results may differ from a plain program's by a relative error of at most 0.015.
Values may be sent and summed in bfloat16 or wider, within the bound.
No kernel may reach another device: no remote copies, remote signals or barrier semaphores. Data moves between devices by JAX's collectives and lax.ppermute only.
A program may use at most 192 MiB of HBM per device.

v0:
```python
import math

import jax
import jax.numpy as jnp
from jax import lax
from jax.sharding import PartitionSpec as P

beta_first = 0.9
beta_second = 0.999
epsilon = 1e-06


def membership(lengths, total_rows):
    finish = jnp.cumsum(lengths)
    begins = finish - lengths
    position = jnp.arange(total_rows, dtype=jnp.int32)[:, None]
    return ((position >= begins[None, :]) & (position < finish[None, :])).astype(jnp.bfloat16)


def reduced_rank(input_rows, output_cotangent, adapter_down, adapter_up):
    backward_adapter = jnp.dot(
        output_cotangent, adapter_up.T, preferred_element_type=jnp.float32
    ).astype(jnp.bfloat16)
    forward_adapter = jnp.dot(input_rows, adapter_down, preferred_element_type=jnp.float32).astype(
        jnp.bfloat16
    )
    return (backward_adapter, forward_adapter)


def normalize(vector):
    return vector / jnp.sqrt(jnp.mean(vector * vector, axis=-1, keepdims=True) + epsilon)


def project(gradient, projection_rows, columns):
    inner = jnp.dot(gradient, columns, precision=lax.Precision.HIGHEST)
    return jnp.einsum("rj,rk->jk", projection_rows, inner, precision=lax.Precision.HIGHEST)


def token_sum(masked, values):
    return lax.dot_general(
        masked, values, (((0,), (0,)), ((), ())), preferred_element_type=jnp.float32
    )


def body(
    training_inputs,
    training_cotangents,
    validation_inputs,
    validation_cotangents,
    adapter_down,
    adapter_up,
    adam_first_moment,
    adam_second_moment,
    slot_block_index,
    example_lengths,
    projection_rows,
    projection_columns,
):
    local_tokens = training_inputs.shape[0]
    adapter_rank = adapter_down.shape[1]
    example_rows = example_lengths.shape[2]
    block_count = slot_block_index.shape[0]
    block_span_width = adam_first_moment.shape[2]
    table_width = projection_columns.shape[1]
    backward_adapter, forward_adapter = reduced_rank(
        training_inputs, training_cotangents, adapter_down, adapter_up
    )
    member_flag = membership(example_lengths[0, 0], local_tokens)
    masked_backward = (backward_adapter[:, None, :] * member_flag[:, :, None]).reshape(
        local_tokens, example_rows * adapter_rank
    )
    forward_masked = (forward_adapter[:, None, :] * member_flag[:, :, None]).reshape(
        local_tokens, example_rows * adapter_rank
    )
    input_blocks = training_inputs.reshape(local_tokens, block_count, block_span_width)
    cotangent_blocks = training_cotangents.reshape(local_tokens, block_count, block_span_width)
    col_tables = projection_columns.reshape(block_count, block_span_width, table_width)
    first_stat = lax.all_gather(adam_first_moment, "shard", axis=0, tiled=True)
    second_stat = lax.all_gather(adam_second_moment, "shard", axis=0, tiled=True)
    segment_count = first_stat.shape[0]
    input_rows = jnp.take(input_blocks, slot_block_index, axis=1).reshape(
        local_tokens, segment_count * block_span_width
    )
    output_cotangent = jnp.take(cotangent_blocks, slot_block_index, axis=1).reshape(
        local_tokens, segment_count * block_span_width
    )
    top_half = token_sum(masked_backward, input_rows).reshape(
        example_rows, adapter_rank, segment_count, block_span_width
    )
    bottom_half = token_sum(forward_masked, output_cotangent).reshape(
        example_rows, adapter_rank, segment_count, block_span_width
    )
    gradient = jnp.concatenate([top_half, bottom_half], axis=1)
    first_part = first_stat.astype(jnp.float32).transpose(1, 0, 2)[None]
    second_part = second_stat.astype(jnp.float32).transpose(1, 0, 2)[None]
    update = (beta_first * first_part + (1 - beta_first) * gradient) / jnp.sqrt(
        beta_second * second_part + (1 - beta_second) * gradient * gradient
    )
    tables = jnp.take(col_tables, slot_block_index, axis=0)
    folded = jnp.einsum("erny,nyk->erk", update, tables, precision=lax.Precision.HIGHEST)
    projected = jnp.einsum("rj,erk->ejk", projection_rows, folded, precision=lax.Precision.HIGHEST)
    directions = normalize(projected.reshape(example_rows, -1))
    validation_backward, validation_forward = reduced_rank(
        validation_inputs, validation_cotangents, adapter_down, adapter_up
    )
    local_grad = jnp.concatenate(
        [
            token_sum(validation_backward, validation_inputs),
            token_sum(validation_forward, validation_cotangents),
        ],
        axis=0,
    )
    summed = lax.psum(local_grad, ("dp", "shard"))
    val_proj = project(summed, projection_rows, projection_columns)
    val_dir = normalize(val_proj.reshape(-1))
    scores = jnp.sum(directions * val_dir, axis=-1) / math.sqrt(directions.shape[-1])
    return (directions[None, None], val_dir, scores[None, None])


def solution(mesh):
    return jax.shard_map(
        body,
        mesh=mesh,
        in_specs=(
            P(("dp", "shard"), None),
            P(("dp", "shard"), None),
            P(("dp", "shard"), None),
            P(("dp", "shard"), None),
            P(),
            P(),
            P("shard", None, None),
            P("shard", None, None),
            P(),
            P("dp", "shard", None),
            P(),
            P(),
        ),
        out_specs=(P("dp", "shard", None, None), P(), P("dp", "shard", None)),
        check_vma=False,
    )
```

profile of v0, /device:TPU:0, one launch (start us, length us, event | category | flops | bytes accessed | tf_op | source)
XLA Modules:
  0.0 260.5 jit_solution(2124621152248565147)
XLA Ops:
  8.1 3.0 %fusion.24 = f32[64,8192]{1,0:T(8,128)S(1)} fusion(bf16[32,8192]{1,0:T(8,128)(2,1)} %param.16, bf16[32,8192]{1,0:T(8,128)(2,1)} %param.17, bf16[64,8192]{1,0:T(8,128)(2,1)} %param.19), kind=kOutput, calls=%fused_computation.34 | convolution fusion | flops 67110912 | bytes 4194304 | tf_op jit(solution)/shard_map/dot_general | solution.py:40
  11.0 3.9 %fusion.25 = f32[64,8192]{1,0:T(8,128)} fusion(bf16[32,8192]{1,0:T(8,128)(2,1)} %param.17, bf16[32,8192]{1,0:T(8,128)(2,1)} %param.16, bf16[8192,64]{0,1:T(8,128)(2,1)S(1)} %copy-done), kind=kOutput, calls=%fused_computation.35 | convolution fusion | flops 67110912 | bytes 4194304 | tf_op jit(solution)/shard_map/dot_general | solution.py:40
  15.0 4.1 %pad_maximum_fusion.2 = f32[128,8192]{1,0:T(8,128)} fusion(f32[64,8192]{1,0:T(8,128)} %fusion.25, f32[64,8192]{1,0:T(8,128)S(1)} %fusion.24), kind=kLoop, calls=%fused_computation.15 | loop fusion | flops 1048576 | bytes 8388608 | tf_op jit(solution)/shard_map/concatenate | solution.py:106
  20.6 2.4 copy.23
  23.0 3.9 %copy.24 = bf16[128,8,1024]{2,0,1:T(8,128)(2,1)} copy(bf16[128,8,1024]{0,2,1:T(8,128)(2,1)} %bitcast.94) | data formatting | bytes 4194304 | tf_op jit(solution)/shard_map/reshape | solution.py:75
  27.0 4.1 %copy.26 = bf16[128,8192]{0,1:T(8,128)(2,1)} copy(bf16[128,8192]{1,0:T(8,128)(2,1)} %param.15) | data formatting | bytes 4194304 | tf_op args[1]
  31.1 4.1 %copy.27 = bf16[128,8,1024]{2,0,1:T(8,128)(2,1)} copy(bf16[128,8,1024]{0,2,1:T(8,128)(2,1)} %bitcast.95) | data formatting | bytes 4194304 | tf_op jit(solution)/shard_map/reshape | solution.py:76
  35.2 3.6 %gather_fusion.1 = bf16[8,128,1024]{2,1,0:T(8,128)(2,1)} fusion(bf16[128,8,1024]{2,0,1:T(8,128)(2,1)} %copy.24, s32[1024]{0:T(1024)S(1)} %pad_clamp_fusion), kind=kCustom, calls=%fused_computation.clone | custom fusion | bytes 4194336 | tf_op jit(solution)/shard_map/jit(_take)/gather | solution.py:81
  38.8 3.7 %gather_fusion.2 = bf16[8,128,1024]{2,1,0:T(8,128)(2,1)} fusion(bf16[128,8,1024]{2,0,1:T(8,128)(2,1)} %copy.27, s32[1024]{0:T(1024)S(1)} %pad_clamp_fusion), kind=kCustom, calls=%fused_computation.1.clone | custom fusion | bytes 4194336 | tf_op jit(solution)/shard_map/jit(_take)/gather | solution.py:84
  42.5 4.7 %select_bitcast_fusion.1 = (bf16[128,8,1024]{2,0,1:T(8,128)(2,1)}, bf16[128,8,1024]{2,0,1:T(8,128)(2,1)}) fusion(bf16[8,128,1024]{2,1,0:T(8,128)(2,1)} %gather_fusion.1, pred[8]{0:T(512)(128)(4,1)S(1)} %compare_and_fusion, bf16[8,128,1024]{2,1,0:T(8,128)(2,1)} %gather_fusion.2), kind=kLoop, calls=%fused_computation.25 | loop fusion | flops 2097152 | bytes 8388616 | tf_op jit(solution)/shard_map/jit(_take)/select_n | solution.py:81
  47.2 3.9 %copy.28 = bf16[128,8,1024]{0,2,1:T(8,128)(2,1)} copy(bf16[128,8,1024]{2,0,1:T(8,128)(2,1)} %get-tuple-element.7) | data formatting | bytes 4194304 | tf_op jit(solution)/shard_map/jit(_take)/select_n | solution.py:84
  51.1 3.9 %copy.25 = bf16[128,8,1024]{0,2,1:T(8,128)(2,1)} copy(bf16[128,8,1024]{2,0,1:T(8,128)(2,1)} %get-tuple-element.6) | data formatting | bytes 4194304 | tf_op jit(solution)/shard_map/jit(_take)/select_n | solution.py:81
  55.1 5.0 %gather_fusion = f32[8,1024,128]{2,1,0:T(8,128)} fusion(f32[8,1024,128]{2,1,0:T(8,128)} %bitcast.93, s32[1024]{0:T(1024)S(1)} %pad_clamp_fusion), kind=kCustom, calls=%fused_computation.2 | custom fusion | bytes 8388640 | tf_op jit(solution)/shard_map/jit(_take)/gather | solution.py:99
  60.3 0.8 convolution_convert_fusion
  61.2 2.7 %convolution_convert_fusion.1 = bf16[128,64]{0,1:T(8,128)(2,1)S(1)} fusion(bf16[128,8192]{1,0:T(8,128)(2,1)} %param.15, bf16[64,8192]{1,0:T(8,128)(2,1)} %param.19), kind=kOutput, calls=%fused_computation.31 | convolution fusion | flops 134225920 | bytes 3162112 | tf_op jit(solution)/shard_map/dot_general | solution.py:21
  63.9 8.5 %fusion.13 = f32[8,64,8,1024]{3,1,2,0:T(8,128)} fusion(bf16[128,8,1024]{0,2,1:T(8,128)(2,1)S(1)} %copy-done.4, bf16[128,64]{0,1:T(8,128)(2,1)S(1)} %convolution_convert_fusion, bf16[128,8]{0,1:T(8,128)(2,1)S(1)} %fusion.38), kind=kOutput, calls=%fused_computation.20 | convolution fusion | flops 1074003968 | bytes 18892800 | tf_op jit(solution)/shard_map/dot_general | solution.py:40
  72.4 8.3 %fusion.15 = f32[8,64,8,1024]{3,1,2,0:T(8,128)} fusion(bf16[128,8,1024]{0,2,1:T(8,128)(2,1)S(1)} %copy-done.5, bf16[128,8]{0,1:T(8,128)(2,1)S(1)} %fusion.38, bf16[128,64]{0,1:T(8,128)(2,1)S(1)} %convolution_convert_fusion.1), kind=kOutput, calls=%fused_computation.22 | convolution fusion | flops 1074003968 | bytes 18892800 | tf_op jit(solution)/shard_map/dot_general | solution.py:40
  80.8 104.0 %all-reduce.2.cloned.1.call-done = f32[128,8192]{1,0:T(8,128)} async-done(((f32[128,8192]{1,0:T(8,128)}), f32[128,8192]{1,0:T(8,128)}) %all-reduce.2.cloned.1.call-update) | async-done | bytes 4194320 | tf_op jit(solution)/shard_map/psum | solution.py:113
  184.7 7.6 %fusion.43 = f32[128,128]{1,0:T(8,128)S(1)} fusion(f32[128,8192]{1,0:T(8,128)} %all-reduce.2.cloned.1.call-done, f32[8192,128]{1,0:T(8,128)} %param.25), kind=kOutput, calls=%fused_computation.66 | convolution fusion | flops 1610612736 | bytes 8454144 | tf_op jit(solution)/shard_map/dot_general | solution.py:35
  192.3 0.8 multiply_reduce_fusion.2
  194.4 4.2 %multiply_bitcast_fusion = f32[128,8,1024]{2,0,1:T(8,128)} fusion(bf16[8,128,1024]{2,1,0:T(8,128)(2,1)} %all-gather.5.cloned.1.call-done), kind=kLoop, calls=%fused_computation.18 | loop fusion | flops 2097152 | bytes 6291456 | tf_op jit(solution)/shard_map/mul | solution.py:97
  198.7 2.3 multiply_bitcast_fusion.1
  201.5 49.4 %fusion.19 = f32[8,128,128]{2,1,0:T(8,128)S(1)} fusion(f32[8,1024,128]{2,1,0:T(8,128)} %gather_fusion, pred[8]{0:T(512)(128)(4,1)S(1)} %compare_and_fusion, f32[8,64,8,1024]{3,1,2,0:T(8,128)} %fusion.13, f32[8,64,8,1024]{3,1,2,0:T(8,128)} %fusion.15, f32[128,8,1024]{2,0,1:T(8,128)S(1)} %copy-done.2, f32[128,8,1024]{2,0,1:T(8,128)S(1)} %multiply_bitcast_fusion.1), kind=kOutput, calls=%fused_computation.28 | convolution fusion | flops 12944670720 | bytes 46661640 | tf_op jit(solution)/shard_map/erny,nyk->erk/dot_general | solution.py:100
  252.3 0.8 broadcast_divide_fusion
  (38 shorter events, 4.3 us)
Async XLA Ops:
  8.0 3.0 %copy-start = (bf16[8192,64]{0,1:T(8,128)(2,1)S(1)}, bf16[8192,64]{0,1:T(8,128)(2,1)}, u32[]{:S(2)}) copy-start(bf16[8192,64]{0,1:T(8,128)(2,1)} %param.18) | copy-start | bytes 3145732
  8.0 176.7 %all-reduce.2.cloned.1.call-start = ((), (), s32[]{:S(2)}) async-start(), calls=%async_computation.2 | async-start | bytes 8388608 | tf_op jit(solution)/shard_map/psum | solution.py:113
  19.0 1.2 copy-start.7
  19.0 1.6 copy-start.3
  19.0 175.4 %all-gather.5.cloned.1.call-start = ((), (), s32[]{:S(2)}) async-start(), calls=%async_computation.1 | async-start | bytes 2359296 | tf_op jit(solution)/shard_map/all_gather | solution.py:79
  19.6 179.1 %all-gather.3.cloned.1.call-start = ((), (), s32[]{:S(2)}) async-start(), calls=%async_computation | async-start | bytes 2359296 | tf_op jit(solution)/shard_map/all_gather | solution.py:78
  55.1 5.0 %copy-start.8 = (s32[1,1,8]{2,1,0:T(1,128)S(1)}, s32[1,1,8]{2,1,0:T(1,128)}, u32[]{:S(2)}) copy-start(s32[1,1,8]{2,1,0:T(1,128)} %param.23) | copy-start | bytes 100
  60.2 3.6 %copy-start.4 = (bf16[128,8,1024]{0,2,1:T(8,128)(2,1)S(1)}, bf16[128,8,1024]{0,2,1:T(8,128)(2,1)}, u32[]{:S(2)}) copy-start(bf16[128,8,1024]{0,2,1:T(8,128)(2,1)} %copy.28) | copy-start | bytes 6291460
  63.9 8.5 %copy-start.5 = (bf16[128,8,1024]{0,2,1:T(8,128)(2,1)S(1)}, bf16[128,8,1024]{0,2,1:T(8,128)(2,1)}, u32[]{:S(2)}) copy-start(bf16[128,8,1024]{0,2,1:T(8,128)(2,1)} %copy.25) | copy-start | bytes 6291460
  80.8 111.6 %copy-start.6 = (f32[128,64]{0,1:T(8,128)S(1)}, f32[128,64]{0,1:T(8,128)}, u32[]{:S(2)}) copy-start(f32[128,64]{0,1:T(8,128)} %param.24) | copy-start | bytes 98308
  198.7 2.8 %copy-start.2 = (f32[128,8,1024]{2,0,1:T(8,128)S(1)}, f32[128,8,1024]{2,0,1:T(8,128)}, u32[]{:S(2)}) copy-start(f32[128,8,1024]{2,0,1:T(8,128)} %multiply_bitcast_fusion) | copy-start | bytes 12582916
  201.5 51.6 %copy-start.1 = (bf16[8192,64]{0,1:T(8,128)(2,1)S(1)}, bf16[8192,64]{0,1:T(8,128)(2,1)}, u32[]{:S(2)}) copy-start(bf16[8192,64]{0,1:T(8,128)(2,1)} %param.18) | copy-start | bytes 3145732
Sparse Core Ops, SparseCore 0:
  19.2 165.5 all-reduce.1
Sparse Core Ops, SparseCore 1:
  21.1 38.2 all-gather.4
  60.8 31.8 all-gather.2
where the time goes:
time: 261 us
  waiting for transfers between devices  105 us (40%)
  matrix products  85.6 us (33%)
  local copies, waits for them, and re-layouts  35.6 us (14%)
  other arithmetic  17.8 us (7%)
  between operations  16.3 us (6%)
    psum x1, waiting for transfers between devices, body(): summed = lax.psum(local_grad, ('dp', 'shard'))  104 us
    dot_general x1, matrix products, body(): jnp.einsum('erny,nyk->erk', update, tables, precision=lax.Precision.HIGHEST)  49.4 us
    dot_general x4, matrix products, token_sum(): lax.dot_general(masked, values, (((0,), (0,)), ((), ())), preferred_eleme...  23.7 us
    dot_general x1, matrix products, project(): inner = jnp.dot(gradient, columns, precision=lax.Precision.HIGHEST)  7.62 us
    unnamed x20, local copies, waits for them, and re-layouts  7.44 us
  transfers between devices with their start and end apart: 3, of which 1 were waited for; matrix products, arithmetic and copies ran while one was open for 28% of the time, Pallas kernels for 0%

commit v1 on v0

v1 whole, which is shorter than its diff:
```python
import functools
import math

import jax
import jax.numpy as jnp
from jax import lax
from jax.experimental import pallas as pl
from jax.experimental.pallas import tpu as pltpu
from jax.sharding import PartitionSpec as P

epsilon = 1e-06
update_scale = 0.1 / math.sqrt(0.001)
HIGHEST = lax.Precision.HIGHEST
TN = (((0,), (0,)), ((), ()))
NT = (((1,), (1,)), ((), ()))


def mm(a, b, dims=(((1,), (0,)), ((), ())), precision=None):
    return lax.dot_general(a, b, dims, precision=precision, preferred_element_type=jnp.float32)


def prepare_kernel(
    lengths, x, g, xv, gv, down, up, columns, rows,
    columns_out, top_out, bottom_out, proj_out,
    back, fwd, vback, vfwd, xc, gc,
):
    step = pl.program_id(0)

    @pl.when(step == 0)
    def _():
        for total in (back, fwd, vback, vfwd, xc, gc):
            total[...] = jnp.zeros_like(total)

    k2 = columns.shape[1]
    exact = columns[...]
    coarse = exact.astype(jnp.bfloat16)
    fine = (exact - coarse.astype(jnp.float32)).astype(jnp.bfloat16)
    table = jnp.concatenate([coarse, fine], axis=1)
    columns_out[...] = table
    back[...] += mm(g[...], up[...], NT)
    fwd[...] += mm(x[...], down[...])
    vback[...] += mm(gv[...], up[...], NT)
    vfwd[...] += mm(xv[...], down[...])
    xc[...] += mm(xv[...], table)
    gc[...] += mm(gv[...], table)

    @pl.when(step == pl.num_programs(0) - 1)
    def _():
        rank = back.shape[1]
        tokens = back.shape[0]
        position = lax.broadcasted_iota(jnp.int32, (rank, tokens), 1)
        back_t = back[...].T
        fwd_t = fwd[...].T
        begin = jnp.int32(0)
        for e in range(lengths.shape[0]):
            finish = begin + lengths[e]
            member = (position >= begin) & (position < finish)
            top_out[pl.ds(e * rank, rank), :] = jnp.where(member, back_t, 0.0).astype(jnp.bfloat16)
            bottom_out[pl.ds(e * rank, rank), :] = jnp.where(member, fwd_t, 0.0).astype(jnp.bfloat16)
            begin = finish
        round_b = vback[...].astype(jnp.bfloat16).astype(jnp.float32)
        round_f = vfwd[...].astype(jnp.bfloat16).astype(jnp.float32)
        inner_top = mm(round_b, xc[:, :k2] + xc[:, k2:], TN, HIGHEST)
        inner_bottom = mm(round_f, gc[:, :k2] + gc[:, k2:], TN, HIGHEST)
        proj_out[...] = mm(rows[pl.ds(0, rank), :], inner_top, TN, HIGHEST) + mm(
            rows[pl.ds(rank, rank), :], inner_bottom, TN, HIGHEST
        )


def prepare(lengths, x, g, xv, gv, down, up, columns, rows):
    tokens, width = x.shape
    val_tokens = xv.shape[0]
    rank = down.shape[1]
    k1, k2 = rows.shape[1], columns.shape[1]
    examples = lengths.shape[0]
    span = 1024
    whole = lambda i: (0, 0)
    across = lambda i: (0, i)
    along = lambda i: (i, 0)
    return pl.pallas_call(
        prepare_kernel,
        grid=(width // span,),
        in_specs=[
            pl.BlockSpec(memory_space=pltpu.SMEM),
            pl.BlockSpec((tokens, span), across),
            pl.BlockSpec((tokens, span), across),
            pl.BlockSpec((val_tokens, span), across),
            pl.BlockSpec((val_tokens, span), across),
            pl.BlockSpec((span, rank), along),
            pl.BlockSpec((rank, span), across),
            pl.BlockSpec((span, k2), along),
            pl.BlockSpec(rows.shape, whole),
        ],
        out_specs=[
            pl.BlockSpec((span, 2 * k2), along),
            pl.BlockSpec((examples * rank, tokens), whole),
            pl.BlockSpec((examples * rank, tokens), whole),
            pl.BlockSpec((k1, k2), whole),
        ],
        out_shape=[
            jax.ShapeDtypeStruct((width, 2 * k2), jnp.bfloat16),
            jax.ShapeDtypeStruct((examples * rank, tokens), jnp.bfloat16),
            jax.ShapeDtypeStruct((examples * rank, tokens), jnp.bfloat16),
            jax.ShapeDtypeStruct((k1, k2), jnp.float32),
        ],
        scratch_shapes=[
            pltpu.VMEM((tokens, rank), jnp.float32),
            pltpu.VMEM((tokens, rank), jnp.float32),
            pltpu.VMEM((val_tokens, rank), jnp.float32),
            pltpu.VMEM((val_tokens, rank), jnp.float32),
            pltpu.VMEM((val_tokens, 2 * k2), jnp.float32),
            pltpu.VMEM((val_tokens, 2 * k2), jnp.float32),
        ],
        compiler_params=pltpu.CompilerParams(vmem_limit_bytes=32 * 1024 * 1024),
        cost_estimate=pl.CostEstimate(
            flops=4 * tokens * width * rank, bytes_accessed=14_000_000, transcendentals=0
        ),
        name="prepare",
    )(lengths, x, g, xv, gv, down, up, columns, rows)


def update_kernel(
    slots, x, g, table, moments, top, bottom, rows, val_sum,
    dirs_out, val_out, scores_out,
    update, inner,
):
    step = pl.program_id(0)
    rank = rows.shape[0] // 2
    span = x.shape[1]
    examples = top.shape[0] // rank
    quarter = moments.shape[3]
    members = moments.shape[0]

    @pl.when(step == 0)
    def _():
        inner[...] = jnp.zeros_like(inner)

    cut = min(span, 256)
    for half, (source, masked) in enumerate(((x, top), (g, bottom))):
        for c in range(0, span, cut):
            cols = pl.ds(c, cut)
            grad = mm(masked[...], source[:, cols])
            parts = [
                moments[q, 0, :, :, cols].astype(jnp.float32)
                for q in range(half * members // 2, (half + 1) * members // 2)
            ]
            joined = jnp.concatenate(parts, axis=1)
            first = 9.0 * joined[0]
            second = 999.0 * joined[1]
            shared = first * lax.rsqrt(second)
            coarse = shared.astype(jnp.bfloat16)
            update[pl.ds(examples * rank, rank), cols] = coarse
            update[pl.ds((examples + 1) * rank, rank), cols] = (
                shared - coarse.astype(jnp.float32)
            ).astype(jnp.bfloat16)
            for e in range(examples):
                piece = grad[e * rank : (e + 1) * rank]
                change = (first + piece) * lax.rsqrt(second + piece * piece) - shared
                update[pl.ds(e * rank, rank), cols] = change.astype(jnp.bfloat16)
        inner[half] += mm(update[...], table[...])

    @pl.when(step == pl.num_programs(0) - 1)
    def _():
        k2 = inner.shape[2] // 2
        size = rows.shape[1] * k2
        val = val_sum[...]
        val_dir = val * lax.rsqrt(jnp.sum(val * val) / size + epsilon)
        val_out[...] = val_dir
        upper = rows[pl.ds(0, rank), :] * update_scale
        lower = rows[pl.ds(rank, rank), :] * update_scale

        def projected(e):
            part = pl.ds(e * rank, rank)
            folded = [inner[half, part, :k2] + inner[half, part, k2:] for half in (0, 1)]
            return mm(upper, folded[0], TN, HIGHEST) + mm(lower, folded[1], TN, HIGHEST)

        base = projected(examples) + projected(examples + 1)
        for e in range(examples):
            proj = projected(e) + base
            direction = proj * lax.rsqrt(jnp.sum(proj * proj) / size + epsilon)
            dirs_out[e] = direction
            scores_out[e] = jnp.sum(direction * val_dir) / math.sqrt(size)


def update_project(slots, x, g, table, moments, top, bottom, rows, val_sum):
    tokens, width = x.shape
    members, blocks, _, quarter, span = moments.shape
    k1, k2 = rows.shape[1], table.shape[1] // 2
    rank = rows.shape[0] // 2
    examples = top.shape[0] // rank
    whole2 = lambda i, s: (0, 0)
    return pl.pallas_call(
        update_kernel,
        grid_spec=pltpu.PrefetchScalarGridSpec(
            num_scalar_prefetch=1,
            grid=(blocks,),
            in_specs=[
                pl.BlockSpec((tokens, span), lambda i, s: (0, s[i])),
                pl.BlockSpec((tokens, span), lambda i, s: (0, s[i])),
                pl.BlockSpec((span, 2 * k2), lambda i, s: (s[i], 0)),
                pl.BlockSpec((members, 1, 2, quarter, span), lambda i, s: (0, i, 0, 0, 0)),
                pl.BlockSpec(top.shape, whole2),
                pl.BlockSpec(bottom.shape, whole2),
                pl.BlockSpec(rows.shape, whole2),
                pl.BlockSpec(val_sum.shape, whole2),
            ],
            out_specs=[
                pl.BlockSpec((examples, k1, k2), lambda i, s: (0, 0, 0)),
                pl.BlockSpec((k1, k2), whole2),
                pl.BlockSpec(memory_space=pltpu.SMEM),
            ],
            scratch_shapes=[
                pltpu.VMEM(((examples + 2) * rank, span), jnp.bfloat16),
                pltpu.VMEM((2, (examples + 2) * rank, 2 * k2), jnp.float32),
            ],
        ),
        out_shape=[
            jax.ShapeDtypeStruct((examples, k1, k2), jnp.float32),
            jax.ShapeDtypeStruct((k1, k2), jnp.float32),
            jax.ShapeDtypeStruct((examples,), jnp.float32),
        ],
        compiler_params=pltpu.CompilerParams(vmem_limit_bytes=40 * 1024 * 1024),
        cost_estimate=pl.CostEstimate(
            flops=4 * tokens * width * rank * examples, bytes_accessed=12_000_000, transcendentals=0
        ),
        name="update_project",
    )(slots, x, g, table, moments, top, bottom, rows, val_sum)


def body(
    training_inputs,
    training_cotangents,
    validation_inputs,
    validation_cotangents,
    adapter_down,
    adapter_up,
    adam_first_moment,
    adam_second_moment,
    slot_block_index,
    example_lengths,
    projection_rows,
    projection_columns,
):
    members = lax.axis_size("dp")
    quarter = adam_first_moment.shape[1] // members
    start = lax.axis_index("dp") * quarter
    own = jnp.concatenate(
        [
            lax.dynamic_slice_in_dim(adam_first_moment, start, quarter, axis=1),
            lax.dynamic_slice_in_dim(adam_second_moment, start, quarter, axis=1),
        ],
        axis=0,
    )
    gathered = lax.all_gather(own, ("dp", "shard"), axis=0, tiled=False)
    moments = gathered.reshape((members, lax.axis_size("shard")) + own.shape)
    table, top, bottom, val_part = prepare(
        example_lengths[0, 0],
        training_inputs,
        training_cotangents,
        validation_inputs,
        validation_cotangents,
        adapter_down,
        adapter_up,
        projection_columns,
        projection_rows,
    )
    val_sum = lax.psum(val_part, ("dp", "shard"))
    dirs, val_dir, scores = update_project(
        slot_block_index,
        training_inputs,
        training_cotangents,
        table,
        moments,
        top,
        bottom,
        projection_rows,
        val_sum,
    )
    return (
        dirs.reshape(1, 1, dirs.shape[0], -1),
        val_dir.reshape(-1),
        scores[None, None],
    )


def solution(mesh):
    return jax.shard_map(
        body,
        mesh=mesh,
        in_specs=(
            P(("dp", "shard"), None),
            P(("dp", "shard"), None),
            P(("dp", "shard"), None),
            P(("dp", "shard"), None),
            P(),
            P(),
            P("shard", None, None),
            P("shard", None, None),
            P(),
            P("dp", "shard", None),
            P(),
            P(),
        ),
        out_specs=(P("dp", "shard", None, None), P(), P("dp", "shard", None)),
        check_vma=False,
    )
```

time: 261 us -> 108 us (0.41)
  waiting for transfers between devices: 105 us -> 5.37 us
  matrix products: 85.6 us -> 0 us
  blocking collectives: 0 us -> 42.9 us
  Pallas kernels: 0 us -> 22.8 us
  other arithmetic: 17.8 us -> 0.67 us
  local copies, waits for them, and re-layouts: 35.6 us -> 21.5 us
    psum x1 -> x0, waiting for transfers between devices: 104 us -> none  [body(): summed = lax.psum(local_grad, ('dp', 'shard'))]
    dot_general x10 -> x0, matrix products: 85.6 us -> none  [the longest x1 49.4 us: body(): jnp.einsum('erny,nyk->erk', update, tables, precision=lax.Precision.HIGHEST)]
    psum x0 -> x1, blocking collectives: none -> 42.9 us  [body(): val_sum = lax.psum(val_part, ('dp', 'shard'))]
    pallas_call x0 -> x2, Pallas kernels: none -> 22.8 us  [the longest x1 17.1 us: update_project(): pl.pallas_call(update_kernel, grid_spec=pltpu.PrefetchScalarGridSpec(num_...]
    gather x3 -> x0, local copies, waits for them, and re-layouts: 12.2 us -> none  [the longest x1 5 us: body(): tables = jnp.take(col_tables, slot_block_index, axis=0)]
    unnamed x20 -> x28, local copies, waits for them, and re-layouts: 7.44 us -> 19.7 us
    select_n x2 -> x0, local copies, waits for them, and re-layouts: 7.87 us -> none  [the longest x1 3.94 us: body(): jnp.take(cotangent_blocks, slot_block_index, axis=1)]
    reshape x3 -> x1, local copies, waits for them, and re-layouts: 8.09 us -> 0.75 us  [body(): dirs.reshape(1, 1, dirs.shape[0], -1)]
  transfers between devices with their start and end apart: 3 -> 1, of which waited for: 1 -> 1; matrix products, arithmetic and copies ran while one was open for 28% -> 3% of each run, Pallas kernels for 0% -> 5%
where the time goes in v1:
time: 108 us; the launch traced here: 107 us
  blocking collectives  42.9 us (40%)
  Pallas kernels  22.8 us (21%)
  local copies, waits for them, and re-layouts  21.5 us (20%)
  between operations  14.1 us (13%)
  waiting for transfers between devices  5.37 us (5%)
    psum x1, blocking collectives, body(): val_sum = lax.psum(val_part, ('dp', 'shard'))  42.9 us
    unnamed x28, local copies, waits for them, and re-layouts  19.7 us
    pallas_call x1, Pallas kernels, update_project(): pl.pallas_call(update_kernel, grid_spec=pltpu.PrefetchScalarGridSpec(num_...  17.1 us
    pallas_call x1, Pallas kernels, prepare(): pl.pallas_call(prepare_kernel, grid=(width // span,), in_specs=[pl.BlockS...  5.7 us
    all_gather x1, waiting for transfers between devices, body(): gathered = lax.all_gather(own, ('dp', 'shard'), axis=0, tiled=False)  5.36 us
  transfers between devices with their start and end apart: 1, of which 1 were waited for; matrix products, arithmetic and copies ran while one was open for 3% of the time, Pallas kernels for 5%

profile of v1, /device:TPU:0, one launch (start us, length us, event | category | flops | bytes accessed | tf_op | source)
XLA Modules:
  0.0 107.3 jit_solution(12800558628138213520)
XLA Ops:
  7.2 0.0 copy-start
  7.2 0.0 all-gather.3.cloned.1.call-start
  7.2 1.0 constant_dynamic-slice_fusion
  8.3 0.7 pad_maximum_fusion
  8.9 0.0 all-gather.3.cloned.1.call-update
  9.0 2.8 %copy.18.down = bf16[8192,64]{1,0:T(8,128)(2,1)} copy(bf16[8192,64]{0,1:T(8,128)(2,1)} %param.16) | data formatting | bytes 2097152 | tf_op args[4]
  11.7 0.8 copy.19.rows
  12.6 0.0 copy-start.1
  12.6 1.6 %copy-done.1 = bf16[128,8192]{1,0:T(8,128)(2,1)S(1)} copy-done((bf16[128,8192]{1,0:T(8,128)(2,1)S(1)}, bf16[128,8192]{1,0:T(8,128)(2,1)}, u32[]{:S(2)}) %copy-start.1) | copy-done | bytes 2097176
  14.2 1.6 %copy-done.3 = bf16[8192,64]{1,0:T(8,128)(2,1)S(1)} copy-done((bf16[8192,64]{1,0:T(8,128)(2,1)S(1)}, bf16[8192,64]{1,0:T(8,128)(2,1)}, u32[]{:S(2)}) %copy-start.3) | copy-done | bytes 1048600
  15.8 2.2 %copy-done.4 = f32[8192,128]{1,0:T(8,128)S(1)} copy-done((f32[8192,128]{1,0:T(8,128)S(1)}, f32[8192,128]{1,0:T(8,128)}, u32[]{:S(2)}) %copy-start.4) | copy-done | bytes 4194328
  18.0 1.0 copy-done.9
  19.0 1.0 copy-done.10
  20.1 0.7 copy-done.11
  20.7 5.7 %prepare.1 = (bf16[8192,256]{1,0:T(8,128)(2,1)S(1)}, bf16[512,128]{1,0:T(8,128)(2,1)S(1)}, bf16[512,128]{1,0:T(8,128)(2,1)S(1)}, f32[64,128]{1,0:T(8,128)S(1)}) custom-call(s32[8]{0:T(128)S(1)} %bitcast.5, bf16[128,8192]{1,0:T(8,128)(2,1)S(1)} %copy-done, bf16[128,8192]{1,0:T(8,128)(2,1)S(1)} %copy-done.1, bf16[32,8192]{1,0:T(8,128)(2,1)S(1)} %copy-done.9, ...), custom_call_target="tpu_custom_call" | custom-call | flops 268435456 | bytes 14000000 | tf_op jit(solution)/shard_map/prepare/pallas_call | solution.py:80
  26.4 0.0 copy-start.6
  26.4 2.0 %copy-done.6 = bf16[8192,256]{1,0:T(8,128)(2,1)} copy-done((bf16[8192,256]{1,0:T(8,128)(2,1)}, bf16[8192,256]{1,0:T(8,128)(2,1)S(1)}, u32[]{:S(2)}) %copy-start.6) | copy-done | bytes 4194328
  28.4 42.9 %psum.7.val_sum = f32[64,128]{1,0:T(8,128)S(1)} all-reduce(f32[64,128]{1,0:T(8,128)S(1)} %get-tuple-element.13), channel_id=1, replica_groups=mesh['dp'=4,'shard'=8] {'dp','shard'}, use_global_device_ids=true, to_apply=%region_0.0 | all-reduce | flops 8192 | bytes 65536 | tf_op jit(solution)/shard_map/psum | solution.py:267
  71.3 5.4 %all-gather.3.cloned.1.call-done = bf16[64,32,1024]{2,1,0:T(8,128)(2,1)} async-done(((bf16[2,32,1024]{2,1,0:T(8,128)(2,1)}), bf16[64,32,1024]{2,1,0:T(8,128)(2,1)}) %all-gather.3.cloned.1.call-update) | async-done | bytes 4194320 | tf_op jit(solution)/shard_map/all_gather | solution.py:254
  76.6 1.6 %copy-done.2 = bf16[128,8192]{1,0:T(8,128)(2,1)S(1)} copy-done((bf16[128,8192]{1,0:T(8,128)(2,1)S(1)}, bf16[128,8192]{1,0:T(8,128)(2,1)}, u32[]{:S(2)}) %copy-start.2) | copy-done | bytes 2097176
  78.2 2.2 %copy-done.5 = bf16[64,32,1024]{2,1,0:T(8,128)(2,1)S(1)} copy-done((bf16[64,32,1024]{2,1,0:T(8,128)(2,1)S(1)}, bf16[64,32,1024]{2,1,0:T(8,128)(2,1)}, u32[]{:S(2)}) %copy-start.5) | copy-done | bytes 4194328
  80.4 2.2 %copy-done.7 = bf16[8192,256]{1,0:T(8,128)(2,1)S(1)} copy-done((bf16[8192,256]{1,0:T(8,128)(2,1)S(1)}, bf16[8192,256]{1,0:T(8,128)(2,1)}, u32[]{:S(2)}) %copy-start.7) | copy-done | bytes 4194328
  82.6 17.1 %update_project.1 = (f32[8,64,128]{2,1,0:T(8,128)S(1)}, f32[64,128]{1,0:T(8,128)}, f32[8]{0:T(128)}) custom-call(s32[8]{0:T(128)S(1)} %copy-done.12, bf16[128,8192]{1,0:T(8,128)(2,1)S(1)} %copy-done, bf16[128,8192]{1,0:T(8,128)(2,1)S(1)} %copy-done.2, bf16[8192,256]{1,0:T(8,128)(2,1)S(1)} %copy-done.7, bf16[4,8,2,32,1024]{4,3,2,1,0:T(8,128)(2,1)S(1)} %bitcast.4, ...), custom_call_target="tpu_custom_call" | custom-call | flops 2147483648 | bytes 12000000 | tf_op jit(solution)/shard_map/update_project/pallas_call | solution.py:192
  99.7 0.8 reshape.16
  (13 shorter events, 0.0 us)
Async XLA Ops:
  7.2 5.4 %copy-start = (bf16[128,8192]{1,0:T(8,128)(2,1)S(1)}, bf16[128,8192]{1,0:T(8,128)(2,1)}, u32[]{:S(2)}) copy-start(bf16[128,8192]{1,0:T(8,128)(2,1)} %x.3) | copy-start | bytes 6291460
  7.2 5.4 %copy-start.8 = (bf16[64,8192]{1,0:T(8,128)(2,1)S(1)}, bf16[64,8192]{1,0:T(8,128)(2,1)}, u32[]{:S(2)}) copy-start(bf16[64,8192]{1,0:T(8,128)(2,1)} %up.1) | copy-start | bytes 3145732
  7.2 69.5 %all-gather.3.cloned.1.call-start = ((), (), s32[]{:S(2)}) async-start(), calls=%async_computation | async-start | bytes 4325376 | tf_op jit(solution)/shard_map/all_gather | solution.py:254
  12.6 1.6 %copy-start.1 = (bf16[128,8192]{1,0:T(8,128)(2,1)S(1)}, bf16[128,8192]{1,0:T(8,128)(2,1)}, u32[]{:S(2)}) copy-start(bf16[128,8192]{1,0:T(8,128)(2,1)} %g.3) | copy-start | bytes 6291460
  14.2 1.6 %copy-start.3 = (bf16[8192,64]{1,0:T(8,128)(2,1)S(1)}, bf16[8192,64]{1,0:T(8,128)(2,1)}, u32[]{:S(2)}) copy-start(bf16[8192,64]{1,0:T(8,128)(2,1)} %copy.18.down) | copy-start | bytes 3145732
  15.8 2.2 %copy-start.4 = (f32[8192,128]{1,0:T(8,128)S(1)}, f32[8192,128]{1,0:T(8,128)}, u32[]{:S(2)}) copy-start(f32[8192,128]{1,0:T(8,128)} %columns.1) | copy-start | bytes 12582916
  18.0 1.0 copy-start.9
  19.0 1.0 copy-start.10
  20.1 0.7 copy-start.11
  20.7 55.9 %copy-start.12 = (s32[8]{0:T(128)S(1)}, s32[8]{0:T(128)}, u32[]{:S(2)}) copy-start(s32[8]{0:T(128)} %slots.1) | copy-start | bytes 100
  26.4 2.0 %copy-start.6 = (bf16[8192,256]{1,0:T(8,128)(2,1)}, bf16[8192,256]{1,0:T(8,128)(2,1)S(1)}, u32[]{:S(2)}) copy-start(bf16[8192,256]{1,0:T(8,128)(2,1)S(1)} %get-tuple-element.10.table) | copy-start | bytes 12582916
  76.6 1.6 %copy-start.2 = (bf16[128,8192]{1,0:T(8,128)(2,1)S(1)}, bf16[128,8192]{1,0:T(8,128)(2,1)}, u32[]{:S(2)}) copy-start(bf16[128,8192]{1,0:T(8,128)(2,1)} %g.3) | copy-start | bytes 6291460
  78.2 2.2 %copy-start.5 = (bf16[64,32,1024]{2,1,0:T(8,128)(2,1)S(1)}, bf16[64,32,1024]{2,1,0:T(8,128)(2,1)}, u32[]{:S(2)}) copy-start(bf16[64,32,1024]{2,1,0:T(8,128)(2,1)} %all-gather.3.cloned.1.call-done) | copy-start | bytes 12582916
  80.4 2.2 %copy-start.7 = (bf16[8192,256]{1,0:T(8,128)(2,1)S(1)}, bf16[8192,256]{1,0:T(8,128)(2,1)}, u32[]{:S(2)}) copy-start(bf16[8192,256]{1,0:T(8,128)(2,1)} %copy-done.6) | copy-start | bytes 12582916
Sparse Core Ops, SparseCore 0:
  11.6 64.9 all-gather.2

commit v2 on v1

v2 whole, which is shorter than its diff:
```python
import functools
import math

import jax
import jax.numpy as jnp
from jax import lax
from jax.experimental import pallas as pl
from jax.experimental.pallas import tpu as pltpu
from jax.sharding import PartitionSpec as P

epsilon = 1e-06
update_scale = 0.1 / math.sqrt(0.001)
HIGHEST = lax.Precision.HIGHEST
NN = (((1,), (0,)), ((), ()))
TN = (((0,), (0,)), ((), ()))
NT = (((1,), (1,)), ((), ()))
VMEM_LIMIT = 56 * 1024 * 1024
ANY = pl.BlockSpec(memory_space=pl.ANY)
SMEM = pl.BlockSpec(memory_space=pltpu.SMEM)


def mm(a, b, dims=NN, precision=None):
    return lax.dot_general(a, b, dims, precision=precision, preferred_element_type=jnp.float32)


def two_terms(exact):
    coarse = exact.astype(jnp.bfloat16)
    fine = (exact - coarse.astype(jnp.float32)).astype(jnp.bfloat16)
    return coarse, fine


def cut_kernel(place, first, second, out, sems):
    width = out.shape[2]
    cols = pl.ds(pl.multiple_of(place[0] * width, width), width)
    copies = [
        pltpu.make_async_copy(source.at[0, :, cols], out.at[i], sems.at[i])
        for i, source in enumerate((first, second))
    ]
    for copy in copies:
        copy.start()
    for copy in copies:
        copy.wait()


def cut_piece(place, first, second, width):
    return pl.pallas_call(
        cut_kernel,
        in_specs=[SMEM, ANY, ANY],
        out_specs=ANY,
        out_shape=jax.ShapeDtypeStruct((2, first.shape[1], width), first.dtype),
        scratch_shapes=[pltpu.SemaphoreType.DMA((2,))],
        compiler_params=pltpu.CompilerParams(vmem_limit_bytes=VMEM_LIMIT),
        name="cut_piece",
    )(place, first, second)


def prepare_kernel(
    lengths, x, g, xv, gv, down_t, up, columns, rows_t,
    top_out, bottom_out, proj_out,
    back, fwd, vback, vfwd, xc, gc,
):
    step = pl.program_id(0)

    @pl.when(step == 0)
    def _():
        for total in (back, fwd, vback, vfwd, xc, gc):
            total[...] = jnp.zeros_like(total)

    k2 = columns.shape[1]
    table = jnp.concatenate(two_terms(columns[...]), axis=1)
    back[...] += mm(g[...], up[...], NT)
    fwd[...] += mm(x[...], down_t[...], NT)
    vback[...] += mm(gv[...], up[...], NT)
    vfwd[...] += mm(xv[...], down_t[...], NT)
    xc[...] += mm(xv[...], table)
    gc[...] += mm(gv[...], table)

    @pl.when(step == pl.num_programs(0) - 1)
    def _():
        tokens, rank = back.shape
        position = lax.broadcasted_iota(jnp.int32, (rank, tokens), 1)
        back_t = back[...].T
        fwd_t = fwd[...].T
        begin = jnp.int32(0)
        for e in range(lengths.shape[0]):
            finish = begin + lengths[e]
            member = (position >= begin) & (position < finish)
            top_out[pl.ds(e * rank, rank), :] = jnp.where(member, back_t, 0.0).astype(jnp.bfloat16)
            bottom_out[pl.ds(e * rank, rank), :] = jnp.where(member, fwd_t, 0.0).astype(jnp.bfloat16)
            begin = finish
        round_b = vback[...].astype(jnp.bfloat16).astype(jnp.float32)
        round_f = vfwd[...].astype(jnp.bfloat16).astype(jnp.float32)
        inner_top = mm(round_b, xc[:, :k2] + xc[:, k2:], TN, HIGHEST)
        inner_bottom = mm(round_f, gc[:, :k2] + gc[:, k2:], TN, HIGHEST)
        inner = jnp.concatenate([inner_top, inner_bottom], axis=0)
        proj_out[...] = mm(rows_t[...], inner, NN, HIGHEST)


def prepare(lengths, x, g, xv, gv, down_t, up, columns, rows_t):
    tokens, width = x.shape
    val_tokens = xv.shape[0]
    rank = up.shape[0]
    k1, k2 = rows_t.shape[0], columns.shape[1]
    examples = lengths.shape[0]
    span = 1024
    whole = lambda i: (0, 0)
    across = lambda i: (0, i)
    along = lambda i: (i, 0)
    return pl.pallas_call(
        prepare_kernel,
        grid=(width // span,),
        in_specs=[
            SMEM,
            pl.BlockSpec((tokens, span), across),
            pl.BlockSpec((tokens, span), across),
            pl.BlockSpec((val_tokens, span), across),
            pl.BlockSpec((val_tokens, span), across),
            pl.BlockSpec((rank, span), across),
            pl.BlockSpec((rank, span), across),
            pl.BlockSpec((span, k2), along),
            pl.BlockSpec(rows_t.shape, whole),
        ],
        out_specs=[
            pl.BlockSpec((examples * rank, tokens), whole),
            pl.BlockSpec((examples * rank, tokens), whole),
            pl.BlockSpec((k1, k2), whole),
        ],
        out_shape=[
            jax.ShapeDtypeStruct((examples * rank, tokens), jnp.bfloat16),
            jax.ShapeDtypeStruct((examples * rank, tokens), jnp.bfloat16),
            jax.ShapeDtypeStruct((k1, k2), jnp.float32),
        ],
        scratch_shapes=[
            pltpu.VMEM((tokens, rank), jnp.float32),
            pltpu.VMEM((tokens, rank), jnp.float32),
            pltpu.VMEM((val_tokens, rank), jnp.float32),
            pltpu.VMEM((val_tokens, rank), jnp.float32),
            pltpu.VMEM((val_tokens, 2 * k2), jnp.float32),
            pltpu.VMEM((val_tokens, 2 * k2), jnp.float32),
        ],
        compiler_params=pltpu.CompilerParams(vmem_limit_bytes=VMEM_LIMIT),
        cost_estimate=pl.CostEstimate(
            flops=4 * tokens * width * rank, bytes_accessed=12_000_000, transcendentals=0
        ),
        name="prepare",
    )(lengths, x, g, xv, gv, down_t, up, columns, rows_t)


def piece_copies(ids, moment_refs, x, g, columns, xs, gs, cs, ms, sems, width):
    copies = []
    for i, (first, second) in enumerate(moment_refs(width)):
        at = pl.multiple_of(ids[i] * width, width)
        cols = pl.ds(at, width)
        copies.append(
            [
                pltpu.make_async_copy(first, ms.at[i, 0], sems.at[i, 0]),
                pltpu.make_async_copy(second, ms.at[i, 1], sems.at[i, 1]),
                pltpu.make_async_copy(x.at[:, cols], xs.at[i], sems.at[i, 2]),
                pltpu.make_async_copy(g.at[:, cols], gs.at[i], sems.at[i, 3]),
                pltpu.make_async_copy(columns.at[cols, :], cs.at[i], sems.at[i, 4]),
            ]
        )
    return copies


def accumulate(ids, moment_refs, x, g, columns, top, bottom, xs, gs, cs, ms, update, inner, sems):
    count, _, width = xs.shape
    rank = ms.shape[2] // 2
    examples = top.shape[0] // rank
    copies = piece_copies(ids, moment_refs, x, g, columns, xs, gs, cs, ms, sems, width)
    for piece in copies:
        for copy in piece:
            copy.start()
    inner[...] = jnp.zeros_like(inner)

    @pl.loop(0, count, step=2)
    def _(i):
        for j in (0, 1):
            for copy in (
                pltpu.make_async_copy(x.at[:, pl.ds(0, width)], xs.at[i + j], sems.at[i + j, 2]),
                pltpu.make_async_copy(g.at[:, pl.ds(0, width)], gs.at[i + j], sems.at[i + j, 3]),
                pltpu.make_async_copy(columns.at[pl.ds(0, width), :], cs.at[i + j], sems.at[i + j, 4]),
                pltpu.make_async_copy(ms.at[0, 0], ms.at[i + j, 0], sems.at[i + j, 0]),
                pltpu.make_async_copy(ms.at[0, 1], ms.at[i + j, 1], sems.at[i + j, 1]),
            ):
                copy.wait()
        terms = [two_terms(cs[i + j]) for j in (0, 1)]
        table = jnp.concatenate(
            [jnp.concatenate([terms[0][k], terms[1][k]], axis=0) for k in (0, 1)], axis=1
        )
        for half, (source, masked) in enumerate(((xs, top), (gs, bottom))):
            for j in (0, 1):
                cols = pl.ds(j * width, width)
                part = pl.ds(half * rank, rank)
                grad = mm(masked[...], source[i + j])
                first = 9.0 * ms[i + j, 0, part, :].astype(jnp.float32)
                second = 999.0 * ms[i + j, 1, part, :].astype(jnp.float32)
                shared = first * lax.rsqrt(second)
                coarse, fine = two_terms(shared)
                update[half, pl.ds(examples * rank, rank), cols] = coarse
                update[half, pl.ds((examples + 1) * rank, rank), cols] = fine
                for e in range(examples):
                    piece = grad[e * rank : (e + 1) * rank]
                    change = (first + piece) * lax.rsqrt(second + piece * piece) - shared
                    update[half, pl.ds(e * rank, rank), cols] = change.astype(jnp.bfloat16)
            inner[half] += mm(update[half], table)


def folded(inner, half, examples, rank, e):
    k2 = inner.shape[2] // 2
    part = pl.ds(e * rank, rank)
    total = inner[half, part, :k2] + inner[half, part, k2:]
    if e == examples:
        part = pl.ds((examples + 1) * rank, rank)
        total = total + inner[half, part, :k2] + inner[half, part, k2:]
    return total


def chunk_kernel(refs_of, n_moments, ids, *refs):
    moments, refs = refs[:n_moments], refs[n_moments:]
    x, g, columns, top, bottom, out, xs, gs, cs, ms, update, inner, sems = refs
    accumulate(
        ids, functools.partial(refs_of, moments), x, g, columns, top, bottom, xs, gs, cs, ms, update, inner, sems
    )
    rank = ms.shape[2] // 2
    examples = top.shape[0] // rank
    for half in (0, 1):
        for e in range(examples + 1):
            out[half, pl.ds(e * rank, rank), :] = folded(inner, half, examples, rank, e)


def last_kernel(refs_of, n_moments, n_partial, ids, *refs):
    moments, refs = refs[:n_moments], refs[n_moments:]
    x, g, columns, top, bottom, rows_t = refs[:6]
    val_parts, refs = refs[6:8], refs[8:]
    partials, refs = refs[:n_partial], refs[n_partial:]
    dirs_out, val_out, scores_out, joined, xs, gs, cs, ms, update, inner, sems = refs
    accumulate(
        ids, functools.partial(refs_of, moments), x, g, columns, top, bottom, xs, gs, cs, ms, update, inner, sems
    )
    rank = ms.shape[2] // 2
    examples = top.shape[0] // rank
    size = rows_t.shape[0] * columns.shape[1]
    val = val_parts[0][...] + val_parts[1][...]
    val_dir = val * lax.rsqrt(jnp.sum(val * val) / size + epsilon)
    val_out[...] = val_dir
    rows = rows_t[...] * update_scale

    k2 = columns.shape[1]
    for e in range(examples + 1):
        for half in (0, 1):
            total = folded(inner, half, examples, rank, e)
            for partial in partials:
                total = total + partial[half, pl.ds(e * rank, rank), :]
            joined[pl.ds(half * rank, rank), pl.ds(e * k2, k2)] = total
    projected = mm(rows, joined[...], NN, HIGHEST)
    base = projected[:, examples * k2 :]
    for e in range(examples):
        proj = projected[:, e * k2 : (e + 1) * k2] + base
        direction = proj * lax.rsqrt(jnp.sum(proj * proj) / size + epsilon)
        dirs_out[e] = direction
        scores_out[e] = jnp.sum(direction * val_dir) / math.sqrt(size)


def chunk(ids, moments, refs_of, width, x, g, columns, top, bottom, last=None):
    count = ids.shape[0]
    tokens = x.shape[0]
    k2 = columns.shape[1]
    rank2 = moments[0].shape[-2]
    rank = rank2 // 2
    examples = top.shape[0] // rank
    scratch = [
        pltpu.VMEM((count, tokens, width), jnp.bfloat16),
        pltpu.VMEM((count, tokens, width), jnp.bfloat16),
        pltpu.VMEM((count, width, k2), jnp.float32),
        pltpu.VMEM((count, 2, rank2, width), jnp.bfloat16),
        pltpu.VMEM((2, (examples + 2) * rank, 2 * width), jnp.bfloat16),
        pltpu.VMEM((2, (examples + 2) * rank, 2 * k2), jnp.float32),
        pltpu.SemaphoreType.DMA((count, 5)),
    ]
    vmem = pl.BlockSpec(memory_space=pltpu.VMEM)
    cost = pl.CostEstimate(
        flops=4 * tokens * width * count * rank * examples,
        bytes_accessed=400_000 * count,
        transcendentals=0,
    )
    common = [SMEM] + [ANY] * len(moments) + [ANY, ANY, ANY, vmem, vmem]
    operands = [ids, *moments, x, g, columns, top, bottom]
    params = pltpu.CompilerParams(vmem_limit_bytes=VMEM_LIMIT)
    if last is None:
        return pl.pallas_call(
            functools.partial(chunk_kernel, refs_of, len(moments)),
            in_specs=common,
            out_specs=vmem,
            out_shape=jax.ShapeDtypeStruct((2, (examples + 1) * rank, k2), jnp.float32),
            scratch_shapes=scratch,
            compiler_params=params,
            cost_estimate=cost,
            name="chunk",
        )(*operands)
    rows_t, val_parts, partials = last
    k1 = rows_t.shape[0]
    return pl.pallas_call(
        functools.partial(last_kernel, refs_of, len(moments), len(partials)),
        in_specs=common + [vmem] * (3 + len(partials)),
        out_specs=[vmem, vmem, SMEM],
        out_shape=[
            jax.ShapeDtypeStruct((examples, k1, k2), jnp.float32),
            jax.ShapeDtypeStruct((k1, k2), jnp.float32),
            jax.ShapeDtypeStruct((examples,), jnp.float32),
        ],
        scratch_shapes=[pltpu.VMEM((rank2, (examples + 1) * k2), jnp.float32), *scratch],
        compiler_params=params,
        cost_estimate=cost,
        name="last_chunk",
    )(*operands, rows_t, *val_parts, *partials)


def refs_of_pieces(moments, width):
    return [(piece.at[0], piece.at[1]) for piece in moments]


def refs_of_blocks(moments, width):
    found = []
    for first, second in zip(moments[::2], moments[1::2]):
        for at in range(0, first.shape[2], width):
            cols = pl.ds(at, width)
            found.append((first.at[0, :, cols], second.at[0, :, cols]))
    return found


def refs_of_gathered(moments, width):
    return [(moments[0].at[b], moments[1].at[b]) for b in range(moments[0].shape[0])]


def exchange(value, axis, bits):
    size = lax.axis_size(axis)
    return lax.ppermute(value, axis, [(i, i ^ bits) for i in range(size)])


def body(
    training_inputs,
    training_cotangents,
    validation_inputs,
    validation_cotangents,
    adapter_down,
    adapter_up,
    adam_first_moment,
    adam_second_moment,
    slot_block_index,
    example_lengths,
    projection_rows,
    projection_columns,
):
    groups = lax.axis_size("dp")
    shards = lax.axis_size("shard")
    block_width = adam_first_moment.shape[2]
    width = block_width // groups
    stepwise = groups == 4 and shards == 8 and width % 128 == 0
    group = lax.axis_index("dp").astype(jnp.int32)
    shard = lax.axis_index("shard").astype(jnp.int32)
    rows_t = projection_rows.T
    prepared = prepare(
        example_lengths[0, 0],
        training_inputs,
        training_cotangents,
        validation_inputs,
        validation_cotangents,
        adapter_down.T,
        adapter_up,
        projection_columns,
        rows_t,
    )
    top, bottom, val_part = prepared
    operands = (training_inputs, training_cotangents, projection_columns, top, bottom)
    if stepwise:
        own = cut_piece(group[None], adam_first_moment, adam_second_moment, width)
        sibling = [exchange(m, "shard", 1) for m in (adam_first_moment, adam_second_moment)]
        pieces = []
        for hop in (1, 2, 3):
            far = exchange(own, "shard", 2 * hop)
            four = [far] + [exchange(far, "dp", bits) for bits in (1, 2, 3)]
            pieces.append(four + [exchange(piece, "shard", 1) for piece in four])
        total = val_part
        for axis, unit in (("dp", 1), ("shard", 2)):
            others = [exchange(total, axis, unit * bits) for bits in (1, 2, 3)]
            total = (total + others[0]) + (others[1] + others[2])
        val_parts = [total, exchange(total, "shard", 1)]

        quarters = jnp.arange(groups, dtype=jnp.int32)

        def ids_of(hop, order):
            blocks = jnp.stack([slot_block_index[shard ^ (2 * hop)], slot_block_index[shard ^ (2 * hop) ^ 1]])
            return (blocks[:, None] * groups + order[None, :]).reshape(-1)

        partials = [
            chunk(
                ids_of(0, quarters),
                [adam_first_moment, adam_second_moment, *sibling],
                refs_of_blocks,
                width,
                *operands,
            )
        ]
        for hop in (1, 2):
            partials.append(chunk(ids_of(hop, group ^ quarters), pieces[hop - 1], refs_of_pieces, width, *operands))
        dirs, val_dir, scores = chunk(
            ids_of(3, group ^ quarters),
            pieces[2],
            refs_of_pieces,
            width,
            *operands,
            last=(rows_t, val_parts, partials),
        )
    else:
        gathered = [
            lax.all_gather(m, "shard", axis=0, tiled=True) for m in (adam_first_moment, adam_second_moment)
        ]
        val_sum = lax.psum(val_part, ("dp", "shard"))
        dirs, val_dir, scores = chunk(
            slot_block_index,
            gathered,
            refs_of_gathered,
            block_width,
            *operands,
            last=(rows_t, [val_sum, jnp.zeros_like(val_sum)], []),
        )
    return (
        dirs.reshape(1, 1, dirs.shape[0], -1),
        val_dir.reshape(-1),
        scores[None, None],
    )


def solution(mesh):
    return jax.shard_map(
        body,
        mesh=mesh,
        in_specs=(
            P(("dp", "shard"), None),
            P(("dp", "shard"), None),
            P(("dp", "shard"), None),
            P(("dp", "shard"), None),
            P(),
            P(),
            P("shard", None, None),
            P("shard", None, None),
            P(),
            P("dp", "shard", None),
            P(),
            P(),
        ),
        out_specs=(P("dp", "shard", None, None), P(), P("dp", "shard", None)),
        check_vma=False,
    )
```

time: 108 us -> 102 us (0.944)
  blocking collectives: 42.9 us -> 0 us
  starting transfers between devices: 0.04 us -> 29.4 us
  Pallas kernels: 22.8 us -> 49.1 us
  local copies, waits for them, and re-layouts: 21.5 us -> 6.42 us
  between operations: 14.1 us -> 1.07 us
  other arithmetic: 0.67 us -> 6.02 us
  waiting for transfers between devices: 5.37 us -> 9.49 us
    psum x1 -> x0, blocking collectives: 42.9 us -> none  [body(): val_sum = lax.psum(val_part, ('dp', 'shard'))]
    ppermute x0 -> x33, starting transfers between devices: none -> 29.4 us  [exchange(): return lax.ppermute(value, axis, [(i, i ^ bits) for i in range(size)])]
    pallas_call x2 -> x6, Pallas kernels: 22.8 us -> 49.1 us  [the longest x3 24.1 us: chunk(): pl.pallas_call(functools.partial(chunk_kernel, refs_of, len(moments)), in...]
    unnamed x28 -> x62, local copies, waits for them, and re-layouts: 19.7 us -> 1.68 us
    ppermute x0 -> x33, waiting for transfers between devices: none -> 9.49 us  [exchange(): return lax.ppermute(value, axis, [(i, i ^ bits) for i in range(size)])]
    all_gather x1 -> x0, waiting for transfers between devices: 5.36 us -> none  [body(): gathered = lax.all_gather(own, ('dp', 'shard'), axis=0, tiled=False)]
    mul x0 -> x2, other arithmetic: none -> 5.09 us  [ids_of(): return (blocks[:, None] * groups + order[None, :]).reshape(-1)]
    add x0 -> x4, local copies, waits for them, and re-layouts: none -> 2.36 us  [ids_of(): return (blocks[:, None] * groups + order[None, :]).reshape(-1)]
  transfers between devices with their start and end apart: 1 -> 33, of which waited for: 1 -> 6; matrix products, arithmetic and copies ran while one was open for 3% -> 9% of each run, Pallas kernels for 5% -> 29%
where the time goes in v2:
time: 102 us; the launch traced here: 101 us
  Pallas kernels  49.1 us (48%)
  starting transfers between devices  29.4 us (29%)
  waiting for transfers between devices  9.49 us (9%)
  local copies, waits for them, and re-layouts  6.42 us (6%)
  other arithmetic  6.02 us (6%)
  between operations  1.07 us (1%)
    ppermute x33, starting transfers between devices, exchange(): return lax.ppermute(value, axis, [(i, i ^ bits) for i in range(size)])  29.4 us
    pallas_call x3, Pallas kernels, chunk(): pl.pallas_call(functools.partial(chunk_kernel, refs_of, len(moments)), in...  24.1 us
    pallas_call x1, Pallas kernels, chunk(): pl.pallas_call(functools.partial(last_kernel, refs_of, len(moments), len(...  10.3 us
    pallas_call x1, Pallas kernels, prepare(): pl.pallas_call(prepare_kernel, grid=(width // span,), in_specs=[SMEM, pl....  9.56 us
    ppermute x33, waiting for transfers between devices, exchange(): return lax.ppermute(value, axis, [(i, i ^ bits) for i in range(size)])  9.49 us
    pallas_call x1, Pallas kernels, cut_piece(): pl.pallas_call(cut_kernel, in_specs=[SMEM, ANY, ANY], out_specs=ANY, out_...  5.09 us
    mul x2, other arithmetic, ids_of(): return (blocks[:, None] * groups + order[None, :]).reshape(-1)  5.09 us
    add x4, local copies, waits for them, and re-layouts, ids_of(): return (blocks[:, None] * groups + order[None, :]).reshape(-1)  2.36 us
  transfers between devices with their start and end apart: 33, of which 6 were waited for; matrix products, arithmetic and copies ran while one was open for 9% of the time, Pallas kernels for 29%

profile of v2, /device:TPU:0, one launch (start us, length us, event | category | flops | bytes accessed | tf_op | source)
XLA Modules:
  0.0 101.4 jit_solution(11907124829489734326)
XLA Ops:
  0.7 9.6 %prepare.1 = (bf16[512,128]{1,0:T(8,128)(2,1)}, bf16[512,128]{1,0:T(8,128)(2,1)}, f32[64,128]{1,0:T(8,128)}) custom-call(s32[8]{0:T(128)} %bitcast.9, bf16[128,8192]{1,0:T(8,128)(2,1)} %refs_8_.5, bf16[128,8192]{1,0:T(8,128)(2,1)} %refs_9_.5, bf16[32,8192]{1,0:T(8,128)(2,1)} %xv.1, bf16[32,8192]{1,0:T(8,128)(2,1)} %gv.1, bf16[64,8192]{1,0:T(8,128)(2,1)} %bitcast.6, ...), custom_call_target="tpu_custom_call" | custom-call | flops 268435456 | bytes 12000000 | tf_op jit(solution)/shard_map/prepare/pallas_call | solution.py:109
  10.2 4.0 %collective-permute-start.10 = (f32[64,128]{1,0:T(8,128)}, f32[64,128]{1,0:T(8,128)S(1)}, u32[]{:S(2)}, u32[]{:S(2)}) collective-permute-start(f32[64,128]{1,0:T(8,128)} %get-tuple-element.11), channel_id=1, source_target_pairs={{0,24},{8,16},{16,8},{24,0},{1,25},{9,17},{17,9},{25,1},{2,26},{10... | collective-permute-start | bytes 98312 | tf_op jit(solution)/shard_map/ppermute | solution.py:338
  14.8 5.1 %cut_piece.1 = bf16[2,128,256]{2,1,0:T(8,128)(2,1)} custom-call(s32[1]{0:T(128)} %bitcast.place, bf16[1,128,1024]{2,1,0:T(8,128)(2,1)} %refs_0_.1, bf16[1,128,1024]{2,1,0:T(8,128)(2,1)} %refs_1_.1), custom_call_target="tpu_custom_call" | custom-call | tf_op jit(solution)/shard_map/cut_piece/pallas_call | solution.py:46
  19.9 3.1 %collective-permute-start.25 = (bf16[2,128,256]{2,1,0:T(8,128)(2,1)}, bf16[2,128,256]{2,1,0:T(8,128)(2,1)S(1)}, u32[]{:S(2)}, u32[]{:S(2)}) collective-permute-start(bf16[2,128,256]{2,1,0:T(8,128)(2,1)} %cut_piece.1), channel_id=1, source_target_pairs={{0,4},{1,5},{2,6},{3,7},{4,0},{5,1},{6,2},{7,3},{8,12},{9,13},{10,... | collective-permute-start | bytes 393224 | tf_op jit(solution)/shard_map/ppermute | solution.py:338
  23.8 1.6 %collective-permute-start.11 = (f32[64,128]{1,0:T(8,128)S(1)}, f32[64,128]{1,0:T(8,128)S(1)}, u32[]{:S(2)}, u32[]{:S(2)}) collective-permute-start(f32[64,128]{1,0:T(8,128)S(1)} %add_add_fusion.1), channel_id=1, source_target_pairs={{0,2},{1,3},{2,0},{3,1},{4,6},{5,7},{6,4},{7,5},{8,10},{9,11},{10,... | collective-permute-start | bytes 98312 | tf_op jit(solution)/shard_map/ppermute | solution.py:338
  25.8 1.4 %collective-permute-start = (bf16[2,128,256]{2,1,0:T(8,128)(2,1)}, bf16[2,128,256]{2,1,0:T(8,128)(2,1)S(1)}, u32[]{:S(2)}, u32[]{:S(2)}) collective-permute-start(bf16[2,128,256]{2,1,0:T(8,128)(2,1)} %cut_piece.1), channel_id=1, source_target_pairs={{0,6},{1,7},{2,4},{3,5},{4,2},{5,3},{6,0},{7,1},{8,14},{9,15},{10,... | collective-permute-start | bytes 393224 | tf_op jit(solution)/shard_map/ppermute | solution.py:338
  27.9 1.7 %collective-permute-start.12 = (f32[64,128]{1,0:T(8,128)S(1)}, f32[64,128]{1,0:T(8,128)S(1)}, u32[]{:S(2)}, u32[]{:S(2)}) collective-permute-start(f32[64,128]{1,0:T(8,128)S(1)} %add_add_fusion.1), channel_id=1, source_target_pairs={{0,4},{1,5},{2,6},{3,7},{4,0},{5,1},{6,2},{7,3},{8,12},{9,13},{10,... | collective-permute-start | bytes 98312 | tf_op jit(solution)/shard_map/ppermute | solution.py:338
  30.5 1.5 %collective-permute-start.26 = (bf16[2,128,256]{2,1,0:T(8,128)(2,1)S(1)}, bf16[2,128,256]{2,1,0:T(8,128)(2,1)S(1)}, u32[]{:S(2)}, u32[]{:S(2)}) collective-permute-start(bf16[2,128,256]{2,1,0:T(8,128)(2,1)S(1)} %collective-permute-done.25.refs_0_), channel_id=1, source_target_pairs={{0,8},{8,0},{16,24},{24,16},{1,9},{9,1},{17,25},{25,17},{2,10},{10... | collective-permute-start | bytes 393224 | tf_op jit(solution)/shard_map/ppermute | solution.py:338
  32.0 2.5 %add_multiply_fusion = (s32[2]{0:T(128)S(1)}, s32[2]{0:T(128)S(1)}) fusion(s32[1]{0:T(128)} %get-tuple-element.23, s32[1]{0:T(128)} %get-tuple-element.24, s32[1]{0:T(128)} %get-tuple-element.21, s32[1]{0:T(128)} %get-tuple-element.22), kind=kLoop, calls=%fused_computation.3 | loop fusion | flops 8 | bytes 32 | tf_op jit(solution)/shard_map/mul | solution.py:394
  34.5 2.3 %collective-permute-done.12 = f32[64,128]{1,0:T(8,128)S(1)} collective-permute-done((f32[64,128]{1,0:T(8,128)S(1)}, f32[64,128]{1,0:T(8,128)S(1)}, u32[]{:S(2)}, u32[]{:S(2)}) %collective-permute-start.12) | collective-permute-done | bytes 32800 | tf_op jit(solution)/shard_map/ppermute | solution.py:338
  36.7 1.6 %collective-permute-start.27 = (bf16[2,128,256]{2,1,0:T(8,128)(2,1)S(1)}, bf16[2,128,256]{2,1,0:T(8,128)(2,1)S(1)}, u32[]{:S(2)}, u32[]{:S(2)}) collective-permute-start(bf16[2,128,256]{2,1,0:T(8,128)(2,1)S(1)} %collective-permute-done.25.refs_0_), channel_id=1, source_target_pairs={{0,16},{8,24},{16,0},{24,8},{1,17},{9,25},{17,1},{25,9},{2,18},{10... | collective-permute-start | bytes 393224 | tf_op jit(solution)/shard_map/ppermute | solution.py:338
  38.3 1.4 %collective-permute-start.28 = (bf16[2,128,256]{2,1,0:T(8,128)(2,1)S(1)}, bf16[2,128,256]{2,1,0:T(8,128)(2,1)S(1)}, u32[]{:S(2)}, u32[]{:S(2)}) collective-permute-start(bf16[2,128,256]{2,1,0:T(8,128)(2,1)S(1)} %collective-permute-done.25.refs_0_), channel_id=1, source_target_pairs={{0,24},{8,16},{16,8},{24,0},{1,25},{9,17},{17,9},{25,1},{2,26},{10... | collective-permute-start | bytes 393224 | tf_op jit(solution)/shard_map/ppermute | solution.py:338
  40.3 2.6 %add_multiply_fusion.2 = (s32[2]{0:T(128)S(1)}, s32[2]{0:T(128)S(1)}) fusion(s32[1]{0:T(128)} %get-tuple-element.19, s32[1]{0:T(128)} %get-tuple-element.20, s32[1]{0:T(128)} %get-tuple-element.25, s32[1]{0:T(128)} %get-tuple-element.18), kind=kLoop, calls=%fused_computation.5 | loop fusion | flops 8 | bytes 32 | tf_op jit(solution)/shard_map/mul | solution.py:394
  43.6 0.9 collective-permute-done.28.refs_3_
  45.2 3.3 %collective-permute-start.20 = (bf16[2,128,256]{2,1,0:T(8,128)(2,1)S(1)}, bf16[2,128,256]{2,1,0:T(8,128)(2,1)S(1)}, u32[]{:S(2)}, u32[]{:S(2)}) collective-permute-start(bf16[2,128,256]{2,1,0:T(8,128)(2,1)S(1)} %collective-permute-done.17.refs_0_), channel_id=1, source_target_pairs={{0,24},{8,16},{16,8},{24,0},{1,25},{9,17},{17,9},{25,1},{2,26},{10... | collective-permute-start | bytes 393224 | tf_op jit(solution)/shard_map/ppermute | solution.py:338
  49.7 2.6 %collective-permute-done.19.refs_2_ = bf16[2,128,256]{2,1,0:T(8,128)(2,1)S(1)} collective-permute-done((bf16[2,128,256]{2,1,0:T(8,128)(2,1)S(1)}, bf16[2,128,256]{2,1,0:T(8,128)(2,1)S(1)}, u32[]{:S(2)}, u32[]{:S(2)}) %collective-permute-start.19) | collective-permute-done | bytes 131104 | tf_op jit(solution)/shard_map/ppermute | solution.py:338
  52.3 2.0 %collective-permute-start.1 = (bf16[2,128,256]{2,1,0:T(8,128)(2,1)S(1)}, bf16[2,128,256]{2,1,0:T(8,128)(2,1)S(1)}, u32[]{:S(2)}, u32[]{:S(2)}) collective-permute-start(bf16[2,128,256]{2,1,0:T(8,128)(2,1)S(1)} %collective-permute-done.refs_0_), channel_id=1, source_target_pairs={{0,8},{8,0},{16,24},{24,16},{1,9},{9,1},{17,25},{25,17},{2,10},{10... | collective-permute-start | bytes 393224 | tf_op jit(solution)/shard_map/ppermute | solution.py:338
  54.8 1.0 %collective-permute-start.3 = (bf16[2,128,256]{2,1,0:T(8,128)(2,1)S(1)}, bf16[2,128,256]{2,1,0:T(8,128)(2,1)S(1)}, u32[]{:S(2)}, u32[]{:S(2)}) collective-permute-start(bf16[2,128,256]{2,1,0:T(8,128)(2,1)S(1)} %collective-permute-done.refs_0_), channel_id=1, source_target_pairs={{0,24},{8,16},{16,8},{24,0},{1,25},{9,17},{17,9},{25,1},{2,26},{10... | collective-permute-start | bytes 393224 | tf_op jit(solution)/shard_map/ppermute | solution.py:338
  58.0 3.1 %collective-permute-done.2.refs_2_ = bf16[2,128,256]{2,1,0:T(8,128)(2,1)S(1)} collective-permute-done((bf16[2,128,256]{2,1,0:T(8,128)(2,1)S(1)}, bf16[2,128,256]{2,1,0:T(8,128)(2,1)S(1)}, u32[]{:S(2)}, u32[]{:S(2)}) %collective-permute-start.2) | collective-permute-done | bytes 131104 | tf_op jit(solution)/shard_map/ppermute | solution.py:338
  63.0 8.1 %chunk.3.refs_16_ = f32[2,576,128]{2,1,0:T(8,128)} custom-call(s32[8]{0:T(128)} %add.123.ids, bf16[1,128,1024]{2,1,0:T(8,128)(2,1)} %refs_0_.1, bf16[1,128,1024]{2,1,0:T(8,128)(2,1)} %refs_1_.1, bf16[1,128,1024]{2,1,0:T(8,128)(2,1)} %copy-done.2, bf16[1,128,1024]{2,1,0:T(8,128)(2,1)} %copy-done.3, bf16[128,8192]{1,0:T(8,128)(2,1)} %refs_8_.5, ...), custom_call_target="tpu_custom_call" | custom-call | flops 536870912 | bytes 3200000 | tf_op jit(solution)/shard_map/chunk/pallas_call | solution.py:291
  71.2 8.0 %chunk.5.refs_18_ = f32[2,576,128]{2,1,0:T(8,128)} custom-call(s32[8]{0:T(128)} %add.133.ids, bf16[2,128,256]{2,1,0:T(8,128)(2,1)} %copy-done.5, bf16[2,128,256]{2,1,0:T(8,128)(2,1)} %copy-done.7, bf16[2,128,256]{2,1,0:T(8,128)(2,1)} %copy-done.8, bf16[2,128,256]{2,1,0:T(8,128)(2,1)} %copy-done.9, bf16[2,128,256]{2,1,0:T(8,128)(2,1)} %copy-done.11, ...), custom_call_target="tpu_custom_call" | custom-call | flops 536870912 | bytes 3200000 | tf_op jit(solution)/shard_map/chunk/pallas_call | solution.py:291
  80.0 8.0 %chunk.4.refs_17_ = f32[2,576,128]{2,1,0:T(8,128)} custom-call(s32[8]{0:T(128)} %add.128.ids, bf16[2,128,256]{2,1,0:T(8,128)(2,1)} %copy-done.6, bf16[2,128,256]{2,1,0:T(8,128)(2,1)} %copy-done.10, bf16[2,128,256]{2,1,0:T(8,128)(2,1)} %copy-done.12, bf16[2,128,256]{2,1,0:T(8,128)(2,1)} %copy-done.14, bf16[2,128,256]{2,1,0:T(8,128)(2,1)} %copy-done.16, ...), custom_call_target="tpu_custom_call" | custom-call | flops 536870912 | bytes 3200000 | tf_op jit(solution)/shard_map/chunk/pallas_call | solution.py:291
  89.4 10.3 %last_chunk.1 = (f32[8,64,128]{2,1,0:T(8,128)}, f32[64,128]{1,0:T(8,128)}, f32[8]{0:T(128)}) custom-call(s32[8]{0:T(128)} %add.111.ids, bf16[2,128,256]{2,1,0:T(8,128)(2,1)} %copy-done.4, bf16[2,128,256]{2,1,0:T(8,128)(2,1)} %copy-done.13, bf16[2,128,256]{2,1,0:T(8,128)(2,1)} %copy-done.15, bf16[2,128,256]{2,1,0:T(8,128)(2,1)} %copy-done.17, ...), custom_call_target="tpu_custom_call" | custom-call | flops 536870912 | bytes 3200000 | tf_op jit(solution)/shard_map/last_chunk/pallas_call | solution.py:303
  99.7 1.7 %reshape.96 = f32[1,1,8,8192]{3,2,1,0:T(8,128)} reshape(f32[8,64,128]{2,1,0:T(8,128)} %get-tuple-element.12) | data formatting | bytes 524288 | tf_op jit(solution)/shard_map/reshape | solution.py:429
  (123 shorter events, 13.1 us)
Async XLA Ops:
  10.2 12.7 %collective-permute-start.10 = (f32[64,128]{1,0:T(8,128)}, f32[64,128]{1,0:T(8,128)S(1)}, u32[]{:S(2)}, u32[]{:S(2)}) collective-permute-start(f32[64,128]{1,0:T(8,128)} %get-tuple-element.11), channel_id=1, source_target_pairs={{0,24},{8,16},{16,8},{24,0},{1,25},{9,17},{17,9},{25,1},{2,26},{10... | collective-permute-start | bytes 98312 | tf_op jit(solution)/shard_map/ppermute | solution.py:338
  14.2 8.8 %collective-permute-start.8 = (f32[64,128]{1,0:T(8,128)}, f32[64,128]{1,0:T(8,128)S(1)}, u32[]{:S(2)}, u32[]{:S(2)}) collective-permute-start(f32[64,128]{1,0:T(8,128)} %get-tuple-element.11), channel_id=1, source_target_pairs={{0,8},{8,0},{16,24},{24,16},{1,9},{9,1},{17,25},{25,17},{2,10},{10... | collective-permute-start | bytes 98312 | tf_op jit(solution)/shard_map/ppermute | solution.py:338
  14.7 8.3 %collective-permute-start.9 = (f32[64,128]{1,0:T(8,128)}, f32[64,128]{1,0:T(8,128)S(1)}, u32[]{:S(2)}, u32[]{:S(2)}) collective-permute-start(f32[64,128]{1,0:T(8,128)} %get-tuple-element.11), channel_id=1, source_target_pairs={{0,16},{8,24},{16,0},{24,8},{1,17},{9,25},{17,1},{25,9},{2,18},{10... | collective-permute-start | bytes 98312 | tf_op jit(solution)/shard_map/ppermute | solution.py:338
  19.9 10.6 %collective-permute-start.25 = (bf16[2,128,256]{2,1,0:T(8,128)(2,1)}, bf16[2,128,256]{2,1,0:T(8,128)(2,1)S(1)}, u32[]{:S(2)}, u32[]{:S(2)}) collective-permute-start(bf16[2,128,256]{2,1,0:T(8,128)(2,1)} %cut_piece.1), channel_id=1, source_target_pairs={{0,4},{1,5},{2,6},{3,7},{4,0},{5,1},{6,2},{7,3},{8,12},{9,13},{10,... | collective-permute-start | bytes 393224 | tf_op jit(solution)/shard_map/ppermute | solution.py:338
  25.4 14.3 %collective-permute-start.17 = (bf16[2,128,256]{2,1,0:T(8,128)(2,1)}, bf16[2,128,256]{2,1,0:T(8,128)(2,1)S(1)}, u32[]{:S(2)}, u32[]{:S(2)}) collective-permute-start(bf16[2,128,256]{2,1,0:T(8,128)(2,1)} %cut_piece.1), channel_id=1, source_target_pairs={{0,2},{1,3},{2,0},{3,1},{4,6},{5,7},{6,4},{7,5},{8,10},{9,11},{10,... | collective-permute-start | bytes 393224 | tf_op jit(solution)/shard_map/ppermute | solution.py:338
  25.8 13.9 %collective-permute-start = (bf16[2,128,256]{2,1,0:T(8,128)(2,1)}, bf16[2,128,256]{2,1,0:T(8,128)(2,1)S(1)}, u32[]{:S(2)}, u32[]{:S(2)}) collective-permute-start(bf16[2,128,256]{2,1,0:T(8,128)(2,1)} %cut_piece.1), channel_id=1, source_target_pairs={{0,6},{1,7},{2,4},{3,5},{4,2},{5,3},{6,0},{7,1},{8,14},{9,15},{10,... | collective-permute-start | bytes 393224 | tf_op jit(solution)/shard_map/ppermute | solution.py:338
  27.9 8.8 %collective-permute-start.12 = (f32[64,128]{1,0:T(8,128)S(1)}, f32[64,128]{1,0:T(8,128)S(1)}, u32[]{:S(2)}, u32[]{:S(2)}) collective-permute-start(f32[64,128]{1,0:T(8,128)S(1)} %add_add_fusion.1), channel_id=1, source_target_pairs={{0,4},{1,5},{2,6},{3,7},{4,0},{5,1},{6,2},{7,3},{8,12},{9,13},{10,... | collective-permute-start | bytes 98312 | tf_op jit(solution)/shard_map/ppermute | solution.py:338
  29.6 8.7 %collective-permute-start.13 = (f32[64,128]{1,0:T(8,128)S(1)}, f32[64,128]{1,0:T(8,128)S(1)}, u32[]{:S(2)}, u32[]{:S(2)}) collective-permute-start(f32[64,128]{1,0:T(8,128)S(1)} %add_add_fusion.1), channel_id=1, source_target_pairs={{0,6},{1,7},{2,4},{3,5},{4,2},{5,3},{6,0},{7,1},{8,14},{9,15},{10,... | collective-permute-start | bytes 98312 | tf_op jit(solution)/shard_map/ppermute | solution.py:338
  30.5 12.4 %collective-permute-start.26 = (bf16[2,128,256]{2,1,0:T(8,128)(2,1)S(1)}, bf16[2,128,256]{2,1,0:T(8,128)(2,1)S(1)}, u32[]{:S(2)}, u32[]{:S(2)}) collective-permute-start(bf16[2,128,256]{2,1,0:T(8,128)(2,1)S(1)} %collective-permute-done.25.refs_0_), channel_id=1, source_target_pairs={{0,8},{8,0},{16,24},{24,16},{1,9},{9,1},{17,25},{25,17},{2,10},{10... | collective-permute-start | bytes 393224 | tf_op jit(solution)/shard_map/ppermute | solution.py:338
  36.7 6.4 %collective-permute-start.27 = (bf16[2,128,256]{2,1,0:T(8,128)(2,1)S(1)}, bf16[2,128,256]{2,1,0:T(8,128)(2,1)S(1)}, u32[]{:S(2)}, u32[]{:S(2)}) collective-permute-start(bf16[2,128,256]{2,1,0:T(8,128)(2,1)S(1)} %collective-permute-done.25.refs_0_), channel_id=1, source_target_pairs={{0,16},{8,24},{16,0},{24,8},{1,17},{9,25},{17,1},{25,9},{2,18},{10... | collective-permute-start | bytes 393224 | tf_op jit(solution)/shard_map/ppermute | solution.py:338
  39.8 8.7 %collective-permute-start.18 = (bf16[2,128,256]{2,1,0:T(8,128)(2,1)S(1)}, bf16[2,128,256]{2,1,0:T(8,128)(2,1)S(1)}, u32[]{:S(2)}, u32[]{:S(2)}) collective-permute-start(bf16[2,128,256]{2,1,0:T(8,128)(2,1)S(1)} %collective-permute-done.17.refs_0_), channel_id=1, source_target_pairs={{0,8},{8,0},{16,24},{24,16},{1,9},{9,1},{17,25},{25,17},{2,10},{10... | collective-permute-start | bytes 393224 | tf_op jit(solution)/shard_map/ppermute | solution.py:338
  42.9 12.9 %collective-permute-start.15 = (bf16[1,128,1024]{2,1,0:T(8,128)(2,1)S(1)}, bf16[1,128,1024]{2,1,0:T(8,128)(2,1)S(1)}, u32[]{:S(2)}, u32[]{:S(2)}) collective-permute-start(bf16[1,128,1024]{2,1,0:T(8,128)(2,1)S(1)} %copy-done), channel_id=1, source_target_pairs={{0,1},{1,0},{2,3},{3,2},{4,5},{5,4},{6,7},{7,6},{8,9},{9,8},{10,11... | collective-permute-start | bytes 786440 | tf_op jit(solution)/shard_map/ppermute | solution.py:338
  43.2 13.9 %collective-permute-start.16 = (bf16[1,128,1024]{2,1,0:T(8,128)(2,1)S(1)}, bf16[1,128,1024]{2,1,0:T(8,128)(2,1)S(1)}, u32[]{:S(2)}, u32[]{:S(2)}) collective-permute-start(bf16[1,128,1024]{2,1,0:T(8,128)(2,1)S(1)} %copy-done.1), channel_id=1, source_target_pairs={{0,1},{1,0},{2,3},{3,2},{4,5},{5,4},{6,7},{7,6},{8,9},{9,8},{10,11... | collective-permute-start | bytes 786440 | tf_op jit(solution)/shard_map/ppermute | solution.py:338
  44.5 7.8 %collective-permute-start.19 = (bf16[2,128,256]{2,1,0:T(8,128)(2,1)S(1)}, bf16[2,128,256]{2,1,0:T(8,128)(2,1)S(1)}, u32[]{:S(2)}, u32[]{:S(2)}) collective-permute-start(bf16[2,128,256]{2,1,0:T(8,128)(2,1)S(1)} %collective-permute-done.17.refs_0_), channel_id=1, source_target_pairs={{0,16},{8,24},{16,0},{24,8},{1,17},{9,25},{17,1},{25,9},{2,18},{10... | collective-permute-start | bytes 393224 | tf_op jit(solution)/shard_map/ppermute | solution.py:338
  45.2 9.1 %collective-permute-start.20 = (bf16[2,128,256]{2,1,0:T(8,128)(2,1)S(1)}, bf16[2,128,256]{2,1,0:T(8,128)(2,1)S(1)}, u32[]{:S(2)}, u32[]{:S(2)}) collective-permute-start(bf16[2,128,256]{2,1,0:T(8,128)(2,1)S(1)} %collective-permute-done.17.refs_0_), channel_id=1, source_target_pairs={{0,24},{8,16},{16,8},{24,0},{1,25},{9,17},{17,9},{25,1},{2,26},{10... | collective-permute-start | bytes 393224 | tf_op jit(solution)/shard_map/ppermute | solution.py:338
  48.4 6.3 %collective-permute-start.21 = (bf16[2,128,256]{2,1,0:T(8,128)(2,1)S(1)}, bf16[2,128,256]{2,1,0:T(8,128)(2,1)S(1)}, u32[]{:S(2)}, u32[]{:S(2)}) collective-permute-start(bf16[2,128,256]{2,1,0:T(8,128)(2,1)S(1)} %collective-permute-done.17.refs_0_), channel_id=1, source_target_pairs={{0,1},{1,0},{2,3},{3,2},{4,5},{5,4},{6,7},{7,6},{8,9},{9,8},{10,11... | collective-permute-start | bytes 393224 | tf_op jit(solution)/shard_map/ppermute | solution.py:338
  54.2 6.9 %collective-permute-start.2 = (bf16[2,128,256]{2,1,0:T(8,128)(2,1)S(1)}, bf16[2,128,256]{2,1,0:T(8,128)(2,1)S(1)}, u32[]{:S(2)}, u32[]{:S(2)}) collective-permute-start(bf16[2,128,256]{2,1,0:T(8,128)(2,1)S(1)} %collective-permute-done.refs_0_), channel_id=1, source_target_pairs={{0,16},{8,24},{16,0},{24,8},{1,17},{9,25},{17,1},{25,9},{2,18},{10... | collective-permute-start | bytes 393224 | tf_op jit(solution)/shard_map/ppermute | solution.py:338
  54.8 6.4 %collective-permute-start.3 = (bf16[2,128,256]{2,1,0:T(8,128)(2,1)S(1)}, bf16[2,128,256]{2,1,0:T(8,128)(2,1)S(1)}, u32[]{:S(2)}, u32[]{:S(2)}) collective-permute-start(bf16[2,128,256]{2,1,0:T(8,128)(2,1)S(1)} %collective-permute-done.refs_0_), channel_id=1, source_target_pairs={{0,24},{8,16},{16,8},{24,0},{1,25},{9,17},{17,9},{25,1},{2,26},{10... | collective-permute-start | bytes 393224 | tf_op jit(solution)/shard_map/ppermute | solution.py:338
  61.6 17.6 %collective-permute-start.24 = (bf16[2,128,256]{2,1,0:T(8,128)(2,1)S(1)}, bf16[2,128,256]{2,1,0:T(8,128)(2,1)S(1)}, u32[]{:S(2)}, u32[]{:S(2)}) collective-permute-start(bf16[2,128,256]{2,1,0:T(8,128)(2,1)S(1)} %collective-permute-done.20.refs_3_), channel_id=1, source_target_pairs={{0,1},{1,0},{2,3},{3,2},{4,5},{5,4},{6,7},{7,6},{8,9},{9,8},{10,11... | collective-permute-start | bytes 393224 | tf_op jit(solution)/shard_map/ppermute | solution.py:338
  61.8 26.3 %collective-permute-start.4 = (bf16[2,128,256]{2,1,0:T(8,128)(2,1)S(1)}, bf16[2,128,256]{2,1,0:T(8,128)(2,1)S(1)}, u32[]{:S(2)}, u32[]{:S(2)}) collective-permute-start(bf16[2,128,256]{2,1,0:T(8,128)(2,1)S(1)} %collective-permute-done.refs_0_), channel_id=1, source_target_pairs={{0,1},{1,0},{2,3},{3,2},{4,5},{5,4},{6,7},{7,6},{8,9},{9,8},{10,11... | collective-permute-start | bytes 393224 | tf_op jit(solution)/shard_map/ppermute | solution.py:338
  62.3 25.8 %collective-permute-start.5 = (bf16[2,128,256]{2,1,0:T(8,128)(2,1)S(1)}, bf16[2,128,256]{2,1,0:T(8,128)(2,1)S(1)}, u32[]{:S(2)}, u32[]{:S(2)}) collective-permute-start(bf16[2,128,256]{2,1,0:T(8,128)(2,1)S(1)} %collective-permute-done.1.refs_1_), channel_id=1, source_target_pairs={{0,1},{1,0},{2,3},{3,2},{4,5},{5,4},{6,7},{7,6},{8,9},{9,8},{10,11... | collective-permute-start | bytes 393224 | tf_op jit(solution)/shard_map/ppermute | solution.py:338
  62.5 25.6 %collective-permute-start.6 = (bf16[2,128,256]{2,1,0:T(8,128)(2,1)S(1)}, bf16[2,128,256]{2,1,0:T(8,128)(2,1)S(1)}, u32[]{:S(2)}, u32[]{:S(2)}) collective-permute-start(bf16[2,128,256]{2,1,0:T(8,128)(2,1)S(1)} %collective-permute-done.2.refs_2_), channel_id=1, source_target_pairs={{0,1},{1,0},{2,3},{3,2},{4,5},{5,4},{6,7},{7,6},{8,9},{9,8},{10,11... | collective-permute-start | bytes 393224 | tf_op jit(solution)/shard_map/ppermute | solution.py:338
  62.8 25.3 %collective-permute-start.7 = (bf16[2,128,256]{2,1,0:T(8,128)(2,1)S(1)}, bf16[2,128,256]{2,1,0:T(8,128)(2,1)S(1)}, u32[]{:S(2)}, u32[]{:S(2)}) collective-permute-start(bf16[2,128,256]{2,1,0:T(8,128)(2,1)S(1)} %collective-permute-done.3.refs_3_), channel_id=1, source_target_pairs={{0,1},{1,0},{2,3},{3,2},{4,5},{5,4},{6,7},{7,6},{8,9},{9,8},{10,11... | collective-permute-start | bytes 393224 | tf_op jit(solution)/shard_map/ppermute | solution.py:338
  79.3 8.7 %collective-permute-start.14 = (f32[64,128]{1,0:T(8,128)S(1)}, f32[64,128]{1,0:T(8,128)S(1)}, u32[]{:S(2)}, u32[]{:S(2)}) collective-permute-start(f32[64,128]{1,0:T(8,128)S(1)} %add_add_fusion.refs_14_), channel_id=1, source_target_pairs={{0,1},{1,0},{2,3},{3,2},{4,5},{5,4},{6,7},{7,6},{8,9},{9,8},{10,11... | collective-permute-start | bytes 98312 | tf_op jit(solution)/shard_map/ppermute | solution.py:338
  (40 other events, 592.2 us)

commit v3 on v2

v3 whole, which is shorter than its diff:
```python
import functools
import math

import jax
import jax.numpy as jnp
from jax import lax
from jax.experimental import pallas as pl
from jax.experimental.pallas import tpu as pltpu
from jax.sharding import PartitionSpec as P

epsilon = 1e-06
update_scale = 0.1 / math.sqrt(0.001)
HIGHEST = lax.Precision.HIGHEST
NN = (((1,), (0,)), ((), ()))
TN = (((0,), (0,)), ((), ()))
NT = (((1,), (1,)), ((), ()))
VMEM_LIMIT = 60 * 1024 * 1024
CHUNK_LIMIT = 24 * 1024 * 1024
ANY = pl.BlockSpec(memory_space=pl.ANY)
SMEM = pl.BlockSpec(memory_space=pltpu.SMEM)
VMEM = pl.BlockSpec(memory_space=pltpu.VMEM)


def mm(a, b, dims=NN, precision=None):
    return lax.dot_general(a, b, dims, precision=precision, preferred_element_type=jnp.float32)


def two_terms(exact):
    coarse = exact.astype(jnp.bfloat16)
    fine = (exact - coarse.astype(jnp.float32)).astype(jnp.bfloat16)
    return coarse, fine


def cut_kernel(first, second, out, sems):
    group = lax.axis_index("dp")
    copies = [
        pltpu.make_async_copy(source.at[group], out.at[i], sems.at[i])
        for i, source in enumerate((first, second))
    ]
    for copy in copies:
        copy.start()
    for copy in copies:
        copy.wait()


def cut_piece(first, second):
    return pl.pallas_call(
        cut_kernel,
        in_specs=[ANY, ANY],
        out_specs=VMEM,
        out_shape=jax.ShapeDtypeStruct((2,) + first.shape[1:], first.dtype),
        scratch_shapes=[pltpu.SemaphoreType.DMA((2,))],
        compiler_params=pltpu.CompilerParams(vmem_limit_bytes=VMEM_LIMIT),
        name="cut_piece",
    )(first, second)


def prepare_kernel(
    span, lengths, x, g, xv, gv, down_t, up, columns, rows_t,
    top_out, bottom_out, proj_out,
    xs, gs, xvs, gvs, downs, ups, tables, sems,
):
    width = x.shape[1]
    steps = width // span
    copies = []
    for i in range(steps):
        cols = pl.ds(i * span, span)
        pairs = [(up, ups), (g, gs), (down_t, downs), (x, xs), (xv, xvs), (gv, gvs)]
        step = [
            pltpu.make_async_copy(source.at[:, cols], target.at[:, cols], sems.at[i, k])
            for k, (source, target) in enumerate(pairs)
        ]
        step.append(pltpu.make_async_copy(columns.at[cols, :], tables.at[cols, :], sems.at[i, len(pairs)]))
        copies.append(step)
    for step in copies:
        for copy in step:
            copy.start()
    back = fwd = vback = vfwd = xc = gc = 0.0
    k2 = columns.shape[1]
    for i in range(steps):
        for copy in copies[i]:
            copy.wait()
        cols = pl.ds(i * span, span)
        table = jnp.concatenate(two_terms(tables[cols, :]), axis=1)
        back = back + mm(gs[:, cols], ups[:, cols], NT)
        fwd = fwd + mm(xs[:, cols], downs[:, cols], NT)
        vback = vback + mm(gvs[:, cols], ups[:, cols], NT)
        vfwd = vfwd + mm(xvs[:, cols], downs[:, cols], NT)
        xc = xc + mm(xvs[:, cols], table)
        gc = gc + mm(gvs[:, cols], table)
    tokens, rank = back.shape
    position = lax.broadcasted_iota(jnp.int32, (rank, tokens), 1)
    back_t = back.T
    fwd_t = fwd.T
    begin = jnp.int32(0)
    for e in range(lengths.shape[0]):
        finish = begin + lengths[e]
        member = (position >= begin) & (position < finish)
        top_out[pl.ds(e * rank, rank), :] = jnp.where(member, back_t, 0.0).astype(jnp.bfloat16)
        bottom_out[pl.ds(e * rank, rank), :] = jnp.where(member, fwd_t, 0.0).astype(jnp.bfloat16)
        begin = finish
    round_b = vback.astype(jnp.bfloat16).astype(jnp.float32)
    round_f = vfwd.astype(jnp.bfloat16).astype(jnp.float32)
    inner_top = mm(round_b, xc[:, :k2] + xc[:, k2:], TN, HIGHEST)
    inner_bottom = mm(round_f, gc[:, :k2] + gc[:, k2:], TN, HIGHEST)
    inner = jnp.concatenate([inner_top, inner_bottom], axis=0)
    proj_out[...] = mm(rows_t[...], inner, NN, HIGHEST)


def prepare(lengths, x, g, xv, gv, down_t, up, columns, rows_t):
    tokens, width = x.shape
    rank = up.shape[0]
    k1, k2 = rows_t.shape[0], columns.shape[1]
    examples = lengths.shape[0]
    span = 2048
    return pl.pallas_call(
        functools.partial(prepare_kernel, span),
        in_specs=[SMEM] + [ANY] * 7 + [VMEM],
        out_specs=[VMEM] * 3,
        out_shape=[
            jax.ShapeDtypeStruct((examples * rank, tokens), jnp.bfloat16),
            jax.ShapeDtypeStruct((examples * rank, tokens), jnp.bfloat16),
            jax.ShapeDtypeStruct((k1, k2), jnp.float32),
        ],
        scratch_shapes=[
            *(pltpu.VMEM(a.shape, a.dtype) for a in (x, g, xv, gv, down_t, up, columns)),
            pltpu.SemaphoreType.DMA((width // span, 7)),
        ],
        compiler_params=pltpu.CompilerParams(vmem_limit_bytes=VMEM_LIMIT),
        cost_estimate=pl.CostEstimate(
            flops=4 * tokens * width * rank, bytes_accessed=20_000_000, transcendentals=0
        ),
        name="prepare",
    )(lengths, x, g, xv, gv, down_t, up, columns, rows_t)


def accumulate(block_of, copies_of, moments, slots, x, g, columns, top, bottom, xs, gs, cs, ms, update, inner, sems):
    count, _, span = xs.shape
    rank = ms.shape[1] * ms.shape[3] // 2
    examples = top.shape[0] // rank
    copies = []
    for b in range(count):
        cols = pl.ds(pl.multiple_of(slots[block_of(b)] * span, span), span)
        pairs = [(x.at[:, cols], xs.at[b]), (g.at[:, cols], gs.at[b]), (columns.at[cols, :], cs.at[b])]
        pairs += copies_of(moments, b, ms.at[b])
        copies.append([pltpu.make_async_copy(p[0], p[1], sems.at[b, k]) for k, p in enumerate(pairs)])
    for block in copies:
        for copy in block:
            copy.start()
    inner[...] = jnp.zeros_like(inner)
    cut = min(span, 256)
    half_parts = ms.shape[1] // 2
    for b in range(count):
        for copy in copies[b]:
            copy.wait()
        table = jnp.concatenate(two_terms(cs[b]), axis=1)
        for half, (source, masked) in enumerate(((xs, top), (gs, bottom))):
            parts = slice(half * half_parts, (half + 1) * half_parts)
            for c in range(0, span, cut):
                cols = pl.ds(c, cut)
                grad = mm(masked[...], source[b, :, cols])
                first = 9.0 * ms[b, parts, 0, :, cols].astype(jnp.float32).reshape(rank, cut)
                second = 999.0 * ms[b, parts, 1, :, cols].astype(jnp.float32).reshape(rank, cut)
                shared = first * lax.rsqrt(second)
                coarse, fine = two_terms(shared)
                update[half, pl.ds(examples * rank, rank), cols] = coarse
                update[half, pl.ds((examples + 1) * rank, rank), cols] = fine
                for e in range(examples):
                    piece = grad[e * rank : (e + 1) * rank]
                    change = (first + piece) * lax.rsqrt(second + piece * piece) - shared
                    update[half, pl.ds(e * rank, rank), cols] = change.astype(jnp.bfloat16)
            inner[half] += mm(update[half], table)


def folded(inner, half, examples, rank, e):
    k2 = inner.shape[2] // 2
    part = pl.ds(e * rank, rank)
    total = inner[half, part, :k2] + inner[half, part, k2:]
    if e == examples:
        part = pl.ds((examples + 1) * rank, rank)
        total = total + inner[half, part, :k2] + inner[half, part, k2:]
    return total


def chunk_kernel(block_of, copies_of, n_moments, slots, *refs):
    moments, refs = refs[:n_moments], refs[n_moments:]
    x, g, columns, top, bottom, out, xs, gs, cs, ms, update, inner, sems = refs
    accumulate(
        block_of, copies_of, moments, slots, x, g, columns, top, bottom, xs, gs, cs, ms, update, inner, sems
    )
    rank = ms.shape[1] * ms.shape[3] // 2
    examples = top.shape[0] // rank
    for half in (0, 1):
        for e in range(examples + 1):
            out[half, pl.ds(e * rank, rank), :] = folded(inner, half, examples, rank, e)


def last_kernel(block_of, copies_of, n_moments, n_partial, slots, *refs):
    moments, refs = refs[:n_moments], refs[n_moments:]
    x, g, columns, top, bottom, rows_t = refs[:6]
    val_parts, refs = refs[6:8], refs[8:]
    partials, refs = refs[:n_partial], refs[n_partial:]
    dirs_out, val_out, scores_out, joined, xs, gs, cs, ms, update, inner, sems = refs
    accumulate(
        block_of, copies_of, moments, slots, x, g, columns, top, bottom, xs, gs, cs, ms, update, inner, sems
    )
    rank = ms.shape[1] * ms.shape[3] // 2
    examples = top.shape[0] // rank
    k1, k2 = rows_t.shape[0], columns.shape[1]
    size = k1 * k2
    val = val_parts[0][...] + val_parts[1][...]
    val_dir = val * lax.rsqrt(jnp.sum(val * val) / size + epsilon)
    val_out[...] = val_dir
    rows = rows_t[...] * update_scale
    for e in range(examples + 1):
        for half in (0, 1):
            total = folded(inner, half, examples, rank, e)
            for partial in partials:
                total = total + partial[half, pl.ds(e * rank, rank), :]
            joined[pl.ds(half * rank, rank), pl.ds(e * k2, k2)] = total
    projected = mm(rows, joined[...], NN, HIGHEST)
    base = projected[:, examples * k2 :]
    for e in range(examples):
        proj = projected[:, e * k2 : (e + 1) * k2] + base
        direction = proj * lax.rsqrt(jnp.sum(proj * proj) / size + epsilon)
        dirs_out[e] = direction
        scores_out[e] = jnp.sum(direction * val_dir) / math.sqrt(size)


def chunk(slots, count, block_of, copies_of, n_copies, parts, moments, x, g, columns, top, bottom, last=None):
    tokens, width = x.shape
    k2 = columns.shape[1]
    span = width // slots.shape[0]
    quarter, rank = parts
    pieces = 2 * rank // quarter
    examples = top.shape[0] // rank
    scratch = [
        pltpu.VMEM((count, tokens, span), jnp.bfloat16),
        pltpu.VMEM((count, tokens, span), jnp.bfloat16),
        pltpu.VMEM((count, span, k2), jnp.float32),
        pltpu.VMEM((count, pieces, 2, quarter, span), jnp.bfloat16),
        pltpu.VMEM((2, (examples + 2) * rank, span), jnp.bfloat16),
        pltpu.VMEM((2, (examples + 2) * rank, 2 * k2), jnp.float32),
        pltpu.SemaphoreType.DMA((count, 3 + n_copies)),
    ]
    cost = pl.CostEstimate(
        flops=4 * tokens * span * count * rank * examples,
        bytes_accessed=6_000_000 * count,
        transcendentals=0,
    )
    common = [SMEM] + [ANY] * len(moments) + [ANY, ANY, ANY, VMEM, VMEM]
    operands = [slots, *moments, x, g, columns, top, bottom]
    params = pltpu.CompilerParams(vmem_limit_bytes=CHUNK_LIMIT)
    if last is None:
        return pl.pallas_call(
            functools.partial(chunk_kernel, block_of, copies_of, len(moments)),
            in_specs=common,
            out_specs=VMEM,
            out_shape=jax.ShapeDtypeStruct((2, (examples + 1) * rank, k2), jnp.float32),
            scratch_shapes=scratch,
            compiler_params=params,
            cost_estimate=cost,
            name="chunk",
        )(*operands)
    rows_t, val_parts, partials = last
    k1 = rows_t.shape[0]
    return pl.pallas_call(
        functools.partial(last_kernel, block_of, copies_of, len(moments), len(partials)),
        in_specs=common + [VMEM] * (3 + len(partials)),
        out_specs=[VMEM, VMEM, SMEM],
        out_shape=[
            jax.ShapeDtypeStruct((examples, k1, k2), jnp.float32),
            jax.ShapeDtypeStruct((k1, k2), jnp.float32),
            jax.ShapeDtypeStruct((examples,), jnp.float32),
        ],
        scratch_shapes=[pltpu.VMEM((2 * rank, (examples + 1) * k2), jnp.float32), *scratch],
        compiler_params=params,
        cost_estimate=cost,
        name="last_chunk",
    )(*operands, rows_t, *val_parts, *partials)


def copies_of_pieces(moments, b, target):
    group = lax.axis_index("dp")
    return [(piece.at[b], target.at[lax.bitwise_xor(group, j)]) for j, piece in enumerate(moments)]


def copies_of_blocks(moments, b, target):
    return [(moments[2 * b + k], target.at[:, k]) for k in (0, 1)]


def copies_of_gathered(moments, b, target):
    return [(moments[k].at[b], target.at[:, k]) for k in (0, 1)]


def slot_at(other, hop):
    return lax.bitwise_xor(lax.axis_index("shard"), 2 * hop + other)


def exchange(value, axis, bits):
    size = lax.axis_size(axis)
    return lax.ppermute(value, axis, [(i, i ^ bits) for i in range(size)])


def spread_sum(own, others):
    return (own + others[0]) + (others[1] + others[2])


def body(
    training_inputs,
    training_cotangents,
    validation_inputs,
    validation_cotangents,
    adapter_down,
    adapter_up,
    adam_first_moment,
    adam_second_moment,
    slot_block_index,
    example_lengths,
    projection_rows,
    projection_columns,
):
    groups = lax.axis_size("dp")
    shards = lax.axis_size("shard")
    rank = adapter_up.shape[0]
    quarter = 2 * rank // groups
    parts = (quarter, rank)
    stepwise = groups == 4 and shards == 8
    rows_t = projection_rows.T
    own = [m.reshape(groups, quarter, -1) for m in (adam_first_moment, adam_second_moment)]
    train = (training_inputs, training_cotangents)
    if stepwise:
        piece = cut_piece(*own)
        sibling = [exchange(m, "shard", 1) for m in own]
        far = [exchange(piece, "shard", 2 * hop) for hop in (1, 2, 3)]
    top, bottom, val_part = prepare(
        example_lengths[0, 0],
        *train,
        validation_inputs,
        validation_cotangents,
        adapter_down.T,
        adapter_up,
        projection_columns,
        rows_t,
    )
    if stepwise:
        *arrived, top, bottom, val_part = lax.optimization_barrier((*far, *sibling, top, bottom, val_part))
        far, sibling = jnp.stack(arrived[:3]), arrived[3:]
        four = [far] + [exchange(far, "dp", bits) for bits in (1, 2, 3)]
        total = spread_sum(val_part, [exchange(val_part, "dp", bits) for bits in (1, 2, 3)])
        total, top, bottom = lax.optimization_barrier((total, top, bottom))
        others = [exchange(total, "shard", 2 * bits) for bits in (1, 2, 3)]
        operands = (*train, projection_columns, top, bottom)
        first = chunk(
            slot_block_index, 2, lambda b: slot_at(b, 0), copies_of_blocks, 2, parts, own + sibling, *operands
        )
        first, *arrived = lax.optimization_barrier((first, *others, *four))
        total = spread_sum(total, arrived[:3])
        val_parts = [total, exchange(total, "shard", 1)]
        four = arrived[3:]
        crossed = [exchange(part, "shard", 1) for part in four]
        second = chunk(
            slot_block_index, 3, lambda b: slot_at(0, b + 1), copies_of_pieces, 4, parts, four, *operands
        )
        partials = [first, second]
        dirs, val_dir, scores = chunk(
            slot_block_index,
            3,
            lambda b: slot_at(1, b + 1),
            copies_of_pieces,
            4,
            parts,
            crossed,
            *operands,
            last=(rows_t, val_parts, partials),
        )
    else:
        operands = (*train, projection_columns, top, bottom)
        gathered = [lax.all_gather(m, "shard", axis=0, tiled=False) for m in own]
        val_sum = lax.psum(val_part, ("dp", "shard"))
        dirs, val_dir, scores = chunk(
            slot_block_index,
            shards,
            lambda b: b,
            copies_of_gathered,
            2,
            parts,
            gathered,
            *operands,
            last=(rows_t, [val_sum, jnp.zeros_like(val_sum)], []),
        )
    return (
        dirs.reshape(1, 1, dirs.shape[0], -1),
        val_dir.reshape(-1),
        scores[None, None],
    )


def solution(mesh):
    return jax.shard_map(
        body,
        mesh=mesh,
        in_specs=(
            P(("dp", "shard"), None),
            P(("dp", "shard"), None),
            P(("dp", "shard"), None),
            P(("dp", "shard"), None),
            P(),
            P(),
            P("shard", None, None),
            P("shard", None, None),
            P(),
            P("dp", "shard", None),
            P(),
            P(),
        ),
        out_specs=(P("dp", "shard", None, None), P(), P("dp", "shard", None)),
        check_vma=False,
    )
```

time: 102 us -> 85.7 us (0.84)
  Pallas kernels: 49.1 us -> 35.9 us
  waiting for transfers between devices: 9.49 us -> 17.3 us
  starting transfers between devices: 29.4 us -> 24.1 us
  other arithmetic: 6.02 us -> 0.86 us
    pallas_call x6 -> x5, Pallas kernels: 49.1 us -> 35.9 us  [the longest x2 14.1 us: chunk(): pl.pallas_call(functools.partial(chunk_kernel, block_of, copies_of, len(m...]
    ppermute x33 -> x19, waiting for transfers between devices: 9.49 us -> 17.3 us  [exchange(): return lax.ppermute(value, axis, [(i, i ^ bits) for i in range(size)])]
    ppermute x33 -> x19, starting transfers between devices: 29.4 us -> 24.1 us  [exchange(): return lax.ppermute(value, axis, [(i, i ^ bits) for i in range(size)])]
    mul x2 -> x0, other arithmetic: 5.09 us -> none  [ids_of(): return (blocks[:, None] * groups + order[None, :]).reshape(-1)]
    unnamed x62 -> x22, local copies, waits for them, and re-layouts: 1.68 us -> 5.61 us
    add x4 -> x0, local copies, waits for them, and re-layouts: 2.36 us -> none  [ids_of(): return (blocks[:, None] * groups + order[None, :]).reshape(-1)]
  transfers between devices with their start and end apart: 33 -> 19, of which waited for: 6 -> 4; matrix products, arithmetic and copies ran while one was open for 9% -> 1% of each run, Pallas kernels for 29% -> 28%
where the time goes in v3:
time: 85.7 us; the launch traced here: 85.4 us
  Pallas kernels  35.9 us (42%)
  starting transfers between devices  24.1 us (28%)
  waiting for transfers between devices  17.3 us (20%)
  local copies, waits for them, and re-layouts  6.37 us (7%)
  other arithmetic  0.86 us (1%)
    ppermute x19, starting transfers between devices, exchange(): return lax.ppermute(value, axis, [(i, i ^ bits) for i in range(size)])  24.1 us
    ppermute x19, waiting for transfers between devices, exchange(): return lax.ppermute(value, axis, [(i, i ^ bits) for i in range(size)])  17.3 us
    pallas_call x2, Pallas kernels, chunk(): pl.pallas_call(functools.partial(chunk_kernel, block_of, copies_of, len(m...  14.1 us
    pallas_call x1, Pallas kernels, chunk(): pl.pallas_call(functools.partial(last_kernel, block_of, copies_of, len(mo...  12.1 us
    pallas_call x1, Pallas kernels, prepare(): pl.pallas_call(functools.partial(prepare_kernel, span), in_specs=[SMEM] +...  8.12 us
    unnamed x22, local copies, waits for them, and re-layouts  5.61 us
  transfers between devices with their start and end apart: 19, of which 4 were waited for; matrix products, arithmetic and copies ran while one was open for 1% of the time, Pallas kernels for 28%

profile of v3, /device:TPU:0, one launch (start us, length us, event | category | flops | bytes accessed | tf_op | source)
XLA Modules:
  0.0 85.4 jit_solution(3448385699665178937)
XLA Ops:
  1.2 1.5 %cut_piece.1 = bf16[2,32,1024]{2,1,0:T(8,128)(2,1)} custom-call(bf16[4,32,1024]{2,1,0:T(8,128)(2,1)} %bitcast.11, bf16[4,32,1024]{2,1,0:T(8,128)(2,1)} %bitcast.14), custom_call_target="tpu_custom_call" | custom-call | tf_op jit(solution)/shard_map/cut_piece/pallas_call | solution.py:47
  2.8 3.1 %collective-permute-start = (bf16[2,32,1024]{2,1,0:T(8,128)(2,1)}, bf16[2,32,1024]{2,1,0:T(8,128)(2,1)S(1)}, u32[]{:S(2)}, u32[]{:S(2)}) collective-permute-start(bf16[2,32,1024]{2,1,0:T(8,128)(2,1)} %cut_piece.1), channel_id=1, source_target_pairs={{0,2},{1,3},{2,0},{3,1},{4,6},{5,7},{6,4},{7,5},{8,10},{9,11},{10,... | collective-permute-start | bytes 393224 | tf_op jit(solution)/shard_map/ppermute | solution.py:302
  5.8 2.6 %collective-permute-start.1 = (bf16[2,32,1024]{2,1,0:T(8,128)(2,1)}, bf16[2,32,1024]{2,1,0:T(8,128)(2,1)S(1)}, u32[]{:S(2)}, u32[]{:S(2)}) collective-permute-start(bf16[2,32,1024]{2,1,0:T(8,128)(2,1)} %cut_piece.1), channel_id=1, source_target_pairs={{0,4},{1,5},{2,6},{3,7},{4,0},{5,1},{6,2},{7,3},{8,12},{9,13},{10,... | collective-permute-start | bytes 393224 | tf_op jit(solution)/shard_map/ppermute | solution.py:302
  8.5 8.1 %prepare.1 = (bf16[512,128]{1,0:T(8,128)(2,1)}, bf16[512,128]{1,0:T(8,128)(2,1)}, f32[64,128]{1,0:T(8,128)}) custom-call(s32[8]{0:T(128)} %bitcast.22, bf16[128,8192]{1,0:T(8,128)(2,1)} %refs_4_.5, bf16[128,8192]{1,0:T(8,128)(2,1)} %refs_5_.5, bf16[32,8192]{1,0:T(8,128)(2,1)} %xv.1, bf16[32,8192]{1,0:T(8,128)(2,1)} %gv.1, bf16[64,8192]{1,0:T(8,128)(2,1)} %bitcast.18, ...), custom_call_target="tpu_custom_call" | custom-call | flops 268435456 | bytes 20000000 | tf_op jit(solution)/shard_map/prepare/pallas_call | solution.py:116
  16.6 2.4 %collective-permute-done.1 = bf16[2,32,1024]{2,1,0:T(8,128)(2,1)S(1)} collective-permute-done((bf16[2,32,1024]{2,1,0:T(8,128)(2,1)}, bf16[2,32,1024]{2,1,0:T(8,128)(2,1)S(1)}, u32[]{:S(2)}, u32[]{:S(2)}) %collective-permute-start.1) | collective-permute-done | bytes 131104 | tf_op jit(solution)/shard_map/ppermute | solution.py:302
  19.0 1.6 %collective-permute-start.11 = (bf16[3,2,32,1024]{3,2,1,0:T(8,128)(2,1)S(1)}, bf16[3,2,32,1024]{3,2,1,0:T(8,128)(2,1)S(1)}, u32[]{:S(2)}, u32[]{:S(2)}) collective-permute-start(bf16[3,2,32,1024]{3,2,1,0:T(8,128)(2,1)S(1)} %pad_maximum_fusion.refs_0_), channel_id=1, source_target_pairs={{0,8},{8,0},{16,24},{24,16},{1,9},{9,1},{17,25},{25,17},{2,10},{10... | collective-permute-start | bytes 1179656 | tf_op jit(solution)/shard_map/ppermute | solution.py:302
  20.6 1.5 %collective-permute-start.12 = (bf16[3,2,32,1024]{3,2,1,0:T(8,128)(2,1)S(1)}, bf16[3,2,32,1024]{3,2,1,0:T(8,128)(2,1)S(1)}, u32[]{:S(2)}, u32[]{:S(2)}) collective-permute-start(bf16[3,2,32,1024]{3,2,1,0:T(8,128)(2,1)S(1)} %pad_maximum_fusion.refs_0_), channel_id=1, source_target_pairs={{0,16},{8,24},{16,0},{24,8},{1,17},{9,25},{17,1},{25,9},{2,18},{10... | collective-permute-start | bytes 1179656 | tf_op jit(solution)/shard_map/ppermute | solution.py:302
  22.6 1.5 %collective-permute-start.5 = (f32[64,128]{1,0:T(8,128)}, f32[64,128]{1,0:T(8,128)S(1)}, u32[]{:S(2)}, u32[]{:S(2)}) collective-permute-start(f32[64,128]{1,0:T(8,128)} %get-tuple-element.33), channel_id=1, source_target_pairs={{0,8},{8,0},{16,24},{24,16},{1,9},{9,1},{17,25},{25,17},{2,10},{10... | collective-permute-start | bytes 98312 | tf_op jit(solution)/shard_map/ppermute | solution.py:302
  24.1 1.5 %collective-permute-start.6 = (f32[64,128]{1,0:T(8,128)}, f32[64,128]{1,0:T(8,128)S(1)}, u32[]{:S(2)}, u32[]{:S(2)}) collective-permute-start(f32[64,128]{1,0:T(8,128)} %get-tuple-element.33), channel_id=1, source_target_pairs={{0,16},{8,24},{16,0},{24,8},{1,17},{9,25},{17,1},{25,9},{2,18},{10... | collective-permute-start | bytes 98312 | tf_op jit(solution)/shard_map/ppermute | solution.py:302
  25.6 11.6 %collective-permute-done.5 = f32[64,128]{1,0:T(8,128)S(1)} collective-permute-done((f32[64,128]{1,0:T(8,128)}, f32[64,128]{1,0:T(8,128)S(1)}, u32[]{:S(2)}, u32[]{:S(2)}) %collective-permute-start.5) | collective-permute-done | bytes 32800 | tf_op jit(solution)/shard_map/ppermute | solution.py:302
  37.2 2.5 %collective-permute-start.7 = (f32[64,128]{1,0:T(8,128)}, f32[64,128]{1,0:T(8,128)S(1)}, u32[]{:S(2)}, u32[]{:S(2)}) collective-permute-start(f32[64,128]{1,0:T(8,128)} %get-tuple-element.33), channel_id=1, source_target_pairs={{0,24},{8,16},{16,8},{24,0},{1,25},{9,17},{17,9},{25,1},{2,26},{10... | collective-permute-start | bytes 98312 | tf_op jit(solution)/shard_map/ppermute | solution.py:302
  39.7 2.5 %collective-permute-done.7 = f32[64,128]{1,0:T(8,128)S(1)} collective-permute-done((f32[64,128]{1,0:T(8,128)}, f32[64,128]{1,0:T(8,128)S(1)}, u32[]{:S(2)}, u32[]{:S(2)}) %collective-permute-start.7) | collective-permute-done | bytes 32800 | tf_op jit(solution)/shard_map/ppermute | solution.py:302
  42.2 0.8 add_add_fusion.1
  43.0 2.9 %collective-permute-start.10 = (f32[64,128]{1,0:T(8,128)S(1)}, f32[64,128]{1,0:T(8,128)S(1)}, u32[]{:S(2)}, u32[]{:S(2)}) collective-permute-start(f32[64,128]{1,0:T(8,128)S(1)} %add_add_fusion.1), channel_id=1, source_target_pairs={{0,6},{1,7},{2,4},{3,5},{4,2},{5,3},{6,0},{7,1},{8,14},{9,15},{10,... | collective-permute-start | bytes 98312 | tf_op jit(solution)/shard_map/ppermute | solution.py:302
  45.9 2.1 %collective-permute-start.8 = (f32[64,128]{1,0:T(8,128)S(1)}, f32[64,128]{1,0:T(8,128)S(1)}, u32[]{:S(2)}, u32[]{:S(2)}) collective-permute-start(f32[64,128]{1,0:T(8,128)S(1)} %add_add_fusion.1), channel_id=1, source_target_pairs={{0,2},{1,3},{2,0},{3,1},{4,6},{5,7},{6,4},{7,5},{8,10},{9,11},{10,... | collective-permute-start | bytes 98312 | tf_op jit(solution)/shard_map/ppermute | solution.py:302
  48.0 0.8 collective-permute-done.10
  48.8 2.6 %collective-permute-start.9 = (f32[64,128]{1,0:T(8,128)S(1)}, f32[64,128]{1,0:T(8,128)S(1)}, u32[]{:S(2)}, u32[]{:S(2)}) collective-permute-start(f32[64,128]{1,0:T(8,128)S(1)} %add_add_fusion.1), channel_id=1, source_target_pairs={{0,4},{1,5},{2,6},{3,7},{4,0},{5,1},{6,2},{7,3},{8,12},{9,13},{10,... | collective-permute-start | bytes 98312 | tf_op jit(solution)/shard_map/ppermute | solution.py:302
  51.4 2.2 %copy-done = f32[8192,128]{1,0:T(8,128)S(1)} copy-done((f32[8192,128]{1,0:T(8,128)S(1)}, f32[8192,128]{1,0:T(8,128)}, u32[]{:S(2)}) %copy-start) | copy-done | bytes 4194328
  53.6 1.6 %copy-done.3 = bf16[128,8192]{1,0:T(8,128)(2,1)S(1)} copy-done((bf16[128,8192]{1,0:T(8,128)(2,1)S(1)}, bf16[128,8192]{1,0:T(8,128)(2,1)}, u32[]{:S(2)}) %copy-start.3) | copy-done | bytes 2097176
  55.2 0.9 %copy-done.4 = bf16[512,128]{1,0:T(8,128)(2,1)S(1)} copy-done((bf16[512,128]{1,0:T(8,128)(2,1)S(1)}, bf16[512,128]{1,0:T(8,128)(2,1)}, u32[]{:S(2)}) %copy-start.4) | copy-done | bytes 131096
  56.1 0.9 %copy-done.5 = bf16[512,128]{1,0:T(8,128)(2,1)S(1)} copy-done((bf16[512,128]{1,0:T(8,128)(2,1)S(1)}, bf16[512,128]{1,0:T(8,128)(2,1)}, u32[]{:S(2)}) %copy-start.5) | copy-done | bytes 131096
  57.0 5.0 %chunk.2.refs_12_ = f32[2,576,128]{2,1,0:T(8,128)S(1)} custom-call(s32[8]{0:T(128)S(1)} %copy-done.10, bf16[4,32,1024]{2,1,0:T(8,128)(2,1)S(1)} %bitcast.12, bf16[4,32,1024]{2,1,0:T(8,128)(2,1)S(1)} %bitcast.15, bf16[4,32,1024]{2,1,0:T(8,128)(2,1)S(1)} %collective-permute-done.3.refs_2_, bf16[4,32,1024]{2,1,0:T(8,128)(2,1)S(1)} %collective-permute-done.4.refs_3_, ...), custom_call_target="tpu_custom_call" | custom-call | flops 536870912 | bytes 12000000 | tf_op jit(solution)/shard_map/chunk/pallas_call | solution.py:255
  63.4 9.1 %chunk.3.refs_13_ = f32[2,576,128]{2,1,0:T(8,128)S(1)} custom-call(s32[8]{0:T(128)S(1)} %copy-done.10, bf16[3,2,32,1024]{3,2,1,0:T(8,128)(2,1)S(1)} %pad_maximum_fusion.refs_0_, bf16[3,2,32,1024]{3,2,1,0:T(8,128)(2,1)S(1)} %collective-permute-done.11.refs_1_, bf16[3,2,32,1024]{3,2,1,0:T(8,128)(2,1)S(1)} %collective-permute-done.12.refs_2_, ...), custom_call_target="tpu_custom_call" | custom-call | flops 805306368 | bytes 18000000 | tf_op jit(solution)/shard_map/chunk/pallas_call | solution.py:255
  72.6 12.1 %last_chunk.1 = (f32[8,64,128]{2,1,0:T(8,128)S(1)}, f32[64,128]{1,0:T(8,128)}, f32[8]{0:T(128)}) custom-call(s32[8]{0:T(128)S(1)} %copy-done.10, bf16[3,2,32,1024]{3,2,1,0:T(8,128)(2,1)S(1)} %collective-permute-done.14.refs_0_, bf16[3,2,32,1024]{3,2,1,0:T(8,128)(2,1)S(1)} %collective-permute-done.15.refs_1_, ...), custom_call_target="tpu_custom_call" | custom-call | flops 805306368 | bytes 18000000 | tf_op jit(solution)/shard_map/last_chunk/pallas_call | solution.py:267
  (45 shorter events, 3.2 us)
Async XLA Ops:
  0.6 18.3 %collective-permute-start.3 = (bf16[4,32,1024]{2,1,0:T(8,128)(2,1)}, bf16[4,32,1024]{2,1,0:T(8,128)(2,1)S(1)}, u32[]{:S(2)}, u32[]{:S(2)}) collective-permute-start(bf16[4,32,1024]{2,1,0:T(8,128)(2,1)} %bitcast.10), channel_id=1, source_target_pairs={{0,1},{1,0},{2,3},{3,2},{4,5},{5,4},{6,7},{7,6},{8,9},{9,8},{10,11... | collective-permute-start | bytes 786440 | tf_op jit(solution)/shard_map/ppermute | solution.py:302
  1.1 17.8 %collective-permute-start.4 = (bf16[4,32,1024]{2,1,0:T(8,128)(2,1)}, bf16[4,32,1024]{2,1,0:T(8,128)(2,1)S(1)}, u32[]{:S(2)}, u32[]{:S(2)}) collective-permute-start(bf16[4,32,1024]{2,1,0:T(8,128)(2,1)} %bitcast.13), channel_id=1, source_target_pairs={{0,1},{1,0},{2,3},{3,2},{4,5},{5,4},{6,7},{7,6},{8,9},{9,8},{10,11... | collective-permute-start | bytes 786440 | tf_op jit(solution)/shard_map/ppermute | solution.py:302
  2.8 13.8 %collective-permute-start = (bf16[2,32,1024]{2,1,0:T(8,128)(2,1)}, bf16[2,32,1024]{2,1,0:T(8,128)(2,1)S(1)}, u32[]{:S(2)}, u32[]{:S(2)}) collective-permute-start(bf16[2,32,1024]{2,1,0:T(8,128)(2,1)} %cut_piece.1), channel_id=1, source_target_pairs={{0,2},{1,3},{2,0},{3,1},{4,6},{5,7},{6,4},{7,5},{8,10},{9,11},{10,... | collective-permute-start | bytes 393224 | tf_op jit(solution)/shard_map/ppermute | solution.py:302
  5.8 13.1 %collective-permute-start.1 = (bf16[2,32,1024]{2,1,0:T(8,128)(2,1)}, bf16[2,32,1024]{2,1,0:T(8,128)(2,1)S(1)}, u32[]{:S(2)}, u32[]{:S(2)}) collective-permute-start(bf16[2,32,1024]{2,1,0:T(8,128)(2,1)} %cut_piece.1), channel_id=1, source_target_pairs={{0,4},{1,5},{2,6},{3,7},{4,0},{5,1},{6,2},{7,3},{8,12},{9,13},{10,... | collective-permute-start | bytes 393224 | tf_op jit(solution)/shard_map/ppermute | solution.py:302
  8.4 10.5 %collective-permute-start.2 = (bf16[2,32,1024]{2,1,0:T(8,128)(2,1)}, bf16[2,32,1024]{2,1,0:T(8,128)(2,1)S(1)}, u32[]{:S(2)}, u32[]{:S(2)}) collective-permute-start(bf16[2,32,1024]{2,1,0:T(8,128)(2,1)} %cut_piece.1), channel_id=1, source_target_pairs={{0,6},{1,7},{2,4},{3,5},{4,2},{5,3},{6,0},{7,1},{8,14},{9,15},{10,... | collective-permute-start | bytes 393224 | tf_op jit(solution)/shard_map/ppermute | solution.py:302
  8.4 43.0 %copy-start.2 = (bf16[128,8192]{1,0:T(8,128)(2,1)S(1)}, bf16[128,8192]{1,0:T(8,128)(2,1)}, u32[]{:S(2)}) copy-start(bf16[128,8192]{1,0:T(8,128)(2,1)} %refs_4_.5) | copy-start | bytes 6291460
  8.4 43.0 %copy-start.7 = (bf16[1,128,1024]{2,1,0:T(8,128)(2,1)S(1)}, bf16[1,128,1024]{2,1,0:T(8,128)(2,1)}, u32[]{:S(2)}) copy-start(bf16[1,128,1024]{2,1,0:T(8,128)(2,1)} %param.18) | copy-start | bytes 786436
  8.4 43.0 %copy-start.8 = (bf16[1,128,1024]{2,1,0:T(8,128)(2,1)S(1)}, bf16[1,128,1024]{2,1,0:T(8,128)(2,1)}, u32[]{:S(2)}) copy-start(bf16[1,128,1024]{2,1,0:T(8,128)(2,1)} %param.19) | copy-start | bytes 786436
  8.4 43.0 %copy-start.10 = (s32[8]{0:T(128)S(1)}, s32[8]{0:T(128)}, u32[]{:S(2)}) copy-start(s32[8]{0:T(128)} %slots.5) | copy-start | bytes 100
  19.0 43.1 %collective-permute-start.11 = (bf16[3,2,32,1024]{3,2,1,0:T(8,128)(2,1)S(1)}, bf16[3,2,32,1024]{3,2,1,0:T(8,128)(2,1)S(1)}, u32[]{:S(2)}, u32[]{:S(2)}) collective-permute-start(bf16[3,2,32,1024]{3,2,1,0:T(8,128)(2,1)S(1)} %pad_maximum_fusion.refs_0_), channel_id=1, source_target_pairs={{0,8},{8,0},{16,24},{24,16},{1,9},{9,1},{17,25},{25,17},{2,10},{10... | collective-permute-start | bytes 1179656 | tf_op jit(solution)/shard_map/ppermute | solution.py:302
  20.6 41.5 %collective-permute-start.12 = (bf16[3,2,32,1024]{3,2,1,0:T(8,128)(2,1)S(1)}, bf16[3,2,32,1024]{3,2,1,0:T(8,128)(2,1)S(1)}, u32[]{:S(2)}, u32[]{:S(2)}) collective-permute-start(bf16[3,2,32,1024]{3,2,1,0:T(8,128)(2,1)S(1)} %pad_maximum_fusion.refs_0_), channel_id=1, source_target_pairs={{0,16},{8,24},{16,0},{24,8},{1,17},{9,25},{17,1},{25,9},{2,18},{10... | collective-permute-start | bytes 1179656 | tf_op jit(solution)/shard_map/ppermute | solution.py:302
  22.1 40.0 %collective-permute-start.13 = (bf16[3,2,32,1024]{3,2,1,0:T(8,128)(2,1)S(1)}, bf16[3,2,32,1024]{3,2,1,0:T(8,128)(2,1)S(1)}, u32[]{:S(2)}, u32[]{:S(2)}) collective-permute-start(bf16[3,2,32,1024]{3,2,1,0:T(8,128)(2,1)S(1)} %pad_maximum_fusion.refs_0_), channel_id=1, source_target_pairs={{0,24},{8,16},{16,8},{24,0},{1,25},{9,17},{17,9},{25,1},{2,26},{10... | collective-permute-start | bytes 1179656 | tf_op jit(solution)/shard_map/ppermute | solution.py:302
  22.6 14.6 %collective-permute-start.5 = (f32[64,128]{1,0:T(8,128)}, f32[64,128]{1,0:T(8,128)S(1)}, u32[]{:S(2)}, u32[]{:S(2)}) collective-permute-start(f32[64,128]{1,0:T(8,128)} %get-tuple-element.33), channel_id=1, source_target_pairs={{0,8},{8,0},{16,24},{24,16},{1,9},{9,1},{17,25},{25,17},{2,10},{10... | collective-permute-start | bytes 98312 | tf_op jit(solution)/shard_map/ppermute | solution.py:302
  24.1 15.7 %collective-permute-start.6 = (f32[64,128]{1,0:T(8,128)}, f32[64,128]{1,0:T(8,128)S(1)}, u32[]{:S(2)}, u32[]{:S(2)}) collective-permute-start(f32[64,128]{1,0:T(8,128)} %get-tuple-element.33), channel_id=1, source_target_pairs={{0,16},{8,24},{16,0},{24,8},{1,17},{9,25},{17,1},{25,9},{2,18},{10... | collective-permute-start | bytes 98312 | tf_op jit(solution)/shard_map/ppermute | solution.py:302
  37.2 5.0 %collective-permute-start.7 = (f32[64,128]{1,0:T(8,128)}, f32[64,128]{1,0:T(8,128)S(1)}, u32[]{:S(2)}, u32[]{:S(2)}) collective-permute-start(f32[64,128]{1,0:T(8,128)} %get-tuple-element.33), channel_id=1, source_target_pairs={{0,24},{8,16},{16,8},{24,0},{1,25},{9,17},{17,9},{25,1},{2,26},{10... | collective-permute-start | bytes 98312 | tf_op jit(solution)/shard_map/ppermute | solution.py:302
  42.2 21.1 %copy-start.6 = (bf16[512,128]{1,0:T(8,128)(2,1)S(1)}, bf16[512,128]{1,0:T(8,128)(2,1)}, u32[]{:S(2)}) copy-start(bf16[512,128]{1,0:T(8,128)(2,1)} %get-tuple-element.37.refs_8_) | copy-start | bytes 393220
  43.0 5.8 %collective-permute-start.10 = (f32[64,128]{1,0:T(8,128)S(1)}, f32[64,128]{1,0:T(8,128)S(1)}, u32[]{:S(2)}, u32[]{:S(2)}) collective-permute-start(f32[64,128]{1,0:T(8,128)S(1)} %add_add_fusion.1), channel_id=1, source_target_pairs={{0,6},{1,7},{2,4},{3,5},{4,2},{5,3},{6,0},{7,1},{8,14},{9,15},{10,... | collective-permute-start | bytes 98312 | tf_op jit(solution)/shard_map/ppermute | solution.py:302
  45.9 16.2 %collective-permute-start.8 = (f32[64,128]{1,0:T(8,128)S(1)}, f32[64,128]{1,0:T(8,128)S(1)}, u32[]{:S(2)}, u32[]{:S(2)}) collective-permute-start(f32[64,128]{1,0:T(8,128)S(1)} %add_add_fusion.1), channel_id=1, source_target_pairs={{0,2},{1,3},{2,0},{3,1},{4,6},{5,7},{6,4},{7,5},{8,10},{9,11},{10,... | collective-permute-start | bytes 98312 | tf_op jit(solution)/shard_map/ppermute | solution.py:302
  48.8 13.3 %collective-permute-start.9 = (f32[64,128]{1,0:T(8,128)S(1)}, f32[64,128]{1,0:T(8,128)S(1)}, u32[]{:S(2)}, u32[]{:S(2)}) collective-permute-start(f32[64,128]{1,0:T(8,128)S(1)} %add_add_fusion.1), channel_id=1, source_target_pairs={{0,4},{1,5},{2,6},{3,7},{4,0},{5,1},{6,2},{7,3},{8,12},{9,13},{10,... | collective-permute-start | bytes 98312 | tf_op jit(solution)/shard_map/ppermute | solution.py:302
  62.1 10.4 %collective-permute-start.14 = (bf16[3,2,32,1024]{3,2,1,0:T(8,128)(2,1)S(1)}, bf16[3,2,32,1024]{3,2,1,0:T(8,128)(2,1)S(1)}, u32[]{:S(2)}, u32[]{:S(2)}) collective-permute-start(bf16[3,2,32,1024]{3,2,1,0:T(8,128)(2,1)S(1)} %pad_maximum_fusion.refs_0_), channel_id=1, source_target_pairs={{0,1},{1,0},{2,3},{3,2},{4,5},{5,4},{6,7},{7,6},{8,9},{9,8},{10,11... | collective-permute-start | bytes 1179656 | tf_op jit(solution)/shard_map/ppermute | solution.py:302
  62.2 10.3 %collective-permute-start.15 = (bf16[3,2,32,1024]{3,2,1,0:T(8,128)(2,1)S(1)}, bf16[3,2,32,1024]{3,2,1,0:T(8,128)(2,1)S(1)}, u32[]{:S(2)}, u32[]{:S(2)}) collective-permute-start(bf16[3,2,32,1024]{3,2,1,0:T(8,128)(2,1)S(1)} %collective-permute-done.11.refs_1_), channel_id=1, source_target_pairs={{0,1},{1,0},{2,3},{3,2},{4,5},{5,4},{6,7},{7,6},{8,9},{9,8},{10,11... | collective-permute-start | bytes 1179656 | tf_op jit(solution)/shard_map/ppermute | solution.py:302
  62.7 9.8 %collective-permute-start.16 = (bf16[3,2,32,1024]{3,2,1,0:T(8,128)(2,1)S(1)}, bf16[3,2,32,1024]{3,2,1,0:T(8,128)(2,1)S(1)}, u32[]{:S(2)}, u32[]{:S(2)}) collective-permute-start(bf16[3,2,32,1024]{3,2,1,0:T(8,128)(2,1)S(1)} %collective-permute-done.12.refs_2_), channel_id=1, source_target_pairs={{0,1},{1,0},{2,3},{3,2},{4,5},{5,4},{6,7},{7,6},{8,9},{9,8},{10,11... | collective-permute-start | bytes 1179656 | tf_op jit(solution)/shard_map/ppermute | solution.py:302
  62.8 9.8 %collective-permute-start.17 = (bf16[3,2,32,1024]{3,2,1,0:T(8,128)(2,1)S(1)}, bf16[3,2,32,1024]{3,2,1,0:T(8,128)(2,1)S(1)}, u32[]{:S(2)}, u32[]{:S(2)}) collective-permute-start(bf16[3,2,32,1024]{3,2,1,0:T(8,128)(2,1)S(1)} %collective-permute-done.13.refs_3_), channel_id=1, source_target_pairs={{0,1},{1,0},{2,3},{3,2},{4,5},{5,4},{6,7},{7,6},{8,9},{9,8},{10,11... | collective-permute-start | bytes 1179656 | tf_op jit(solution)/shard_map/ppermute | solution.py:302
  63.2 9.3 %collective-permute-start.18 = (f32[64,128]{1,0:T(8,128)S(1)}, f32[64,128]{1,0:T(8,128)S(1)}, u32[]{:S(2)}, u32[]{:S(2)}) collective-permute-start(f32[64,128]{1,0:T(8,128)S(1)} %add_add_fusion.refs_10_), channel_id=1, source_target_pairs={{0,1},{1,0},{2,3},{3,2},{4,5},{5,4},{6,7},{7,6},{8,9},{9,8},{10,11... | collective-permute-start | bytes 98312 | tf_op jit(solution)/shard_map/ppermute | solution.py:302
  (6 other events, 21.3 us)

commit v4 on v3

--- a/solution.py
+++ b/solution.py
@@ -55,39 +55,56 @@
     )(first, second)
 
 
-def prepare_kernel(
-    span, lengths, x, g, xv, gv, down_t, up, columns, rows_t,
-    top_out, bottom_out, proj_out,
-    xs, gs, xvs, gvs, downs, ups, tables, sems,
-):
-    width = x.shape[1]
-    steps = width // span
+def load(pairs, sems):
+    steps = sems.shape[0]
     copies = []
     for i in range(steps):
-        cols = pl.ds(i * span, span)
-        pairs = [(up, ups), (g, gs), (down_t, downs), (x, xs), (xv, xvs), (gv, gvs)]
-        step = [
-            pltpu.make_async_copy(source.at[:, cols], target.at[:, cols], sems.at[i, k])
-            for k, (source, target) in enumerate(pairs)
-        ]
-        step.append(pltpu.make_async_copy(columns.at[cols, :], tables.at[cols, :], sems.at[i, len(pairs)]))
+        step = []
+        for k, (source, target, axis) in enumerate(pairs):
+            span = source.shape[axis] // steps
+            at = (slice(None),) * axis + (pl.ds(i * span, span),)
+            step.append(pltpu.make_async_copy(source.at[at], target.at[at], sems.at[i, k]))
         copies.append(step)
     for step in copies:
         for copy in step:
             copy.start()
-    back = fwd = vback = vfwd = xc = gc = 0.0
+    return copies
+
+
+def validation_kernel(xv, gv, down_t, up, columns, rows_t, proj_out, xvs, gvs, downs, ups, tables, sems):
+    pairs = [(xv, xvs, 1), (gv, gvs, 1), (up, ups, 1), (down_t, downs, 1), (columns, tables, 0)]
+    copies = load(pairs, sems)
+    steps = len(copies)
+    span = xv.shape[1] // steps
+    tokens = xv.shape[0]
     k2 = columns.shape[1]
+    back = fwd = mixed = 0.0
     for i in range(steps):
         for copy in copies[i]:
             copy.wait()
         cols = pl.ds(i * span, span)
         table = jnp.concatenate(two_terms(tables[cols, :]), axis=1)
+        back = back + mm(gvs[:, cols], ups[:, cols], NT)
+        fwd = fwd + mm(xvs[:, cols], downs[:, cols], NT)
+        mixed = mixed + mm(jnp.concatenate([xvs[:, cols], gvs[:, cols]], axis=0), table)
+    mixed = mixed[:, :k2] + mixed[:, k2:]
+    inner_top = mm(back.astype(jnp.bfloat16).astype(jnp.float32), mixed[:tokens], TN, HIGHEST)
+    inner_bottom = mm(fwd.astype(jnp.bfloat16).astype(jnp.float32), mixed[tokens:], TN, HIGHEST)
+    inner = jnp.concatenate([inner_top, inner_bottom], axis=0)
+    proj_out[...] = mm(rows_t[...], inner, NN, HIGHEST)
+
+
+def prepare_kernel(lengths, x, g, down_t, up, top_out, bottom_out, xs, gs, downs, ups, sems):
+    copies = load([(g, gs, 1), (up, ups, 1), (x, xs, 1), (down_t, downs, 1)], sems)
+    steps = len(copies)
+    span = x.shape[1] // steps
+    back = fwd = 0.0
+    for i in range(steps):
+        for copy in copies[i]:
+            copy.wait()
+        cols = pl.ds(i * span, span)
         back = back + mm(gs[:, cols], ups[:, cols], NT)
         fwd = fwd + mm(xs[:, cols], downs[:, cols], NT)
-        vback = vback + mm(gvs[:, cols], ups[:, cols], NT)
-        vfwd = vfwd + mm(xvs[:, cols], downs[:, cols], NT)
-        xc = xc + mm(xvs[:, cols], table)
-        gc = gc + mm(gvs[:, cols], table)
     tokens, rank = back.shape
     position = lax.broadcasted_iota(jnp.int32, (rank, tokens), 1)
     back_t = back.T
@@ -99,39 +116,42 @@
         top_out[pl.ds(e * rank, rank), :] = jnp.where(member, back_t, 0.0).astype(jnp.bfloat16)
         bottom_out[pl.ds(e * rank, rank), :] = jnp.where(member, fwd_t, 0.0).astype(jnp.bfloat16)
         begin = finish
-    round_b = vback.astype(jnp.bfloat16).astype(jnp.float32)
-    round_f = vfwd.astype(jnp.bfloat16).astype(jnp.float32)
-    inner_top = mm(round_b, xc[:, :k2] + xc[:, k2:], TN, HIGHEST)
-    inner_bottom = mm(round_f, gc[:, :k2] + gc[:, k2:], TN, HIGHEST)
-    inner = jnp.concatenate([inner_top, inner_bottom], axis=0)
-    proj_out[...] = mm(rows_t[...], inner, NN, HIGHEST)
-
-
-def prepare(lengths, x, g, xv, gv, down_t, up, columns, rows_t):
-    tokens, width = x.shape
-    rank = up.shape[0]
-    k1, k2 = rows_t.shape[0], columns.shape[1]
-    examples = lengths.shape[0]
-    span = 2048
+
+
+STEPS = 4
+
+
+def validation(xv, gv, down_t, up, columns, rows_t):
     return pl.pallas_call(
-        functools.partial(prepare_kernel, span),
-        in_specs=[SMEM] + [ANY] * 7 + [VMEM],
-        out_specs=[VMEM] * 3,
-        out_shape=[
-            jax.ShapeDtypeStruct((examples * rank, tokens), jnp.bfloat16),
-            jax.ShapeDtypeStruct((examples * rank, tokens), jnp.bfloat16),
-            jax.ShapeDtypeStruct((k1, k2), jnp.float32),
-        ],
+        validation_kernel,
+        in_specs=[ANY] * 5 + [VMEM],
+        out_specs=VMEM,
+        out_shape=jax.ShapeDtypeStruct((rows_t.shape[0], columns.shape[1]), jnp.float32),
         scratch_shapes=[
-            *(pltpu.VMEM(a.shape, a.dtype) for a in (x, g, xv, gv, down_t, up, columns)),
-            pltpu.SemaphoreType.DMA((width // span, 7)),
+            *(pltpu.VMEM(a.shape, a.dtype) for a in (xv, gv, down_t, up, columns)),
+            pltpu.SemaphoreType.DMA((STEPS, 5)),
         ],
         compiler_params=pltpu.CompilerParams(vmem_limit_bytes=VMEM_LIMIT),
-        cost_estimate=pl.CostEstimate(
-            flops=4 * tokens * width * rank, bytes_accessed=20_000_000, transcendentals=0
-        ),
+        cost_estimate=pl.CostEstimate(flops=10**6, bytes_accessed=10**6, transcendentals=0),
+        name="validation",
+    )(xv, gv, down_t, up, columns, rows_t)
+
+
+def prepare(lengths, x, g, down_t, up):
+    shape = jax.ShapeDtypeStruct((lengths.shape[0] * up.shape[0], x.shape[0]), jnp.bfloat16)
+    return pl.pallas_call(
+        prepare_kernel,
+        in_specs=[SMEM] + [ANY] * 4,
+        out_specs=[VMEM] * 2,
+        out_shape=[shape, shape],
+        scratch_shapes=[
+            *(pltpu.VMEM(a.shape, a.dtype) for a in (x, g, down_t, up)),
+            pltpu.SemaphoreType.DMA((STEPS, 4)),
+        ],
+        compiler_params=pltpu.CompilerParams(vmem_limit_bytes=VMEM_LIMIT),
+        cost_estimate=pl.CostEstimate(flops=10**6, bytes_accessed=10**6, transcendentals=0),
         name="prepare",
-    )(lengths, x, g, xv, gv, down_t, up, columns, rows_t)
+    )(lengths, x, g, down_t, up)
 
 
 def accumulate(block_of, copies_of, moments, slots, x, g, columns, top, bottom, xs, gs, cs, ms, update, inner, sems):
@@ -144,31 +164,47 @@
         pairs = [(x.at[:, cols], xs.at[b]), (g.at[:, cols], gs.at[b]), (columns.at[cols, :], cs.at[b])]
         pairs += copies_of(moments, b, ms.at[b])
         copies.append([pltpu.make_async_copy(p[0], p[1], sems.at[b, k]) for k, p in enumerate(pairs)])
-    for block in copies:
-        for copy in block:
-            copy.start()
+    for copy in copies[0]:
+        copy.start()
     inner[...] = jnp.zeros_like(inner)
     cut = min(span, 256)
     half_parts = ms.shape[1] // 2
-    for b in range(count):
-        for copy in copies[b]:
-            copy.wait()
-        table = jnp.concatenate(two_terms(cs[b]), axis=1)
-        for half, (source, masked) in enumerate(((xs, top), (gs, bottom))):
-            parts = slice(half * half_parts, (half + 1) * half_parts)
-            for c in range(0, span, cut):
-                cols = pl.ds(c, cut)
-                grad = mm(masked[...], source[b, :, cols])
-                first = 9.0 * ms[b, parts, 0, :, cols].astype(jnp.float32).reshape(rank, cut)
-                second = 999.0 * ms[b, parts, 1, :, cols].astype(jnp.float32).reshape(rank, cut)
-                shared = first * lax.rsqrt(second)
-                coarse, fine = two_terms(shared)
-                update[half, pl.ds(examples * rank, rank), cols] = coarse
-                update[half, pl.ds((examples + 1) * rank, rank), cols] = fine
-                for e in range(examples):
-                    piece = grad[e * rank : (e + 1) * rank]
-                    change = (first + piece) * lax.rsqrt(second + piece * piece) - shared
-                    update[half, pl.ds(e * rank, rank), cols] = change.astype(jnp.bfloat16)
+    tiles = [(b, half, c) for b in range(count) for half in (0, 1) for c in range(0, span, cut)]
+    sources, masks = (xs, gs), (top, bottom)
+
+    def gradient(tile):
+        b, half, c = tile
+        if half == 0 and c == 0:
+            for copy in copies[b]:
+                copy.wait()
+            if b + 1 < count:
+                for copy in copies[b + 1]:
+                    copy.start()
+        return mm(masks[half][...], sources[half][b, :, pl.ds(c, cut)])
+
+    def elementwise(tile, grad):
+        b, half, c = tile
+        cols = pl.ds(c, cut)
+        parts = slice(half * half_parts, (half + 1) * half_parts)
+        first = 9.0 * ms[b, parts, 0, :, cols].astype(jnp.float32).reshape(rank, cut)
+        second = 999.0 * ms[b, parts, 1, :, cols].astype(jnp.float32).reshape(rank, cut)
+        shared = first * lax.rsqrt(second)
+        coarse, fine = two_terms(shared)
+        update[half, pl.ds(examples * rank, rank), cols] = coarse
+        update[half, pl.ds((examples + 1) * rank, rank), cols] = fine
+        for e in range(examples):
+            piece = grad[e * rank : (e + 1) * rank]
+            change = (first + piece) * lax.rsqrt(second + piece * piece) - shared
+            update[half, pl.ds(e * rank, rank), cols] = change.astype(jnp.bfloat16)
+
+    grad = gradient(tiles[0])
+    for i, tile in enumerate(tiles):
+        following = gradient(tiles[i + 1]) if i + 1 < len(tiles) else None
+        elementwise(tile, grad)
+        grad = following
+        b, half, c = tile
+        if c + cut == span:
+            table = jnp.concatenate(two_terms(cs[b]), axis=1)
             inner[half] += mm(update[half], table)
 
 
@@ -302,10 +338,6 @@
     return lax.ppermute(value, axis, [(i, i ^ bits) for i in range(size)])
 
 
-def spread_sum(own, others):
-    return (own + others[0]) + (others[1] + others[2])
-
-
 def body(
     training_inputs,
     training_cotangents,
@@ -333,31 +365,30 @@
         piece = cut_piece(*own)
         sibling = [exchange(m, "shard", 1) for m in own]
         far = [exchange(piece, "shard", 2 * hop) for hop in (1, 2, 3)]
-    top, bottom, val_part = prepare(
-        example_lengths[0, 0],
-        *train,
-        validation_inputs,
-        validation_cotangents,
-        adapter_down.T,
-        adapter_up,
-        projection_columns,
-        rows_t,
-    )
+        validation_inputs, _ = lax.optimization_barrier((validation_inputs, piece))
+    down_t = adapter_down.T
+    val_part = validation(
+        validation_inputs, validation_cotangents, down_t, adapter_up, projection_columns, rows_t
+    )
+    lengths, val_part = lax.optimization_barrier((example_lengths[0, 0], val_part))
+    top, bottom = prepare(lengths, *train, down_t, adapter_up)
     if stepwise:
-        *arrived, top, bottom, val_part = lax.optimization_barrier((*far, *sibling, top, bottom, val_part))
-        far, sibling = jnp.stack(arrived[:3]), arrived[3:]
+        val_part, *sibling, far[0] = lax.optimization_barrier((val_part, *sibling, far[0]))
+        near = [exchange(val_part, "dp", bits) for bits in (1, 2, 3)]
+        *arrived, top, bottom = lax.optimization_barrier((*far, *near, top, bottom))
+        far, near = jnp.stack(arrived[:3]), arrived[3:]
         four = [far] + [exchange(far, "dp", bits) for bits in (1, 2, 3)]
-        total = spread_sum(val_part, [exchange(val_part, "dp", bits) for bits in (1, 2, 3)])
+        total = (val_part + near[0]) + (near[1] + near[2])
+        total = total + exchange(total, "shard", 2)
         total, top, bottom = lax.optimization_barrier((total, top, bottom))
-        others = [exchange(total, "shard", 2 * bits) for bits in (1, 2, 3)]
+        other = exchange(total, "shard", 4)
         operands = (*train, projection_columns, top, bottom)
         first = chunk(
             slot_block_index, 2, lambda b: slot_at(b, 0), copies_of_blocks, 2, parts, own + sibling, *operands
         )
-        first, *arrived = lax.optimization_barrier((first, *others, *four))
-        total = spread_sum(total, arrived[:3])
+        first, other, *four = lax.optimization_barrier((first, other, *four))
+        total = total + other
         val_parts = [total, exchange(total, "shard", 1)]
-        four = arrived[3:]
         crossed = [exchange(part, "shard", 1) for part in four]
         second = chunk(
             slot_block_index, 3, lambda b: slot_at(0, b + 1), copies_of_pieces, 4, parts, four, *operands

time: 85.7 us -> 67.7 us (0.79)
  waiting for transfers between devices: 17.3 us -> 3.06 us
  starting transfers between devices: 24.1 us -> 18.2 us
  Pallas kernels: 35.9 us -> 38.7 us
    ppermute x19 -> x18, waiting for transfers between devices: 17.3 us -> 3.06 us  [exchange(): return lax.ppermute(value, axis, [(i, i ^ bits) for i in range(size)])]
    ppermute x19 -> x18, starting transfers between devices: 24.1 us -> 18.2 us  [exchange(): return lax.ppermute(value, axis, [(i, i ^ bits) for i in range(size)])]
    pallas_call x1 -> x2, Pallas kernels: 8.12 us -> 10.9 us  [the longest x1 5.99 us: validation(): pl.pallas_call(validation_kernel, in_specs=[ANY] * 5 + [VMEM], out_specs=...]
    unnamed x22 -> x24, local copies, waits for them, and re-layouts: 5.61 us -> 5.62 us
  transfers between devices with their start and end apart: 19 -> 18, of which waited for: 4 -> 1; matrix products, arithmetic and copies ran while one was open for 1% -> 0% of each run, Pallas kernels for 28% -> 40%
where the time goes in v4:
time: 67.7 us; the launch traced here: 67.3 us
  Pallas kernels  38.7 us (57%)
  starting transfers between devices  18.2 us (27%)
  local copies, waits for them, and re-layouts  6.37 us (9%)
  waiting for transfers between devices  3.06 us (5%)
  between operations  0.9 us (1%)
    ppermute x18, starting transfers between devices, exchange(): return lax.ppermute(value, axis, [(i, i ^ bits) for i in range(size)])  18.2 us
    pallas_call x2, Pallas kernels, chunk(): pl.pallas_call(functools.partial(chunk_kernel, block_of, copies_of, len(m...  14.3 us
    pallas_call x1, Pallas kernels, chunk(): pl.pallas_call(functools.partial(last_kernel, block_of, copies_of, len(mo...  12 us
    pallas_call x1, Pallas kernels, validation(): pl.pallas_call(validation_kernel, in_specs=[ANY] * 5 + [VMEM], out_specs=...  5.99 us
    unnamed x24, local copies, waits for them, and re-layouts  5.62 us
    pallas_call x1, Pallas kernels, prepare(): pl.pallas_call(prepare_kernel, in_specs=[SMEM] + [ANY] * 4, out_specs=[VM...  4.92 us
    ppermute x18, waiting for transfers between devices, exchange(): return lax.ppermute(value, axis, [(i, i ^ bits) for i in range(size)])  3.06 us
    pallas_call x1, Pallas kernels, cut_piece(): pl.pallas_call(cut_kernel, in_specs=[ANY, ANY], out_specs=VMEM, out_shape...  1.54 us
  transfers between devices with their start and end apart: 18, of which 1 were waited for; matrix products, arithmetic and copies ran while one was open for 0% of the time, Pallas kernels for 40%

profile of v4, /device:TPU:0, one launch (start us, length us, event | category | flops | bytes accessed | tf_op | source)
XLA Modules:
  0.0 67.3 jit_solution(16438746752249928744)
XLA Ops:
  0.6 0.5 collective-permute-start
  1.2 1.5 %cut_piece.1 = bf16[2,32,1024]{2,1,0:T(8,128)(2,1)} custom-call(bf16[4,32,1024]{2,1,0:T(8,128)(2,1)} %bitcast.11, bf16[4,32,1024]{2,1,0:T(8,128)(2,1)} %bitcast.14), custom_call_target="tpu_custom_call" | custom-call | tf_op jit(solution)/shard_map/cut_piece/pallas_call | solution.py:47
  2.8 3.1 %collective-permute-start.2 = (bf16[2,32,1024]{2,1,0:T(8,128)(2,1)}, bf16[2,32,1024]{2,1,0:T(8,128)(2,1)S(1)}, u32[]{:S(2)}, u32[]{:S(2)}) collective-permute-start(bf16[2,32,1024]{2,1,0:T(8,128)(2,1)} %cut_piece.1), channel_id=1, source_target_pairs={{0,2},{1,3},{2,0},{3,1},{4,6},{5,7},{6,4},{7,5},{8,10},{9,11},{10,... | collective-permute-start | bytes 393224 | tf_op jit(solution)/shard_map/ppermute | solution.py:338
  5.8 2.6 %collective-permute-start.3 = (bf16[2,32,1024]{2,1,0:T(8,128)(2,1)}, bf16[2,32,1024]{2,1,0:T(8,128)(2,1)S(1)}, u32[]{:S(2)}, u32[]{:S(2)}) collective-permute-start(bf16[2,32,1024]{2,1,0:T(8,128)(2,1)} %cut_piece.1), channel_id=1, source_target_pairs={{0,4},{1,5},{2,6},{3,7},{4,0},{5,1},{6,2},{7,3},{8,12},{9,13},{10,... | collective-permute-start | bytes 393224 | tf_op jit(solution)/shard_map/ppermute | solution.py:338
  8.4 6.0 %validation.1 = f32[64,128]{1,0:T(8,128)} custom-call(bf16[32,8192]{1,0:T(8,128)(2,1)} %xv, bf16[32,8192]{1,0:T(8,128)(2,1)} %gv.1, bf16[64,8192]{1,0:T(8,128)(2,1)} %bitcast.18, bf16[64,8192]{1,0:T(8,128)(2,1)} %up.3, f32[8192,128]{1,0:T(8,128)} %refs_6_.5, f32[64,128]{1,0:T(8,128)} %bitcast.16), custom_call_target="tpu_custom_call" | custom-call | flops 1000000 | bytes 1000000 | tf_op jit(solution)/shard_map/validation/pallas_call | solution.py:125
  14.5 1.8 %collective-permute-start.5 = (f32[64,128]{1,0:T(8,128)}, f32[64,128]{1,0:T(8,128)S(1)}, u32[]{:S(2)}, u32[]{:S(2)}) collective-permute-start(f32[64,128]{1,0:T(8,128)} %validation.1), channel_id=1, source_target_pairs={{0,8},{8,0},{16,24},{24,16},{1,9},{9,1},{17,25},{25,17},{2,10},{10... | collective-permute-start | bytes 98312 | tf_op jit(solution)/shard_map/ppermute | solution.py:338
  16.3 1.5 %collective-permute-start.6 = (f32[64,128]{1,0:T(8,128)}, f32[64,128]{1,0:T(8,128)S(1)}, u32[]{:S(2)}, u32[]{:S(2)}) collective-permute-start(f32[64,128]{1,0:T(8,128)} %validation.1), channel_id=1, source_target_pairs={{0,16},{8,24},{16,0},{24,8},{1,17},{9,25},{17,1},{25,9},{2,18},{10... | collective-permute-start | bytes 98312 | tf_op jit(solution)/shard_map/ppermute | solution.py:338
  17.8 0.3 collective-permute-start.7
  18.1 4.9 %prepare.1 = (bf16[512,128]{1,0:T(8,128)(2,1)}, bf16[512,128]{1,0:T(8,128)(2,1)}) custom-call(s32[8]{0:T(128)} %bitcast.23, bf16[128,8192]{1,0:T(8,128)(2,1)} %refs_4_.5, bf16[128,8192]{1,0:T(8,128)(2,1)} %refs_5_.5, bf16[64,8192]{1,0:T(8,128)(2,1)} %bitcast.19, bf16[64,8192]{1,0:T(8,128)(2,1)} %up.3), custom_call_target="tpu_custom_call" | custom-call | flops 1000000 | bytes 1000000 | tf_op jit(solution)/shard_map/prepare/pallas_call | solution.py:142
  23.1 1.8 %collective-permute-start.10 = (bf16[3,2,32,1024]{3,2,1,0:T(8,128)(2,1)S(1)}, bf16[3,2,32,1024]{3,2,1,0:T(8,128)(2,1)S(1)}, u32[]{:S(2)}, u32[]{:S(2)}) collective-permute-start(bf16[3,2,32,1024]{3,2,1,0:T(8,128)(2,1)S(1)} %pad_maximum_fusion.refs_0_), channel_id=1, source_target_pairs={{0,8},{8,0},{16,24},{24,16},{1,9},{9,1},{17,25},{25,17},{2,10},{10... | collective-permute-start | bytes 1179656 | tf_op jit(solution)/shard_map/ppermute | solution.py:338
  24.9 1.5 %collective-permute-start.11 = (bf16[3,2,32,1024]{3,2,1,0:T(8,128)(2,1)S(1)}, bf16[3,2,32,1024]{3,2,1,0:T(8,128)(2,1)S(1)}, u32[]{:S(2)}, u32[]{:S(2)}) collective-permute-start(bf16[3,2,32,1024]{3,2,1,0:T(8,128)(2,1)S(1)} %pad_maximum_fusion.refs_0_), channel_id=1, source_target_pairs={{0,16},{8,24},{16,0},{24,8},{1,17},{9,25},{17,1},{25,9},{2,18},{10... | collective-permute-start | bytes 1179656 | tf_op jit(solution)/shard_map/ppermute | solution.py:338
  26.7 1.0 %collective-permute-start.8 = (f32[64,128]{1,0:T(8,128)S(1)}, f32[64,128]{1,0:T(8,128)S(1)}, u32[]{:S(2)}, u32[]{:S(2)}) collective-permute-start(f32[64,128]{1,0:T(8,128)S(1)} %add_add_fusion), channel_id=1, source_target_pairs={{0,2},{1,3},{2,0},{3,1},{4,6},{5,7},{6,4},{7,5},{8,10},{9,11},{10,... | collective-permute-start | bytes 98312 | tf_op jit(solution)/shard_map/ppermute | solution.py:338
  27.6 3.0 %collective-permute-done.8 = f32[64,128]{1,0:T(8,128)S(1)} collective-permute-done((f32[64,128]{1,0:T(8,128)S(1)}, f32[64,128]{1,0:T(8,128)S(1)}, u32[]{:S(2)}, u32[]{:S(2)}) %collective-permute-start.8) | collective-permute-done | bytes 32800 | tf_op jit(solution)/shard_map/ppermute | solution.py:338
  30.7 2.6 %collective-permute-start.9 = (f32[64,128]{1,0:T(8,128)S(1)}, f32[64,128]{1,0:T(8,128)S(1)}, u32[]{:S(2)}, u32[]{:S(2)}) collective-permute-start(f32[64,128]{1,0:T(8,128)S(1)} %add.18), channel_id=1, source_target_pairs={{0,4},{1,5},{2,6},{3,7},{4,0},{5,1},{6,2},{7,3},{8,12},{9,13},{10,... | collective-permute-start | bytes 98312 | tf_op jit(solution)/shard_map/ppermute | solution.py:338
  33.3 2.2 %copy-done = f32[8192,128]{1,0:T(8,128)S(1)} copy-done((f32[8192,128]{1,0:T(8,128)S(1)}, f32[8192,128]{1,0:T(8,128)}, u32[]{:S(2)}) %copy-start) | copy-done | bytes 4194328
  35.5 1.6 %copy-done.3 = bf16[128,8192]{1,0:T(8,128)(2,1)S(1)} copy-done((bf16[128,8192]{1,0:T(8,128)(2,1)S(1)}, bf16[128,8192]{1,0:T(8,128)(2,1)}, u32[]{:S(2)}) %copy-start.3) | copy-done | bytes 2097176
  37.1 0.9 %copy-done.4 = bf16[512,128]{1,0:T(8,128)(2,1)S(1)} copy-done((bf16[512,128]{1,0:T(8,128)(2,1)S(1)}, bf16[512,128]{1,0:T(8,128)(2,1)}, u32[]{:S(2)}) %copy-start.4) | copy-done | bytes 131096
  38.0 0.9 %copy-done.6 = bf16[512,128]{1,0:T(8,128)(2,1)S(1)} copy-done((bf16[512,128]{1,0:T(8,128)(2,1)S(1)}, bf16[512,128]{1,0:T(8,128)(2,1)}, u32[]{:S(2)}) %copy-start.6) | copy-done | bytes 131096
  38.9 5.0 %chunk.2.refs_12_ = f32[2,576,128]{2,1,0:T(8,128)S(1)} custom-call(s32[8]{0:T(128)S(1)} %copy-done.10, bf16[4,32,1024]{2,1,0:T(8,128)(2,1)S(1)} %bitcast.12, bf16[4,32,1024]{2,1,0:T(8,128)(2,1)S(1)} %bitcast.15, bf16[4,32,1024]{2,1,0:T(8,128)(2,1)S(1)} %collective-permute-done.refs_2_, bf16[4,32,1024]{2,1,0:T(8,128)(2,1)S(1)} %collective-permute-done.1.refs_3_, ...), custom_call_target="tpu_custom_call" | custom-call | flops 536870912 | bytes 12000000 | tf_op jit(solution)/shard_map/chunk/pallas_call | solution.py:291
  44.0 0.5 collective-permute-start.14
  44.6 0.4 collective-permute-start.16
  45.2 9.3 %chunk.3.refs_13_ = f32[2,576,128]{2,1,0:T(8,128)S(1)} custom-call(s32[8]{0:T(128)S(1)} %copy-done.10, bf16[3,2,32,1024]{3,2,1,0:T(8,128)(2,1)S(1)} %pad_maximum_fusion.refs_0_, bf16[3,2,32,1024]{3,2,1,0:T(8,128)(2,1)S(1)} %collective-permute-done.10.refs_1_, bf16[3,2,32,1024]{3,2,1,0:T(8,128)(2,1)S(1)} %collective-permute-done.11.refs_2_, ...), custom_call_target="tpu_custom_call" | custom-call | flops 805306368 | bytes 18000000 | tf_op jit(solution)/shard_map/chunk/pallas_call | solution.py:291
  54.6 12.0 %last_chunk.1 = (f32[8,64,128]{2,1,0:T(8,128)S(1)}, f32[64,128]{1,0:T(8,128)}, f32[8]{0:T(128)}) custom-call(s32[8]{0:T(128)S(1)} %copy-done.10, bf16[3,2,32,1024]{3,2,1,0:T(8,128)(2,1)S(1)} %collective-permute-done.13.refs_0_, bf16[3,2,32,1024]{3,2,1,0:T(8,128)(2,1)S(1)} %collective-permute-done.14.refs_1_, ...), custom_call_target="tpu_custom_call" | custom-call | flops 805306368 | bytes 18000000 | tf_op jit(solution)/shard_map/last_chunk/pallas_call | solution.py:303
  66.6 0.8 %reshape.20 = f32[1,1,8,8192]{3,2,1,0:T(8,128)} reshape(f32[8,64,128]{2,1,0:T(8,128)S(1)} %get-tuple-element.58) | data formatting | bytes 524288 | tf_op jit(solution)/shard_map/reshape | solution.py:424
  (47 shorter events, 0.8 us)
Async XLA Ops:
  0.6 13.9 %collective-permute-start = (bf16[4,32,1024]{2,1,0:T(8,128)(2,1)}, bf16[4,32,1024]{2,1,0:T(8,128)(2,1)S(1)}, u32[]{:S(2)}, u32[]{:S(2)}) collective-permute-start(bf16[4,32,1024]{2,1,0:T(8,128)(2,1)} %bitcast.10), channel_id=1, source_target_pairs={{0,1},{1,0},{2,3},{3,2},{4,5},{5,4},{6,7},{7,6},{8,9},{9,8},{10,11... | collective-permute-start | bytes 786440 | tf_op jit(solution)/shard_map/ppermute | solution.py:338
  1.1 13.4 %collective-permute-start.1 = (bf16[4,32,1024]{2,1,0:T(8,128)(2,1)}, bf16[4,32,1024]{2,1,0:T(8,128)(2,1)S(1)}, u32[]{:S(2)}, u32[]{:S(2)}) collective-permute-start(bf16[4,32,1024]{2,1,0:T(8,128)(2,1)} %bitcast.13), channel_id=1, source_target_pairs={{0,1},{1,0},{2,3},{3,2},{4,5},{5,4},{6,7},{7,6},{8,9},{9,8},{10,11... | collective-permute-start | bytes 786440 | tf_op jit(solution)/shard_map/ppermute | solution.py:338
  2.8 11.7 %collective-permute-start.2 = (bf16[2,32,1024]{2,1,0:T(8,128)(2,1)}, bf16[2,32,1024]{2,1,0:T(8,128)(2,1)S(1)}, u32[]{:S(2)}, u32[]{:S(2)}) collective-permute-start(bf16[2,32,1024]{2,1,0:T(8,128)(2,1)} %cut_piece.1), channel_id=1, source_target_pairs={{0,2},{1,3},{2,0},{3,1},{4,6},{5,7},{6,4},{7,5},{8,10},{9,11},{10,... | collective-permute-start | bytes 393224 | tf_op jit(solution)/shard_map/ppermute | solution.py:338
  5.8 17.2 %collective-permute-start.3 = (bf16[2,32,1024]{2,1,0:T(8,128)(2,1)}, bf16[2,32,1024]{2,1,0:T(8,128)(2,1)S(1)}, u32[]{:S(2)}, u32[]{:S(2)}) collective-permute-start(bf16[2,32,1024]{2,1,0:T(8,128)(2,1)} %cut_piece.1), channel_id=1, source_target_pairs={{0,4},{1,5},{2,6},{3,7},{4,0},{5,1},{6,2},{7,3},{8,12},{9,13},{10,... | collective-permute-start | bytes 393224 | tf_op jit(solution)/shard_map/ppermute | solution.py:338
  8.4 14.6 %collective-permute-start.4 = (bf16[2,32,1024]{2,1,0:T(8,128)(2,1)}, bf16[2,32,1024]{2,1,0:T(8,128)(2,1)S(1)}, u32[]{:S(2)}, u32[]{:S(2)}) collective-permute-start(bf16[2,32,1024]{2,1,0:T(8,128)(2,1)} %cut_piece.1), channel_id=1, source_target_pairs={{0,6},{1,7},{2,4},{3,5},{4,2},{5,3},{6,0},{7,1},{8,14},{9,15},{10,... | collective-permute-start | bytes 393224 | tf_op jit(solution)/shard_map/ppermute | solution.py:338
  14.4 12.2 %copy-start.11 = (f32[64,128]{1,0:T(8,128)S(1)}, f32[64,128]{1,0:T(8,128)}, u32[]{:S(2)}) copy-start(f32[64,128]{1,0:T(8,128)} %validation.1) | copy-start | bytes 98308
  14.4 18.9 %copy-start.7 = (bf16[1,128,1024]{2,1,0:T(8,128)(2,1)S(1)}, bf16[1,128,1024]{2,1,0:T(8,128)(2,1)}, u32[]{:S(2)}) copy-start(bf16[1,128,1024]{2,1,0:T(8,128)(2,1)} %param.18) | copy-start | bytes 786436
  14.5 18.9 %copy-start.8 = (bf16[1,128,1024]{2,1,0:T(8,128)(2,1)S(1)}, bf16[1,128,1024]{2,1,0:T(8,128)(2,1)}, u32[]{:S(2)}) copy-start(bf16[1,128,1024]{2,1,0:T(8,128)(2,1)} %param.19) | copy-start | bytes 786436
  14.5 18.9 %copy-start.10 = (s32[8]{0:T(128)S(1)}, s32[8]{0:T(128)}, u32[]{:S(2)}) copy-start(s32[8]{0:T(128)} %slots.5) | copy-start | bytes 100
  14.5 8.5 %collective-permute-start.5 = (f32[64,128]{1,0:T(8,128)}, f32[64,128]{1,0:T(8,128)S(1)}, u32[]{:S(2)}, u32[]{:S(2)}) collective-permute-start(f32[64,128]{1,0:T(8,128)} %validation.1), channel_id=1, source_target_pairs={{0,8},{8,0},{16,24},{24,16},{1,9},{9,1},{17,25},{25,17},{2,10},{10... | collective-permute-start | bytes 98312 | tf_op jit(solution)/shard_map/ppermute | solution.py:338
  16.3 6.7 %collective-permute-start.6 = (f32[64,128]{1,0:T(8,128)}, f32[64,128]{1,0:T(8,128)S(1)}, u32[]{:S(2)}, u32[]{:S(2)}) collective-permute-start(f32[64,128]{1,0:T(8,128)} %validation.1), channel_id=1, source_target_pairs={{0,16},{8,24},{16,0},{24,8},{1,17},{9,25},{17,1},{25,9},{2,18},{10... | collective-permute-start | bytes 98312 | tf_op jit(solution)/shard_map/ppermute | solution.py:338
  17.8 5.2 %collective-permute-start.7 = (f32[64,128]{1,0:T(8,128)}, f32[64,128]{1,0:T(8,128)S(1)}, u32[]{:S(2)}, u32[]{:S(2)}) collective-permute-start(f32[64,128]{1,0:T(8,128)} %validation.1), channel_id=1, source_target_pairs={{0,24},{8,16},{16,8},{24,0},{1,25},{9,17},{17,9},{25,1},{2,26},{10... | collective-permute-start | bytes 98312 | tf_op jit(solution)/shard_map/ppermute | solution.py:338
  18.1 15.3 %copy-start.2 = (bf16[128,8192]{1,0:T(8,128)(2,1)S(1)}, bf16[128,8192]{1,0:T(8,128)(2,1)}, u32[]{:S(2)}) copy-start(bf16[128,8192]{1,0:T(8,128)(2,1)} %refs_4_.5) | copy-start | bytes 6291460
  23.1 20.8 %collective-permute-start.10 = (bf16[3,2,32,1024]{3,2,1,0:T(8,128)(2,1)S(1)}, bf16[3,2,32,1024]{3,2,1,0:T(8,128)(2,1)S(1)}, u32[]{:S(2)}, u32[]{:S(2)}) collective-permute-start(bf16[3,2,32,1024]{3,2,1,0:T(8,128)(2,1)S(1)} %pad_maximum_fusion.refs_0_), channel_id=1, source_target_pairs={{0,8},{8,0},{16,24},{24,16},{1,9},{9,1},{17,25},{25,17},{2,10},{10... | collective-permute-start | bytes 1179656 | tf_op jit(solution)/shard_map/ppermute | solution.py:338
  24.9 19.0 %collective-permute-start.11 = (bf16[3,2,32,1024]{3,2,1,0:T(8,128)(2,1)S(1)}, bf16[3,2,32,1024]{3,2,1,0:T(8,128)(2,1)S(1)}, u32[]{:S(2)}, u32[]{:S(2)}) collective-permute-start(bf16[3,2,32,1024]{3,2,1,0:T(8,128)(2,1)S(1)} %pad_maximum_fusion.refs_0_), channel_id=1, source_target_pairs={{0,16},{8,24},{16,0},{24,8},{1,17},{9,25},{17,1},{25,9},{2,18},{10... | collective-permute-start | bytes 1179656 | tf_op jit(solution)/shard_map/ppermute | solution.py:338
  26.4 17.5 %collective-permute-start.12 = (bf16[3,2,32,1024]{3,2,1,0:T(8,128)(2,1)S(1)}, bf16[3,2,32,1024]{3,2,1,0:T(8,128)(2,1)S(1)}, u32[]{:S(2)}, u32[]{:S(2)}) collective-permute-start(bf16[3,2,32,1024]{3,2,1,0:T(8,128)(2,1)S(1)} %pad_maximum_fusion.refs_0_), channel_id=1, source_target_pairs={{0,24},{8,16},{16,8},{24,0},{1,25},{9,17},{17,9},{25,1},{2,26},{10... | collective-permute-start | bytes 1179656 | tf_op jit(solution)/shard_map/ppermute | solution.py:338
  26.7 4.0 %collective-permute-start.8 = (f32[64,128]{1,0:T(8,128)S(1)}, f32[64,128]{1,0:T(8,128)S(1)}, u32[]{:S(2)}, u32[]{:S(2)}) collective-permute-start(f32[64,128]{1,0:T(8,128)S(1)} %add_add_fusion), channel_id=1, source_target_pairs={{0,2},{1,3},{2,0},{3,1},{4,6},{5,7},{6,4},{7,5},{8,10},{9,11},{10,... | collective-permute-start | bytes 98312 | tf_op jit(solution)/shard_map/ppermute | solution.py:338
  30.7 13.2 %collective-permute-start.9 = (f32[64,128]{1,0:T(8,128)S(1)}, f32[64,128]{1,0:T(8,128)S(1)}, u32[]{:S(2)}, u32[]{:S(2)}) collective-permute-start(f32[64,128]{1,0:T(8,128)S(1)} %add.18), channel_id=1, source_target_pairs={{0,4},{1,5},{2,6},{3,7},{4,0},{5,1},{6,2},{7,3},{8,12},{9,13},{10,... | collective-permute-start | bytes 98312 | tf_op jit(solution)/shard_map/ppermute | solution.py:338
  44.0 10.6 %collective-permute-start.13 = (bf16[3,2,32,1024]{3,2,1,0:T(8,128)(2,1)S(1)}, bf16[3,2,32,1024]{3,2,1,0:T(8,128)(2,1)S(1)}, u32[]{:S(2)}, u32[]{:S(2)}) collective-permute-start(bf16[3,2,32,1024]{3,2,1,0:T(8,128)(2,1)S(1)} %pad_maximum_fusion.refs_0_), channel_id=1, source_target_pairs={{0,1},{1,0},{2,3},{3,2},{4,5},{5,4},{6,7},{7,6},{8,9},{9,8},{10,11... | collective-permute-start | bytes 1179656 | tf_op jit(solution)/shard_map/ppermute | solution.py:338
  44.0 10.5 %collective-permute-start.14 = (bf16[3,2,32,1024]{3,2,1,0:T(8,128)(2,1)S(1)}, bf16[3,2,32,1024]{3,2,1,0:T(8,128)(2,1)S(1)}, u32[]{:S(2)}, u32[]{:S(2)}) collective-permute-start(bf16[3,2,32,1024]{3,2,1,0:T(8,128)(2,1)S(1)} %collective-permute-done.10.refs_1_), channel_id=1, source_target_pairs={{0,1},{1,0},{2,3},{3,2},{4,5},{5,4},{6,7},{7,6},{8,9},{9,8},{10,11... | collective-permute-start | bytes 1179656 | tf_op jit(solution)/shard_map/ppermute | solution.py:338
  44.5 10.1 %collective-permute-start.15 = (bf16[3,2,32,1024]{3,2,1,0:T(8,128)(2,1)S(1)}, bf16[3,2,32,1024]{3,2,1,0:T(8,128)(2,1)S(1)}, u32[]{:S(2)}, u32[]{:S(2)}) collective-permute-start(bf16[3,2,32,1024]{3,2,1,0:T(8,128)(2,1)S(1)} %collective-permute-done.11.refs_2_), channel_id=1, source_target_pairs={{0,1},{1,0},{2,3},{3,2},{4,5},{5,4},{6,7},{7,6},{8,9},{9,8},{10,11... | collective-permute-start | bytes 1179656 | tf_op jit(solution)/shard_map/ppermute | solution.py:338
  44.6 10.0 %collective-permute-start.16 = (bf16[3,2,32,1024]{3,2,1,0:T(8,128)(2,1)S(1)}, bf16[3,2,32,1024]{3,2,1,0:T(8,128)(2,1)S(1)}, u32[]{:S(2)}, u32[]{:S(2)}) collective-permute-start(bf16[3,2,32,1024]{3,2,1,0:T(8,128)(2,1)S(1)} %collective-permute-done.12.refs_3_), channel_id=1, source_target_pairs={{0,1},{1,0},{2,3},{3,2},{4,5},{5,4},{6,7},{7,6},{8,9},{9,8},{10,11... | collective-permute-start | bytes 1179656 | tf_op jit(solution)/shard_map/ppermute | solution.py:338
  45.0 9.6 %copy-start.9 = (f32[128,64]{0,1:T(8,128)S(1)}, f32[128,64]{0,1:T(8,128)}, u32[]{:S(2)}) copy-start(f32[128,64]{0,1:T(8,128)} %param.22) | copy-start | bytes 98308
  45.0 9.5 %collective-permute-start.17 = (f32[64,128]{1,0:T(8,128)S(1)}, f32[64,128]{1,0:T(8,128)S(1)}, u32[]{:S(2)}, u32[]{:S(2)}) collective-permute-start(f32[64,128]{1,0:T(8,128)S(1)} %add.19.refs_10_), channel_id=1, source_target_pairs={{0,1},{1,0},{2,3},{3,2},{4,5},{5,4},{6,7},{7,6},{8,9},{9,8},{10,11... | collective-permute-start | bytes 98312 | tf_op jit(solution)/shard_map/ppermute | solution.py:338
  (6 other events, 18.1 us)

commit v5 on v4

--- a/solution.py
+++ b/solution.py
@@ -33,8 +33,9 @@
 
 def cut_kernel(first, second, out, sems):
     group = lax.axis_index("dp")
+    quarter = first.shape[1]
     copies = [
-        pltpu.make_async_copy(source.at[group], out.at[i], sems.at[i])
+        pltpu.make_async_copy(source.at[group], out.at[pl.ds(i * quarter, quarter)], sems.at[i])
         for i, source in enumerate((first, second))
     ]
     for copy in copies:
@@ -48,45 +49,90 @@
         cut_kernel,
         in_specs=[ANY, ANY],
         out_specs=VMEM,
-        out_shape=jax.ShapeDtypeStruct((2,) + first.shape[1:], first.dtype),
+        out_shape=jax.ShapeDtypeStruct((2 * first.shape[1], first.shape[2]), first.dtype),
         scratch_shapes=[pltpu.SemaphoreType.DMA((2,))],
         compiler_params=pltpu.CompilerParams(vmem_limit_bytes=VMEM_LIMIT),
         name="cut_piece",
     )(first, second)
 
 
-def load(pairs, sems):
+def pack_kernel(first, second, third, val, near1, near2, near3, out):
+    rows = first.shape[0]
+    for i, part in enumerate((first, second, third)):
+        out[pl.ds(i * rows, rows), :] = part[...]
+    total = (val[...] + near1[...]) + (near2[...] + near3[...])
+    wide = fold(total, out.shape[1] // total.shape[1])
+    coarse = wide.astype(jnp.bfloat16).astype(jnp.float32)
+    terms = jnp.concatenate([coarse, wide - coarse], axis=0)
+    out[pl.ds(3 * rows, terms.shape[0]), :] = terms.astype(jnp.bfloat16)
+
+
+def fold(tall, times):
+    rows = tall.shape[0] // times
+    return jnp.concatenate([tall[i * rows : (i + 1) * rows] for i in range(times)], axis=1)
+
+
+def unfold(wide, times):
+    cols = wide.shape[1] // times
+    return jnp.concatenate([wide[:, i * cols : (i + 1) * cols] for i in range(times)], axis=0)
+
+
+def pack(far, val, near):
+    rows, span = far[0].shape
+    return pl.pallas_call(
+        pack_kernel,
+        in_specs=[VMEM] * 7,
+        out_specs=VMEM,
+        out_shape=jax.ShapeDtypeStruct((3 * rows + 2 * val.size // span, span), far[0].dtype),
+        compiler_params=pltpu.CompilerParams(vmem_limit_bytes=CHUNK_LIMIT),
+        name="pack",
+    )(*far, val, *near)
+
+
+def columns_loop(pairs, sems, start, step):
     steps = sems.shape[0]
-    copies = []
-    for i in range(steps):
-        step = []
+
+    def copies(i):
+        found = []
         for k, (source, target, axis) in enumerate(pairs):
             span = source.shape[axis] // steps
-            at = (slice(None),) * axis + (pl.ds(i * span, span),)
-            step.append(pltpu.make_async_copy(source.at[at], target.at[at], sems.at[i, k]))
-        copies.append(step)
-    for step in copies:
-        for copy in step:
+            at = (slice(None),) * axis + (pl.ds(pl.multiple_of(i * span, span), span),)
+            found.append(pltpu.make_async_copy(source.at[at], target.at[at], sems.at[i, k]))
+        return found
+
+    for i in range(steps):
+        for copy in copies(i):
             copy.start()
-    return copies
+    span = pairs[0][0].shape[pairs[0][2]] // steps
+
+    def one(i, total):
+        for copy in copies(i):
+            copy.wait()
+        return step(pl.ds(pl.multiple_of(i * span, span), span), total)
+
+    return lax.fori_loop(0, steps, one, start)
+
+
+def zeros(*shape):
+    return jnp.zeros(shape, jnp.float32)
 
 
 def validation_kernel(xv, gv, down_t, up, columns, rows_t, proj_out, xvs, gvs, downs, ups, tables, sems):
     pairs = [(xv, xvs, 1), (gv, gvs, 1), (up, ups, 1), (down_t, downs, 1), (columns, tables, 0)]
-    copies = load(pairs, sems)
-    steps = len(copies)
-    span = xv.shape[1] // steps
-    tokens = xv.shape[0]
-    k2 = columns.shape[1]
-    back = fwd = mixed = 0.0
-    for i in range(steps):
-        for copy in copies[i]:
-            copy.wait()
-        cols = pl.ds(i * span, span)
+    tokens, rank, k2 = xv.shape[0], up.shape[0], columns.shape[1]
+
+    def step(cols, total):
+        back, fwd, mixed = total
         table = jnp.concatenate(two_terms(tables[cols, :]), axis=1)
-        back = back + mm(gvs[:, cols], ups[:, cols], NT)
-        fwd = fwd + mm(xvs[:, cols], downs[:, cols], NT)
-        mixed = mixed + mm(jnp.concatenate([xvs[:, cols], gvs[:, cols]], axis=0), table)
+        both = jnp.concatenate([xvs[:, cols], gvs[:, cols]], axis=0)
+        return (
+            back + mm(gvs[:, cols], ups[:, cols], NT),
+            fwd + mm(xvs[:, cols], downs[:, cols], NT),
+            mixed + mm(both, table),
+        )
+
+    start = (zeros(tokens, rank), zeros(tokens, rank), zeros(2 * tokens, 2 * k2))
+    back, fwd, mixed = columns_loop(pairs, sems, start, step)
     mixed = mixed[:, :k2] + mixed[:, k2:]
     inner_top = mm(back.astype(jnp.bfloat16).astype(jnp.float32), mixed[:tokens], TN, HIGHEST)
     inner_bottom = mm(fwd.astype(jnp.bfloat16).astype(jnp.float32), mixed[tokens:], TN, HIGHEST)
@@ -95,17 +141,14 @@
 
 
 def prepare_kernel(lengths, x, g, down_t, up, top_out, bottom_out, xs, gs, downs, ups, sems):
-    copies = load([(g, gs, 1), (up, ups, 1), (x, xs, 1), (down_t, downs, 1)], sems)
-    steps = len(copies)
-    span = x.shape[1] // steps
-    back = fwd = 0.0
-    for i in range(steps):
-        for copy in copies[i]:
-            copy.wait()
-        cols = pl.ds(i * span, span)
-        back = back + mm(gs[:, cols], ups[:, cols], NT)
-        fwd = fwd + mm(xs[:, cols], downs[:, cols], NT)
-    tokens, rank = back.shape
+    tokens, rank = x.shape[0], up.shape[0]
+
+    def step(cols, total):
+        back, fwd = total
+        return back + mm(gs[:, cols], ups[:, cols], NT), fwd + mm(xs[:, cols], downs[:, cols], NT)
+
+    pairs = [(g, gs, 1), (up, ups, 1), (x, xs, 1), (down_t, downs, 1)]
+    back, fwd = columns_loop(pairs, sems, (zeros(tokens, rank), zeros(tokens, rank)), step)
     position = lax.broadcasted_iota(jnp.int32, (rank, tokens), 1)
     back_t = back.T
     fwd_t = fwd.T
@@ -118,7 +161,7 @@
         begin = finish
 
 
-STEPS = 4
+STEPS = 8
 
 
 def validation(xv, gv, down_t, up, columns, rows_t):
@@ -156,55 +199,48 @@
 
 def accumulate(block_of, copies_of, moments, slots, x, g, columns, top, bottom, xs, gs, cs, ms, update, inner, sems):
     count, _, span = xs.shape
-    rank = ms.shape[1] * ms.shape[3] // 2
+    quarter = ms.shape[2] // 2
+    rank = ms.shape[1] * quarter // 2
     examples = top.shape[0] // rank
-    copies = []
+    half_parts = ms.shape[1] // 2
+    cut = min(span, 256)
+
+    def copies(b, cols, moment_copies):
+        pairs = [(x.at[:, cols], xs.at[b]), (g.at[:, cols], gs.at[b]), (columns.at[cols, :], cs.at[b])]
+        pairs += moment_copies
+        return [pltpu.make_async_copy(p[0], p[1], sems.at[b, k]) for k, p in enumerate(pairs)]
+
     for b in range(count):
         cols = pl.ds(pl.multiple_of(slots[block_of(b)] * span, span), span)
-        pairs = [(x.at[:, cols], xs.at[b]), (g.at[:, cols], gs.at[b]), (columns.at[cols, :], cs.at[b])]
-        pairs += copies_of(moments, b, ms.at[b])
-        copies.append([pltpu.make_async_copy(p[0], p[1], sems.at[b, k]) for k, p in enumerate(pairs)])
-    for copy in copies[0]:
-        copy.start()
+        for copy in copies(b, cols, copies_of(moments, b, ms.at[b])):
+            copy.start()
     inner[...] = jnp.zeros_like(inner)
-    cut = min(span, 256)
-    half_parts = ms.shape[1] // 2
-    tiles = [(b, half, c) for b in range(count) for half in (0, 1) for c in range(0, span, cut)]
-    sources, masks = (xs, gs), (top, bottom)
-
-    def gradient(tile):
-        b, half, c = tile
-        if half == 0 and c == 0:
-            for copy in copies[b]:
-                copy.wait()
-            if b + 1 < count:
-                for copy in copies[b + 1]:
-                    copy.start()
-        return mm(masks[half][...], sources[half][b, :, pl.ds(c, cut)])
-
-    def elementwise(tile, grad):
-        b, half, c = tile
-        cols = pl.ds(c, cut)
-        parts = slice(half * half_parts, (half + 1) * half_parts)
-        first = 9.0 * ms[b, parts, 0, :, cols].astype(jnp.float32).reshape(rank, cut)
-        second = 999.0 * ms[b, parts, 1, :, cols].astype(jnp.float32).reshape(rank, cut)
-        shared = first * lax.rsqrt(second)
-        coarse, fine = two_terms(shared)
-        update[half, pl.ds(examples * rank, rank), cols] = coarse
-        update[half, pl.ds((examples + 1) * rank, rank), cols] = fine
-        for e in range(examples):
-            piece = grad[e * rank : (e + 1) * rank]
-            change = (first + piece) * lax.rsqrt(second + piece * piece) - shared
-            update[half, pl.ds(e * rank, rank), cols] = change.astype(jnp.bfloat16)
-
-    grad = gradient(tiles[0])
-    for i, tile in enumerate(tiles):
-        following = gradient(tiles[i + 1]) if i + 1 < len(tiles) else None
-        elementwise(tile, grad)
-        grad = following
-        b, half, c = tile
-        if c + cut == span:
-            table = jnp.concatenate(two_terms(cs[b]), axis=1)
+
+    @pl.loop(0, count)
+    def _(b):
+        for copy in copies(b, pl.ds(0, span), copies_of(moments, 0, ms.at[b])):
+            copy.wait()
+
+        @pl.loop(0, span // cut)
+        def _(c):
+            cols = pl.ds(pl.multiple_of(c * cut, cut), cut)
+            grads = [mm(mask[...], source[b, :, cols]) for source, mask in ((xs, top), (gs, bottom))]
+            for half, grad in enumerate(grads):
+                parts = slice(half * half_parts, (half + 1) * half_parts)
+                low, high = pl.ds(0, quarter), pl.ds(quarter, quarter)
+                first = 9.0 * ms[b, parts, low, cols].astype(jnp.float32).reshape(rank, cut)
+                second = 999.0 * ms[b, parts, high, cols].astype(jnp.float32).reshape(rank, cut)
+                shared = first * lax.rsqrt(second)
+                coarse, fine = two_terms(shared)
+                update[half, pl.ds(examples * rank, rank), cols] = coarse
+                update[half, pl.ds((examples + 1) * rank, rank), cols] = fine
+                for e in range(examples):
+                    piece = grad[e * rank : (e + 1) * rank]
+                    change = (first + piece) * lax.rsqrt(second + piece * piece) - shared
+                    update[half, pl.ds(e * rank, rank), cols] = change.astype(jnp.bfloat16)
+
+        table = jnp.concatenate(two_terms(cs[b]), axis=1)
+        for half in (0, 1):
             inner[half] += mm(update[half], table)
 
 
@@ -224,27 +260,44 @@
     accumulate(
         block_of, copies_of, moments, slots, x, g, columns, top, bottom, xs, gs, cs, ms, update, inner, sems
     )
-    rank = ms.shape[1] * ms.shape[3] // 2
+    rank = ms.shape[1] * ms.shape[2] // 4
     examples = top.shape[0] // rank
     for half in (0, 1):
         for e in range(examples + 1):
             out[half, pl.ds(e * rank, rank), :] = folded(inner, half, examples, rank, e)
 
 
-def last_kernel(block_of, copies_of, n_moments, n_partial, slots, *refs):
+def last_kernel(block_of, copies_of, n_moments, n_val, n_partial, slots, *refs):
     moments, refs = refs[:n_moments], refs[n_moments:]
     x, g, columns, top, bottom, rows_t = refs[:6]
-    val_parts, refs = refs[6:8], refs[8:]
+    val_parts, refs = refs[6 : 6 + n_val], refs[6 + n_val :]
     partials, refs = refs[:n_partial], refs[n_partial:]
-    dirs_out, val_out, scores_out, joined, xs, gs, cs, ms, update, inner, sems = refs
+    dirs_out, val_out, scores_out, joined, vals, val_sems, xs, gs, cs, ms, update, inner, sems = refs
+    val_rows = vals.shape[1]
+    val_copies = []
+    if n_val > 1:
+        val_copies = [
+            pltpu.make_async_copy(part.at[pl.ds(part.shape[0] - val_rows, val_rows)], vals.at[i], val_sems.at[i])
+            for i, part in enumerate(val_parts)
+        ]
+    for copy in val_copies:
+        copy.start()
     accumulate(
         block_of, copies_of, moments, slots, x, g, columns, top, bottom, xs, gs, cs, ms, update, inner, sems
     )
-    rank = ms.shape[1] * ms.shape[3] // 2
+    rank = ms.shape[1] * ms.shape[2] // 4
     examples = top.shape[0] // rank
     k1, k2 = rows_t.shape[0], columns.shape[1]
     size = k1 * k2
-    val = val_parts[0][...] + val_parts[1][...]
+    for copy in val_copies:
+        copy.wait()
+    if n_val > 1:
+        terms = [vals[i].astype(jnp.float32) for i in range(n_val)]
+        terms = [term[: val_rows // 2] + term[val_rows // 2 :] for term in terms]
+        half = [(t[0] + t[1]) + (t[2] + t[3]) for t in (terms[:4], terms[4:])]
+        val = unfold(half[0] + half[1], vals.shape[2] // k2)
+    else:
+        val = val_parts[0][...]
     val_dir = val * lax.rsqrt(jnp.sum(val * val) / size + epsilon)
     val_out[...] = val_dir
     rows = rows_t[...] * update_scale
@@ -274,14 +327,14 @@
         pltpu.VMEM((count, tokens, span), jnp.bfloat16),
         pltpu.VMEM((count, tokens, span), jnp.bfloat16),
         pltpu.VMEM((count, span, k2), jnp.float32),
-        pltpu.VMEM((count, pieces, 2, quarter, span), jnp.bfloat16),
+        pltpu.VMEM((count, pieces, 2 * quarter, span), jnp.bfloat16),
         pltpu.VMEM((2, (examples + 2) * rank, span), jnp.bfloat16),
         pltpu.VMEM((2, (examples + 2) * rank, 2 * k2), jnp.float32),
         pltpu.SemaphoreType.DMA((count, 3 + n_copies)),
     ]
     cost = pl.CostEstimate(
-        flops=4 * tokens * span * count * rank * examples,
-        bytes_accessed=6_000_000 * count,
+        flops=10**6,
+        bytes_accessed=10**6,
         transcendentals=0,
     )
     common = [SMEM] + [ANY] * len(moments) + [ANY, ANY, ANY, VMEM, VMEM]
@@ -300,16 +353,23 @@
         )(*operands)
     rows_t, val_parts, partials = last
     k1 = rows_t.shape[0]
+    packed = len(val_parts) > 1
+    val_shape = (len(val_parts), 2 * k1 * k2 // span if packed else 8, span)
     return pl.pallas_call(
-        functools.partial(last_kernel, block_of, copies_of, len(moments), len(partials)),
-        in_specs=common + [VMEM] * (3 + len(partials)),
+        functools.partial(last_kernel, block_of, copies_of, len(moments), len(val_parts), len(partials)),
+        in_specs=common + [VMEM] + [ANY if packed else VMEM] * len(val_parts) + [VMEM] * len(partials),
         out_specs=[VMEM, VMEM, SMEM],
         out_shape=[
             jax.ShapeDtypeStruct((examples, k1, k2), jnp.float32),
             jax.ShapeDtypeStruct((k1, k2), jnp.float32),
             jax.ShapeDtypeStruct((examples,), jnp.float32),
         ],
-        scratch_shapes=[pltpu.VMEM((2 * rank, (examples + 1) * k2), jnp.float32), *scratch],
+        scratch_shapes=[
+            pltpu.VMEM((2 * rank, (examples + 1) * k2), jnp.float32),
+            pltpu.VMEM(val_shape, jnp.bfloat16),
+            pltpu.SemaphoreType.DMA((len(val_parts),)),
+            *scratch,
+        ],
         compiler_params=params,
         cost_estimate=cost,
         name="last_chunk",
@@ -318,15 +378,23 @@
 
 def copies_of_pieces(moments, b, target):
     group = lax.axis_index("dp")
-    return [(piece.at[b], target.at[lax.bitwise_xor(group, j)]) for j, piece in enumerate(moments)]
+    rows = target.shape[1]
+    return [
+        (piece.at[pl.ds(b * rows, rows)], target.at[lax.bitwise_xor(group, j)]) for j, piece in enumerate(moments)
+    ]
+
+
+def both_moments(first, second, target):
+    quarter = target.shape[1] // 2
+    return [(first, target.at[:, pl.ds(0, quarter)]), (second, target.at[:, pl.ds(quarter, quarter)])]
 
 
 def copies_of_blocks(moments, b, target):
-    return [(moments[2 * b + k], target.at[:, k]) for k in (0, 1)]
+    return both_moments(moments[2 * b], moments[2 * b + 1], target)
 
 
 def copies_of_gathered(moments, b, target):
-    return [(moments[k].at[b], target.at[:, k]) for k in (0, 1)]
+    return both_moments(moments[0].at[b], moments[1].at[b], target)
 
 
 def slot_at(other, hop):
@@ -374,21 +442,15 @@
     top, bottom = prepare(lengths, *train, down_t, adapter_up)
     if stepwise:
         val_part, *sibling, far[0] = lax.optimization_barrier((val_part, *sibling, far[0]))
-        near = [exchange(val_part, "dp", bits) for bits in (1, 2, 3)]
+        near = [exchange(val_part, "shard", 2 * hop) for hop in (1, 2, 3)]
         *arrived, top, bottom = lax.optimization_barrier((*far, *near, top, bottom))
-        far, near = jnp.stack(arrived[:3]), arrived[3:]
+        far = pack(arrived[:3], val_part, arrived[3:])
         four = [far] + [exchange(far, "dp", bits) for bits in (1, 2, 3)]
-        total = (val_part + near[0]) + (near[1] + near[2])
-        total = total + exchange(total, "shard", 2)
-        total, top, bottom = lax.optimization_barrier((total, top, bottom))
-        other = exchange(total, "shard", 4)
         operands = (*train, projection_columns, top, bottom)
         first = chunk(
             slot_block_index, 2, lambda b: slot_at(b, 0), copies_of_blocks, 2, parts, own + sibling, *operands
         )
-        first, other, *four = lax.optimization_barrier((first, other, *four))
-        total = total + other
-        val_parts = [total, exchange(total, "shard", 1)]
+        first, *four = lax.optimization_barrier((first, *four))
         crossed = [exchange(part, "shard", 1) for part in four]
         second = chunk(
             slot_block_index, 3, lambda b: slot_at(0, b + 1), copies_of_pieces, 4, parts, four, *operands
@@ -403,7 +465,7 @@
             parts,
             crossed,
             *operands,
-            last=(rows_t, val_parts, partials),
+            last=(rows_t, four + crossed, partials),
         )
     else:
         operands = (*train, projection_columns, top, bottom)
@@ -418,7 +480,7 @@
             parts,
             gathered,
             *operands,
-            last=(rows_t, [val_sum, jnp.zeros_like(val_sum)], []),
+            last=(rows_t, [val_sum], []),
         )
     return (
         dirs.reshape(1, 1, dirs.shape[0], -1),

time: 67.7 us -> 72.5 us (1.071)
  Pallas kernels: 38.7 us -> 44.5 us
  starting transfers between devices: 18.2 us -> 15.3 us
  waiting for transfers between devices: 3.06 us -> 5.13 us
    pallas_call x2, Pallas kernels: 14.3 us -> 17.4 us  [chunk(): pl.pallas_call(functools.partial(chunk_kernel, block_of, copies_of, len(m...]
    ppermute x18 -> x15, starting transfers between devices: 18.2 us -> 15.3 us  [exchange(): return lax.ppermute(value, axis, [(i, i ^ bits) for i in range(size)])]
    pallas_call x1, Pallas kernels: 12 us -> 14.4 us  [chunk(): pl.pallas_call(functools.partial(last_kernel, block_of, copies_of, len(mo...]
    ppermute x18 -> x15, waiting for transfers between devices: 3.06 us -> 5.13 us  [exchange(): return lax.ppermute(value, axis, [(i, i ^ bits) for i in range(size)])]
  transfers between devices with their start and end apart: 18 -> 15, of which waited for: 1 -> 2; matrix products, arithmetic and copies ran while one was open for 0% -> 0% of each run, Pallas kernels for 40% -> 42%
where the time goes in v5:
time: 72.5 us; the launch traced here: 72.1 us
  Pallas kernels  44.5 us (61%)
  starting transfers between devices  15.3 us (21%)
  local copies, waits for them, and re-layouts  6.38 us (9%)
  waiting for transfers between devices  5.13 us (7%)
  between operations  0.88 us (1%)
    pallas_call x2, Pallas kernels, chunk(): pl.pallas_call(functools.partial(chunk_kernel, block_of, copies_of, len(m...  17.4 us
    ppermute x15, starting transfers between devices, exchange(): return lax.ppermute(value, axis, [(i, i ^ bits) for i in range(size)])  15.3 us
    pallas_call x1, Pallas kernels, chunk(): pl.pallas_call(functools.partial(last_kernel, block_of, copies_of, len(mo...  14.4 us
    pallas_call x1, Pallas kernels, validation(): pl.pallas_call(validation_kernel, in_specs=[ANY] * 5 + [VMEM], out_specs=...  5.83 us
    unnamed x24, local copies, waits for them, and re-layouts  5.63 us
    pallas_call x1, Pallas kernels, prepare(): pl.pallas_call(prepare_kernel, in_specs=[SMEM] + [ANY] * 4, out_specs=[VM...  5.24 us
    ppermute x15, waiting for transfers between devices, exchange(): return lax.ppermute(value, axis, [(i, i ^ bits) for i in range(size)])  5.13 us
    pallas_call x1, Pallas kernels, cut_piece(): pl.pallas_call(cut_kernel, in_specs=[ANY, ANY], out_specs=VMEM, out_shape...  1.54 us
  transfers between devices with their start and end apart: 15, of which 2 were waited for; matrix products, arithmetic and copies ran while one was open for 0% of the time, Pallas kernels for 42%

profile of v5, /device:TPU:0, one launch (start us, length us, event | category | flops | bytes accessed | tf_op | source)
XLA Modules:
  0.0 72.1 jit_solution(16376625564884734265)
XLA Ops:
  0.6 0.5 collective-permute-start
  1.2 1.5 %cut_piece.1 = bf16[64,1024]{1,0:T(8,128)(2,1)} custom-call(bf16[4,32,1024]{2,1,0:T(8,128)(2,1)} %bitcast.8, bf16[4,32,1024]{2,1,0:T(8,128)(2,1)} %bitcast.11), custom_call_target="tpu_custom_call" | custom-call | tf_op jit(solution)/shard_map/cut_piece/pallas_call | solution.py:48
  2.8 3.1 %collective-permute-start.2 = (bf16[64,1024]{1,0:T(8,128)(2,1)}, bf16[64,1024]{1,0:T(8,128)(2,1)S(1)}, u32[]{:S(2)}, u32[]{:S(2)}) collective-permute-start(bf16[64,1024]{1,0:T(8,128)(2,1)} %cut_piece.1), channel_id=1, source_target_pairs={{0,2},{1,3},{2,0},{3,1},{4,6},{5,7},{6,4},{7,5},{8,10},{9,11},{10,... | collective-permute-start | bytes 393224 | tf_op jit(solution)/shard_map/ppermute | solution.py:406
  5.8 2.5 %collective-permute-start.4 = (bf16[64,1024]{1,0:T(8,128)(2,1)}, bf16[64,1024]{1,0:T(8,128)(2,1)S(1)}, u32[]{:S(2)}, u32[]{:S(2)}) collective-permute-start(bf16[64,1024]{1,0:T(8,128)(2,1)} %cut_piece.1), channel_id=1, source_target_pairs={{0,6},{1,7},{2,4},{3,5},{4,2},{5,3},{6,0},{7,1},{8,14},{9,15},{10,... | collective-permute-start | bytes 393224 | tf_op jit(solution)/shard_map/ppermute | solution.py:406
  8.3 0.1 collective-permute-start.3
  8.4 5.8 %validation.1.val = f32[64,128]{1,0:T(8,128)} custom-call(bf16[32,8192]{1,0:T(8,128)(2,1)} %xv, bf16[32,8192]{1,0:T(8,128)(2,1)} %gv.1, bf16[64,8192]{1,0:T(8,128)(2,1)} %bitcast.15, bf16[64,8192]{1,0:T(8,128)(2,1)} %up.3, f32[8192,128]{1,0:T(8,128)} %refs_6_.5, f32[64,128]{1,0:T(8,128)} %bitcast.13), custom_call_target="tpu_custom_call" | custom-call | flops 1000000 | bytes 1000000 | tf_op jit(solution)/shard_map/validation/pallas_call | solution.py:168
  14.4 3.0 %collective-permute-start.7 = (f32[64,128]{1,0:T(8,128)}, f32[64,128]{1,0:T(8,128)S(1)}, u32[]{:S(2)}, u32[]{:S(2)}) collective-permute-start(f32[64,128]{1,0:T(8,128)} %validation.1.val), channel_id=1, source_target_pairs={{0,6},{1,7},{2,4},{3,5},{4,2},{5,3},{6,0},{7,1},{8,14},{9,15},{10,... | collective-permute-start | bytes 98312 | tf_op jit(solution)/shard_map/ppermute | solution.py:406
  17.4 0.3 collective-permute-start.6
  17.7 1.1 %collective-permute-start.5 = (f32[64,128]{1,0:T(8,128)}, f32[64,128]{1,0:T(8,128)S(1)}, u32[]{:S(2)}, u32[]{:S(2)}) collective-permute-start(f32[64,128]{1,0:T(8,128)} %validation.1.val), channel_id=1, source_target_pairs={{0,2},{1,3},{2,0},{3,1},{4,6},{5,7},{6,4},{7,5},{8,10},{9,11},{10,... | collective-permute-start | bytes 98312 | tf_op jit(solution)/shard_map/ppermute | solution.py:406
  18.8 5.2 %prepare.1 = (bf16[512,128]{1,0:T(8,128)(2,1)}, bf16[512,128]{1,0:T(8,128)(2,1)}) custom-call(s32[8]{0:T(128)} %bitcast.17, bf16[128,8192]{1,0:T(8,128)(2,1)} %refs_4_.5, bf16[128,8192]{1,0:T(8,128)(2,1)} %refs_5_.5, bf16[64,8192]{1,0:T(8,128)(2,1)} %bitcast.16, bf16[64,8192]{1,0:T(8,128)(2,1)} %up.3), custom_call_target="tpu_custom_call" | custom-call | flops 1000000 | bytes 1000000 | tf_op jit(solution)/shard_map/prepare/pallas_call | solution.py:185
  24.2 2.5 %collective-permute-start.10 = (bf16[208,1024]{1,0:T(8,128)(2,1)S(1)}, bf16[208,1024]{1,0:T(8,128)(2,1)S(1)}, u32[]{:S(2)}, u32[]{:S(2)}) collective-permute-start(bf16[208,1024]{1,0:T(8,128)(2,1)S(1)} %pack.1.refs_0_.refs_10_), channel_id=1, source_target_pairs={{0,24},{8,16},{16,8},{24,0},{1,25},{9,17},{17,9},{25,1},{2,26},{10... | collective-permute-start | bytes 1277960 | tf_op jit(solution)/shard_map/ppermute | solution.py:406
  26.7 0.5 collective-permute-start.9
  27.2 0.5 collective-permute-start.8
  27.8 2.2 %copy-done = f32[8192,128]{1,0:T(8,128)S(1)} copy-done((f32[8192,128]{1,0:T(8,128)S(1)}, f32[8192,128]{1,0:T(8,128)}, u32[]{:S(2)}) %copy-start) | copy-done | bytes 4194328
  29.9 1.6 %copy-done.3 = bf16[128,8192]{1,0:T(8,128)(2,1)S(1)} copy-done((bf16[128,8192]{1,0:T(8,128)(2,1)S(1)}, bf16[128,8192]{1,0:T(8,128)(2,1)}, u32[]{:S(2)}) %copy-start.3) | copy-done | bytes 2097176
  31.5 0.9 %copy-done.5 = bf16[512,128]{1,0:T(8,128)(2,1)S(1)} copy-done((bf16[512,128]{1,0:T(8,128)(2,1)S(1)}, bf16[512,128]{1,0:T(8,128)(2,1)}, u32[]{:S(2)}) %copy-start.5) | copy-done | bytes 131096
  32.4 0.9 %copy-done.6 = bf16[512,128]{1,0:T(8,128)(2,1)S(1)} copy-done((bf16[512,128]{1,0:T(8,128)(2,1)S(1)}, bf16[512,128]{1,0:T(8,128)(2,1)}, u32[]{:S(2)}) %copy-start.6) | copy-done | bytes 131096
  33.3 6.3 %chunk.2.refs_18_ = f32[2,576,128]{2,1,0:T(8,128)S(1)} custom-call(s32[8]{0:T(128)S(1)} %copy-done.11, bf16[4,32,1024]{2,1,0:T(8,128)(2,1)S(1)} %bitcast.9, bf16[4,32,1024]{2,1,0:T(8,128)(2,1)S(1)} %bitcast.12, bf16[4,32,1024]{2,1,0:T(8,128)(2,1)S(1)} %collective-permute-done.refs_2_, bf16[4,32,1024]{2,1,0:T(8,128)(2,1)S(1)} %collective-permute-done.1.refs_3_, ...), custom_call_target="tpu_custom_call" | custom-call | flops 1000000 | bytes 1000000 | tf_op jit(solution)/shard_map/chunk/pallas_call | solution.py:344
  39.7 5.0 %collective-permute-done.9.refs_2_.refs_12_ = bf16[208,1024]{1,0:T(8,128)(2,1)S(1)} collective-permute-done((bf16[208,1024]{1,0:T(8,128)(2,1)S(1)}, bf16[208,1024]{1,0:T(8,128)(2,1)S(1)}, u32[]{:S(2)}, u32[]{:S(2)}) %collective-permute-start.9) | collective-permute-done | bytes 426016 | tf_op jit(solution)/shard_map/ppermute | solution.py:406
  44.8 0.5 collective-permute-start.12
  45.3 0.5 collective-permute-start.14
  45.8 11.1 %chunk.3.refs_19_ = f32[2,576,128]{2,1,0:T(8,128)S(1)} custom-call(s32[8]{0:T(128)S(1)} %copy-done.11, bf16[208,1024]{1,0:T(8,128)(2,1)S(1)} %pack.1.refs_0_.refs_10_, bf16[208,1024]{1,0:T(8,128)(2,1)S(1)} %collective-permute-done.8.refs_1_.refs_11_, bf16[208,1024]{1,0:T(8,128)(2,1)S(1)} %collective-permute-done.9.refs_2_.refs_12_, ...), custom_call_target="tpu_custom_call" | custom-call | flops 1000000 | bytes 1000000 | tf_op jit(solution)/shard_map/chunk/pallas_call | solution.py:344
  57.0 14.4 %last_chunk.1 = (f32[8,64,128]{2,1,0:T(8,128)S(1)}, f32[64,128]{1,0:T(8,128)}, f32[8]{0:T(128)}) custom-call(s32[8]{0:T(128)S(1)} %copy-done.11, bf16[208,1024]{1,0:T(8,128)(2,1)S(1)} %collective-permute-done.11.refs_0_.refs_14_, bf16[208,1024]{1,0:T(8,128)(2,1)S(1)} %collective-permute-done.12.refs_1_.refs_15_, ...), custom_call_target="tpu_custom_call" | custom-call | flops 1000000 | bytes 1000000 | tf_op jit(solution)/shard_map/last_chunk/pallas_call | solution.py:358
  71.4 0.8 %reshape.20 = f32[1,1,8,8192]{3,2,1,0:T(8,128)} reshape(f32[8,64,128]{2,1,0:T(8,128)S(1)} %get-tuple-element.50) | data formatting | bytes 524288 | tf_op jit(solution)/shard_map/reshape | solution.py:486
  (38 shorter events, 0.3 us)
Async XLA Ops:
  0.6 13.7 %collective-permute-start = (bf16[4,32,1024]{2,1,0:T(8,128)(2,1)}, bf16[4,32,1024]{2,1,0:T(8,128)(2,1)S(1)}, u32[]{:S(2)}, u32[]{:S(2)}) collective-permute-start(bf16[4,32,1024]{2,1,0:T(8,128)(2,1)} %bitcast.7), channel_id=1, source_target_pairs={{0,1},{1,0},{2,3},{3,2},{4,5},{5,4},{6,7},{7,6},{8,9},{9,8},{10,11... | collective-permute-start | bytes 786440 | tf_op jit(solution)/shard_map/ppermute | solution.py:406
  1.1 13.2 %collective-permute-start.1 = (bf16[4,32,1024]{2,1,0:T(8,128)(2,1)}, bf16[4,32,1024]{2,1,0:T(8,128)(2,1)S(1)}, u32[]{:S(2)}, u32[]{:S(2)}) collective-permute-start(bf16[4,32,1024]{2,1,0:T(8,128)(2,1)} %bitcast.10), channel_id=1, source_target_pairs={{0,1},{1,0},{2,3},{3,2},{4,5},{5,4},{6,7},{7,6},{8,9},{9,8},{10,11... | collective-permute-start | bytes 786440 | tf_op jit(solution)/shard_map/ppermute | solution.py:406
  2.8 11.6 %collective-permute-start.2 = (bf16[64,1024]{1,0:T(8,128)(2,1)}, bf16[64,1024]{1,0:T(8,128)(2,1)S(1)}, u32[]{:S(2)}, u32[]{:S(2)}) collective-permute-start(bf16[64,1024]{1,0:T(8,128)(2,1)} %cut_piece.1), channel_id=1, source_target_pairs={{0,2},{1,3},{2,0},{3,1},{4,6},{5,7},{6,4},{7,5},{8,10},{9,11},{10,... | collective-permute-start | bytes 393224 | tf_op jit(solution)/shard_map/ppermute | solution.py:406
  5.8 18.2 %collective-permute-start.4 = (bf16[64,1024]{1,0:T(8,128)(2,1)}, bf16[64,1024]{1,0:T(8,128)(2,1)S(1)}, u32[]{:S(2)}, u32[]{:S(2)}) collective-permute-start(bf16[64,1024]{1,0:T(8,128)(2,1)} %cut_piece.1), channel_id=1, source_target_pairs={{0,6},{1,7},{2,4},{3,5},{4,2},{5,3},{6,0},{7,1},{8,14},{9,15},{10,... | collective-permute-start | bytes 393224 | tf_op jit(solution)/shard_map/ppermute | solution.py:406
  8.3 15.8 %collective-permute-start.3 = (bf16[64,1024]{1,0:T(8,128)(2,1)}, bf16[64,1024]{1,0:T(8,128)(2,1)S(1)}, u32[]{:S(2)}, u32[]{:S(2)}) collective-permute-start(bf16[64,1024]{1,0:T(8,128)(2,1)} %cut_piece.1), channel_id=1, source_target_pairs={{0,4},{1,5},{2,6},{3,7},{4,0},{5,1},{6,2},{7,3},{8,12},{9,13},{10,... | collective-permute-start | bytes 393224 | tf_op jit(solution)/shard_map/ppermute | solution.py:406
  14.3 9.8 %copy-start.10 = (f32[64,128]{1,0:T(8,128)S(1)}, f32[64,128]{1,0:T(8,128)}, u32[]{:S(2)}) copy-start(f32[64,128]{1,0:T(8,128)} %validation.1.val) | copy-start | bytes 98308
  14.3 13.5 %copy-start.2 = (bf16[128,8192]{1,0:T(8,128)(2,1)S(1)}, bf16[128,8192]{1,0:T(8,128)(2,1)}, u32[]{:S(2)}) copy-start(bf16[128,8192]{1,0:T(8,128)(2,1)} %refs_4_.5) | copy-start | bytes 6291460
  14.3 13.4 %copy-start.7 = (bf16[1,128,1024]{2,1,0:T(8,128)(2,1)S(1)}, bf16[1,128,1024]{2,1,0:T(8,128)(2,1)}, u32[]{:S(2)}) copy-start(bf16[1,128,1024]{2,1,0:T(8,128)(2,1)} %param.18) | copy-start | bytes 786436
  14.3 13.4 %copy-start.8 = (bf16[1,128,1024]{2,1,0:T(8,128)(2,1)S(1)}, bf16[1,128,1024]{2,1,0:T(8,128)(2,1)}, u32[]{:S(2)}) copy-start(bf16[1,128,1024]{2,1,0:T(8,128)(2,1)} %param.19) | copy-start | bytes 786436
  14.3 13.4 %copy-start.11 = (s32[8]{0:T(128)S(1)}, s32[8]{0:T(128)}, u32[]{:S(2)}) copy-start(s32[8]{0:T(128)} %slots.5) | copy-start | bytes 100
  14.4 9.7 %collective-permute-start.7 = (f32[64,128]{1,0:T(8,128)}, f32[64,128]{1,0:T(8,128)S(1)}, u32[]{:S(2)}, u32[]{:S(2)}) collective-permute-start(f32[64,128]{1,0:T(8,128)} %validation.1.val), channel_id=1, source_target_pairs={{0,6},{1,7},{2,4},{3,5},{4,2},{5,3},{6,0},{7,1},{8,14},{9,15},{10,... | collective-permute-start | bytes 98312 | tf_op jit(solution)/shard_map/ppermute | solution.py:406
  17.4 6.7 %collective-permute-start.6 = (f32[64,128]{1,0:T(8,128)}, f32[64,128]{1,0:T(8,128)S(1)}, u32[]{:S(2)}, u32[]{:S(2)}) collective-permute-start(f32[64,128]{1,0:T(8,128)} %validation.1.val), channel_id=1, source_target_pairs={{0,4},{1,5},{2,6},{3,7},{4,0},{5,1},{6,2},{7,3},{8,12},{9,13},{10,... | collective-permute-start | bytes 98312 | tf_op jit(solution)/shard_map/ppermute | solution.py:406
  17.7 6.4 %collective-permute-start.5 = (f32[64,128]{1,0:T(8,128)}, f32[64,128]{1,0:T(8,128)S(1)}, u32[]{:S(2)}, u32[]{:S(2)}) collective-permute-start(f32[64,128]{1,0:T(8,128)} %validation.1.val), channel_id=1, source_target_pairs={{0,2},{1,3},{2,0},{3,1},{4,6},{5,7},{6,4},{7,5},{8,10},{9,11},{10,... | collective-permute-start | bytes 98312 | tf_op jit(solution)/shard_map/ppermute | solution.py:406
  24.2 15.5 %collective-permute-start.10 = (bf16[208,1024]{1,0:T(8,128)(2,1)S(1)}, bf16[208,1024]{1,0:T(8,128)(2,1)S(1)}, u32[]{:S(2)}, u32[]{:S(2)}) collective-permute-start(bf16[208,1024]{1,0:T(8,128)(2,1)S(1)} %pack.1.refs_0_.refs_10_), channel_id=1, source_target_pairs={{0,24},{8,16},{16,8},{24,0},{1,25},{9,17},{17,9},{25,1},{2,26},{10... | collective-permute-start | bytes 1277960 | tf_op jit(solution)/shard_map/ppermute | solution.py:406
  26.7 18.0 %collective-permute-start.9 = (bf16[208,1024]{1,0:T(8,128)(2,1)S(1)}, bf16[208,1024]{1,0:T(8,128)(2,1)S(1)}, u32[]{:S(2)}, u32[]{:S(2)}) collective-permute-start(bf16[208,1024]{1,0:T(8,128)(2,1)S(1)} %pack.1.refs_0_.refs_10_), channel_id=1, source_target_pairs={{0,16},{8,24},{16,0},{24,8},{1,17},{9,25},{17,1},{25,9},{2,18},{10... | collective-permute-start | bytes 1277960 | tf_op jit(solution)/shard_map/ppermute | solution.py:406
  27.2 17.6 %collective-permute-start.8 = (bf16[208,1024]{1,0:T(8,128)(2,1)S(1)}, bf16[208,1024]{1,0:T(8,128)(2,1)S(1)}, u32[]{:S(2)}, u32[]{:S(2)}) collective-permute-start(bf16[208,1024]{1,0:T(8,128)(2,1)S(1)} %pack.1.refs_0_.refs_10_), channel_id=1, source_target_pairs={{0,8},{8,0},{16,24},{24,16},{1,9},{9,1},{17,25},{25,17},{2,10},{10... | collective-permute-start | bytes 1277960 | tf_op jit(solution)/shard_map/ppermute | solution.py:406
  27.7 2.2 %copy-start = (f32[8192,128]{1,0:T(8,128)S(1)}, f32[8192,128]{1,0:T(8,128)}, u32[]{:S(2)}) copy-start(f32[8192,128]{1,0:T(8,128)} %refs_6_.5) | copy-start | bytes 12582916
  33.3 12.5 %copy-start.1 = (f32[8192,128]{1,0:T(8,128)S(1)}, f32[8192,128]{1,0:T(8,128)}, u32[]{:S(2)}) copy-start(f32[8192,128]{1,0:T(8,128)} %refs_6_.5) | copy-start | bytes 12582916
  33.3 12.5 %copy-start.4 = (bf16[128,8192]{1,0:T(8,128)(2,1)S(1)}, bf16[128,8192]{1,0:T(8,128)(2,1)}, u32[]{:S(2)}) copy-start(bf16[128,8192]{1,0:T(8,128)(2,1)} %refs_5_.5) | copy-start | bytes 6291460
  39.7 17.3 %copy-start.9 = (f32[128,64]{0,1:T(8,128)S(1)}, f32[128,64]{0,1:T(8,128)}, u32[]{:S(2)}) copy-start(f32[128,64]{0,1:T(8,128)} %param.22) | copy-start | bytes 98308
  44.8 12.1 %collective-permute-start.11 = (bf16[208,1024]{1,0:T(8,128)(2,1)S(1)}, bf16[208,1024]{1,0:T(8,128)(2,1)S(1)}, u32[]{:S(2)}, u32[]{:S(2)}) collective-permute-start(bf16[208,1024]{1,0:T(8,128)(2,1)S(1)} %pack.1.refs_0_.refs_10_), channel_id=1, source_target_pairs={{0,1},{1,0},{2,3},{3,2},{4,5},{5,4},{6,7},{7,6},{8,9},{9,8},{10,11... | collective-permute-start | bytes 1277960 | tf_op jit(solution)/shard_map/ppermute | solution.py:406
  44.8 12.1 %collective-permute-start.12 = (bf16[208,1024]{1,0:T(8,128)(2,1)S(1)}, bf16[208,1024]{1,0:T(8,128)(2,1)S(1)}, u32[]{:S(2)}, u32[]{:S(2)}) collective-permute-start(bf16[208,1024]{1,0:T(8,128)(2,1)S(1)} %collective-permute-done.8.refs_1_.refs_11_), channel_id=1, source_target_pairs={{0,1},{1,0},{2,3},{3,2},{4,5},{5,4},{6,7},{7,6},{8,9},{9,8},{10,11... | collective-permute-start | bytes 1277960 | tf_op jit(solution)/shard_map/ppermute | solution.py:406
  45.3 11.6 %collective-permute-start.13 = (bf16[208,1024]{1,0:T(8,128)(2,1)S(1)}, bf16[208,1024]{1,0:T(8,128)(2,1)S(1)}, u32[]{:S(2)}, u32[]{:S(2)}) collective-permute-start(bf16[208,1024]{1,0:T(8,128)(2,1)S(1)} %collective-permute-done.9.refs_2_.refs_12_), channel_id=1, source_target_pairs={{0,1},{1,0},{2,3},{3,2},{4,5},{5,4},{6,7},{7,6},{8,9},{9,8},{10,11... | collective-permute-start | bytes 1277960 | tf_op jit(solution)/shard_map/ppermute | solution.py:406
  45.3 11.7 %collective-permute-start.14 = (bf16[208,1024]{1,0:T(8,128)(2,1)S(1)}, bf16[208,1024]{1,0:T(8,128)(2,1)S(1)}, u32[]{:S(2)}, u32[]{:S(2)}) collective-permute-start(bf16[208,1024]{1,0:T(8,128)(2,1)S(1)} %collective-permute-done.10.refs_3_.refs_13_), channel_id=1, source_target_pairs={{0,1},{1,0},{2,3},{3,2},{4,5},{5,4},{6,7},{7,6},{8,9},{9,8},{10,11... | collective-permute-start | bytes 1277960 | tf_op jit(solution)/shard_map/ppermute | solution.py:406
  (3 other events, 3.4 us)

commit v6 on v4

v6 whole, which is shorter than its diff:
```python
import functools
import math

import jax
import jax.numpy as jnp
from jax import lax
from jax.experimental import pallas as pl
from jax.experimental.pallas import tpu as pltpu
from jax.sharding import PartitionSpec as P

epsilon = 1e-06
update_scale = 0.1 / math.sqrt(0.001)
HIGHEST = lax.Precision.HIGHEST
NN = (((1,), (0,)), ((), ()))
TN = (((0,), (0,)), ((), ()))
NT = (((1,), (1,)), ((), ()))
VMEM_LIMIT = 60 * 1024 * 1024
CHUNK_LIMIT = 24 * 1024 * 1024
ANY = pl.BlockSpec(memory_space=pl.ANY)
SMEM = pl.BlockSpec(memory_space=pltpu.SMEM)
VMEM = pl.BlockSpec(memory_space=pltpu.VMEM)


def mm(a, b, dims=NN, precision=None):
    return lax.dot_general(a, b, dims, precision=precision, preferred_element_type=jnp.float32)


def two_terms(exact):
    coarse = exact.astype(jnp.bfloat16)
    fine = (exact - coarse.astype(jnp.float32)).astype(jnp.bfloat16)
    return coarse, fine


def cut_kernel(first, second, out, sems):
    group = lax.axis_index("dp")
    quarter = first.shape[1]
    copies = [
        pltpu.make_async_copy(source.at[group], out.at[pl.ds(i * quarter, quarter)], sems.at[i])
        for i, source in enumerate((first, second))
    ]
    for copy in copies:
        copy.start()
    for copy in copies:
        copy.wait()


def cut_piece(first, second):
    return pl.pallas_call(
        cut_kernel,
        in_specs=[ANY, ANY],
        out_specs=VMEM,
        out_shape=jax.ShapeDtypeStruct((2 * first.shape[1], first.shape[2]), first.dtype),
        scratch_shapes=[pltpu.SemaphoreType.DMA((2,))],
        compiler_params=pltpu.CompilerParams(vmem_limit_bytes=VMEM_LIMIT),
        name="cut_piece",
    )(first, second)


def fold(tall, times):
    rows = tall.shape[0] // times
    return jnp.concatenate([tall[i * rows : (i + 1) * rows] for i in range(times)], axis=1)


def unfold(wide, times):
    cols = wide.shape[1] // times
    return jnp.concatenate([wide[:, i * cols : (i + 1) * cols] for i in range(times)], axis=0)


def on_vmem(kernel, shape, dtype, name, *operands):
    return pl.pallas_call(
        kernel,
        in_specs=[VMEM] * len(operands),
        out_specs=VMEM,
        out_shape=jax.ShapeDtypeStruct(shape, dtype),
        compiler_params=pltpu.CompilerParams(vmem_limit_bytes=CHUNK_LIMIT),
        name=name,
    )(*operands)


def pack_kernel(piece, val, out):
    rows = piece.shape[0]
    out[pl.ds(0, rows), :] = piece[...]
    wide = fold(val[...], out.shape[1] // val.shape[1])
    coarse = wide.astype(jnp.bfloat16).astype(jnp.float32)
    terms = jnp.concatenate([coarse, wide - coarse], axis=0)
    out[pl.ds(rows, terms.shape[0]), :] = terms.astype(jnp.bfloat16)


def pack(piece, val):
    rows, span = piece.shape
    return on_vmem(pack_kernel, (rows + 2 * val.size // span, span), piece.dtype, "pack", piece, val)


def join_kernel(first, second, out):
    rows = first.shape[0]
    out[pl.ds(0, rows), :] = first[...]
    out[pl.ds(rows, rows), :] = second[...]


def join(first, second):
    rows, span = first.shape
    return on_vmem(join_kernel, (2 * rows, span), first.dtype, "join", first, second)


def order_kernel(first, second, third, fourth, out):
    group = lax.axis_index("dp")
    for j, part in enumerate((first, second, third, fourth)):
        out[lax.bitwise_xor(group, j)] = part[...]


def order(four):
    return on_vmem(order_kernel, (4,) + four[0].shape, four[0].dtype, "order", *four)


def plane_kernel(rows, own, crossed, out):
    total = None
    for part in (own, crossed):
        terms = [part[q, rows:, :].astype(jnp.float32) for q in range(4)]
        terms = [term[: term.shape[0] // 2] + term[term.shape[0] // 2 :] for term in terms]
        found = (terms[0] + terms[1]) + (terms[2] + terms[3])
        total = found if total is None else total + found
    out[...] = unfold(total, total.shape[1] // out.shape[1])


def plane_sum(rows, shape, own, crossed):
    return on_vmem(functools.partial(plane_kernel, rows), shape, jnp.float32, "plane_sum", own, crossed)


def zeros(*shape):
    return jnp.zeros(shape, jnp.float32)


def split_copies(source, target, axis, count, sems, first):
    span = source.shape[axis] // count
    found = []
    for i in range(count):
        at = (slice(None),) * axis + (pl.ds(i * span, span),)
        found.append(pltpu.make_async_copy(source.at[at], target.at[at], sems.at[first + i]))
    return found


PARTS = 4
HALVES = 2


def validation_kernel(xv, gv, down_t, up, columns, rows_t, proj_out, xvs, gvs, downs, ups, tables, sems):
    tokens, width = xv.shape
    k2 = columns.shape[1]
    pairs = [(gv, gvs), (up, ups), (xv, xvs), (down_t, downs)]
    whole = [pltpu.make_async_copy(p[0], p[1], sems.at[i]) for i, p in enumerate(pairs)]
    parts = split_copies(columns, tables, 0, PARTS, sems, len(pairs))
    for copy in whole + parts:
        copy.start()
    whole[0].wait()
    whole[1].wait()
    back = mm(gvs[...], ups[...], NT)
    whole[2].wait()
    whole[3].wait()
    fwd = mm(xvs[...], downs[...], NT)
    mixed = zeros(2 * tokens, 2 * k2)
    span = width // PARTS
    for i in range(PARTS):
        parts[i].wait()
        cols = pl.ds(i * span, span)
        table = jnp.concatenate(two_terms(tables[cols, :]), axis=1)
        mixed = mixed + mm(jnp.concatenate([xvs[:, cols], gvs[:, cols]], axis=0), table)
    mixed = mixed[:, :k2] + mixed[:, k2:]
    inner_top = mm(back.astype(jnp.bfloat16).astype(jnp.float32), mixed[:tokens], TN, HIGHEST)
    inner_bottom = mm(fwd.astype(jnp.bfloat16).astype(jnp.float32), mixed[tokens:], TN, HIGHEST)
    inner = jnp.concatenate([inner_top, inner_bottom], axis=0)
    proj_out[...] = mm(rows_t[...], inner, NN, HIGHEST)


def prepare_kernel(lengths, x, g, down_t, up, top_out, bottom_out, xs, gs, downs, ups, sems):
    tokens, width = x.shape
    examples, rank = lengths.shape[0], up.shape[0]
    copies = []
    for i, (source, target) in enumerate(((up, ups), (g, gs), (down_t, downs), (x, xs))):
        copies.append(split_copies(source, target, 1, HALVES, sems, i * HALVES))
    for i in range(HALVES):
        for pair in copies[:2]:
            pair[i].start()
    for i in range(HALVES):
        for pair in copies[2:]:
            pair[i].start()
    span = width // HALVES
    position = lax.broadcasted_iota(jnp.int32, (rank, tokens), 1)
    for first, (left, right, out) in enumerate(((gs, ups, top_out), (xs, downs, bottom_out))):
        total = zeros(tokens, rank)
        for i in range(HALVES):
            copies[2 * first][i].wait()
            copies[2 * first + 1][i].wait()
            cols = pl.ds(i * span, span)
            total = total + mm(left[:, cols], right[:, cols], NT)
        turned = total.T
        begin = jnp.int32(0)
        for e in range(examples):
            finish = begin + lengths[e]
            member = (position >= begin) & (position < finish)
            out[pl.ds(e * rank, rank), :] = jnp.where(member, turned, 0.0).astype(jnp.bfloat16)
            begin = finish


def validation(xv, gv, down_t, up, columns, rows_t):
    return pl.pallas_call(
        validation_kernel,
        in_specs=[ANY] * 5 + [VMEM],
        out_specs=VMEM,
        out_shape=jax.ShapeDtypeStruct((rows_t.shape[0], columns.shape[1]), jnp.float32),
        scratch_shapes=[
            *(pltpu.VMEM(a.shape, a.dtype) for a in (xv, gv, down_t, up, columns)),
            pltpu.SemaphoreType.DMA((4 + PARTS,)),
        ],
        compiler_params=pltpu.CompilerParams(vmem_limit_bytes=VMEM_LIMIT),
        cost_estimate=pl.CostEstimate(flops=10**6, bytes_accessed=10**6, transcendentals=0),
        name="validation",
    )(xv, gv, down_t, up, columns, rows_t)


def prepare(lengths, x, g, down_t, up):
    shape = jax.ShapeDtypeStruct((lengths.shape[0] * up.shape[0], x.shape[0]), jnp.bfloat16)
    return pl.pallas_call(
        prepare_kernel,
        in_specs=[SMEM] + [ANY] * 4,
        out_specs=[VMEM] * 2,
        out_shape=[shape, shape],
        scratch_shapes=[
            *(pltpu.VMEM(a.shape, a.dtype) for a in (x, g, down_t, up)),
            pltpu.SemaphoreType.DMA((4 * HALVES,)),
        ],
        compiler_params=pltpu.CompilerParams(vmem_limit_bytes=VMEM_LIMIT),
        cost_estimate=pl.CostEstimate(flops=10**6, bytes_accessed=10**6, transcendentals=0),
        name="prepare",
    )(lengths, x, g, down_t, up)


def accumulate(blocks, moments, slots, x, g, columns, top, bottom, update, inner):
    _, rows2, span = update.shape
    rank = (rows2 - top.shape[0]) // 2
    examples = top.shape[0] // rank
    cut = min(span, 256)
    starts = [pl.multiple_of(slots[slot_of()] * span, span) for slot_of, _ in blocks]
    tiles = [(b, half, c) for b in range(len(blocks)) for half in (0, 1) for c in range(0, span, cut)]
    sources, masks = (x, g), (top, bottom)

    def gradient(tile):
        b, half, c = tile
        cols = pl.ds(pl.multiple_of(starts[b] + c, cut), cut)
        return mm(masks[half][...], sources[half][:, cols])

    def moment(b, k, half, cols):
        ref, low, quarter = blocks[b][1](moments, k)
        parts = ref.shape[0] // 2
        found = ref[half * parts : (half + 1) * parts, low : low + quarter, cols]
        return found.astype(jnp.float32).reshape(rank, cut)

    def elementwise(tile, grad):
        b, half, c = tile
        cols = pl.ds(c, cut)
        first = 9.0 * moment(b, 0, half, cols)
        second = 999.0 * moment(b, 1, half, cols)
        shared = first * lax.rsqrt(second)
        coarse, fine = two_terms(shared)
        update[half, pl.ds(examples * rank, rank), cols] = coarse
        update[half, pl.ds((examples + 1) * rank, rank), cols] = fine
        for e in range(examples):
            piece = grad[e * rank : (e + 1) * rank]
            change = (first + piece) * lax.rsqrt(second + piece * piece) - shared
            update[half, pl.ds(e * rank, rank), cols] = change.astype(jnp.bfloat16)

    grad = gradient(tiles[0])
    for i, tile in enumerate(tiles):
        following = gradient(tiles[i + 1]) if i + 1 < len(tiles) else None
        elementwise(tile, grad)
        grad = following
        b, half, c = tile
        if c + cut == span:
            if half == 0:
                table = jnp.concatenate(two_terms(columns[pl.ds(starts[b], span), :]), axis=1)
            product = mm(update[half], table)
            inner[half] = product if b == 0 else inner[half] + product


def folded(inner, half, examples, rank, e):
    k2 = inner.shape[2] // 2
    part = pl.ds(e * rank, rank)
    total = inner[half, part, :k2] + inner[half, part, k2:]
    if e == examples:
        part = pl.ds((examples + 1) * rank, rank)
        total = total + inner[half, part, :k2] + inner[half, part, k2:]
    return total


def chunk_kernel(blocks, n_moments, slots, *refs):
    moments, refs = refs[:n_moments], refs[n_moments:]
    x, g, columns, top, bottom, out, update, inner = refs
    accumulate(blocks, moments, slots, x, g, columns, top, bottom, update, inner)
    rank = (update.shape[1] - top.shape[0]) // 2
    examples = top.shape[0] // rank
    for half in (0, 1):
        for e in range(examples + 1):
            out[half, pl.ds(e * rank, rank), :] = folded(inner, half, examples, rank, e)


def last_kernel(blocks, n_moments, n_val, n_partial, slots, *refs):
    moments, refs = refs[:n_moments], refs[n_moments:]
    x, g, columns, top, bottom, rows_t = refs[:6]
    val_parts, refs = refs[6 : 6 + n_val], refs[6 + n_val :]
    partials, refs = refs[:n_partial], refs[n_partial:]
    dirs_out, val_out, scores_out, joined, update, inner = refs
    accumulate(blocks, moments, slots, x, g, columns, top, bottom, update, inner)
    rank = (update.shape[1] - top.shape[0]) // 2
    examples = top.shape[0] // rank
    k1, k2 = rows_t.shape[0], columns.shape[1]
    size = k1 * k2
    val = val_parts[0][...]
    for part in val_parts[1:]:
        val = val + part[...]
    val_dir = val * lax.rsqrt(jnp.sum(val * val) / size + epsilon)
    val_out[...] = val_dir
    rows = rows_t[...] * update_scale
    for e in range(examples + 1):
        for half in (0, 1):
            total = folded(inner, half, examples, rank, e)
            for partial in partials:
                total = total + partial[half, pl.ds(e * rank, rank), :]
            joined[pl.ds(half * rank, rank), pl.ds(e * k2, k2)] = total
    projected = mm(rows, joined[...], NN, HIGHEST)
    base = projected[:, examples * k2 :]
    for e in range(examples):
        proj = projected[:, e * k2 : (e + 1) * k2] + base
        direction = proj * lax.rsqrt(jnp.sum(proj * proj) / size + epsilon)
        dirs_out[e] = direction
        scores_out[e] = jnp.sum(direction * val_dir) / math.sqrt(size)


def chunk(slots, blocks, moments, x, g, columns, top, bottom, rank, last=None):
    tokens, width = x.shape
    k2 = columns.shape[1]
    span = width // slots.shape[0]
    examples = top.shape[0] // rank
    scratch = [
        pltpu.VMEM((2, (examples + 2) * rank, span), jnp.bfloat16),
        pltpu.VMEM((2, (examples + 2) * rank, 2 * k2), jnp.float32),
    ]
    common = [SMEM] + [VMEM] * (len(moments) + 5)
    operands = [slots, *moments, x, g, columns, top, bottom]
    options = dict(
        compiler_params=pltpu.CompilerParams(vmem_limit_bytes=CHUNK_LIMIT),
        cost_estimate=pl.CostEstimate(flops=10**6, bytes_accessed=10**6, transcendentals=0),
    )
    if last is None:
        return pl.pallas_call(
            functools.partial(chunk_kernel, blocks, len(moments)),
            in_specs=common,
            out_specs=VMEM,
            out_shape=jax.ShapeDtypeStruct((2, (examples + 1) * rank, k2), jnp.float32),
            scratch_shapes=scratch,
            name="chunk",
            **options,
        )(*operands)
    rows_t, val_parts, partials = last
    k1 = rows_t.shape[0]
    return pl.pallas_call(
        functools.partial(last_kernel, blocks, len(moments), len(val_parts), len(partials)),
        in_specs=common + [VMEM] * (1 + len(val_parts) + len(partials)),
        out_specs=[VMEM, VMEM, SMEM],
        out_shape=[
            jax.ShapeDtypeStruct((examples, k1, k2), jnp.float32),
            jax.ShapeDtypeStruct((k1, k2), jnp.float32),
            jax.ShapeDtypeStruct((examples,), jnp.float32),
        ],
        scratch_shapes=[pltpu.VMEM((2 * rank, (examples + 1) * k2), jnp.float32), *scratch],
        name="last_chunk",
        **options,
    )(*operands, rows_t, *val_parts, *partials)


def slot_at(other, hop):
    return lambda: lax.bitwise_xor(lax.axis_index("shard"), 2 * hop + other)


def ordered_block(quarter, other, hop, which, place):
    return slot_at(other, hop), lambda moments, k: (moments[which], (2 * place + k) * quarter, quarter)


def paired_block(quarter, other, which):
    return slot_at(other, 0), lambda moments, k: (moments[2 * which + k], 0, quarter)


def gathered_block(quarter, b):
    return lambda: b, lambda moments, k: (moments[k].at[b], 0, quarter)


def exchange(value, axis, bits):
    size = lax.axis_size(axis)
    return lax.ppermute(value, axis, [(i, i ^ bits) for i in range(size)])


def body(
    training_inputs,
    training_cotangents,
    validation_inputs,
    validation_cotangents,
    adapter_down,
    adapter_up,
    adam_first_moment,
    adam_second_moment,
    slot_block_index,
    example_lengths,
    projection_rows,
    projection_columns,
):
    groups = lax.axis_size("dp")
    shards = lax.axis_size("shard")
    rank = adapter_up.shape[0]
    quarter = 2 * rank // groups
    stepwise = groups == 4 and shards == 8
    rows_t = projection_rows.T
    own = [m.reshape(groups, quarter, -1) for m in (adam_first_moment, adam_second_moment)]
    train = (training_inputs, training_cotangents)
    if stepwise:
        piece = cut_piece(*own)
        sibling = [exchange(m, "shard", 1) for m in own]
        far = [exchange(piece, "shard", 2 * hop) for hop in (1, 2, 3)]
        validation_inputs, _ = lax.optimization_barrier((validation_inputs, piece))
    down_t = adapter_down.T
    val_part = validation(
        validation_inputs, validation_cotangents, down_t, adapter_up, projection_columns, rows_t
    )
    lengths, val_part = lax.optimization_barrier((example_lengths[0, 0], val_part))
    top, bottom = prepare(lengths, *train, down_t, adapter_up)
    if stepwise:
        val_part, *sibling, far[0], far[1] = lax.optimization_barrier((val_part, *sibling, far[0], far[1]))
        packed = pack(far[0], val_part)
        near = [packed] + [exchange(packed, "dp", bits) for bits in (1, 2, 3)]
        *arrived, top, bottom = lax.optimization_barrier((*far[1:], *near, top, bottom))
        rest = join(*arrived[:2])
        four = [rest] + [exchange(rest, "dp", bits) for bits in (1, 2, 3)]
        one = order(arrived[2:])
        one, top, bottom = lax.optimization_barrier((one, top, bottom))
        one_crossed = exchange(one, "shard", 1)
        operands = (*train, projection_columns, top, bottom, rank)
        slots = slot_block_index
        partials = [chunk(slots, [paired_block(quarter, i, i) for i in (0, 1)], own + sibling, *operands)]
        partials[0], one_crossed = lax.optimization_barrier((partials[0], one_crossed))
        total = plane_sum(2 * quarter, val_part.shape, one, one_crossed)
        total, one_crossed = lax.optimization_barrier((total, one_crossed))
        other = exchange(total, "shard", 2)
        partials.append(
            chunk(slots, [ordered_block(quarter, i, 1, i, 0) for i in (0, 1)], [one, one_crossed], *operands)
        )
        partials[1], other, *four = lax.optimization_barrier((partials[1], other, *four))
        total = total + other
        both = order(four)
        total, both = lax.optimization_barrier((total, both))
        val_parts = [total, exchange(total, "shard", 4)]
        both_crossed = exchange(both, "shard", 1)
        partials.append(chunk(slots, [ordered_block(quarter, 0, 2 + i, 0, i) for i in (0, 1)], [both], *operands))
        dirs, val_dir, scores = chunk(
            slots,
            [ordered_block(quarter, 1, 2 + i, 0, i) for i in (0, 1)],
            [both_crossed],
            *operands,
            last=(rows_t, val_parts, partials),
        )
    else:
        operands = (*train, projection_columns, top, bottom, rank)
        gathered = [lax.all_gather(m, "shard", axis=0, tiled=False) for m in own]
        val_sum = lax.psum(val_part, ("dp", "shard"))
        dirs, val_dir, scores = chunk(
            slot_block_index,
            [gathered_block(quarter, b) for b in range(shards)],
            gathered,
            *operands,
            last=(rows_t, [val_sum], []),
        )
    return (
        dirs.reshape(1, 1, dirs.shape[0], -1),
        val_dir.reshape(-1),
        scores[None, None],
    )


def solution(mesh):
    return jax.shard_map(
        body,
        mesh=mesh,
        in_specs=(
            P(("dp", "shard"), None),
            P(("dp", "shard"), None),
            P(("dp", "shard"), None),
            P(("dp", "shard"), None),
            P(),
            P(),
            P("shard", None, None),
            P("shard", None, None),
            P(),
            P("dp", "shard", None),
            P(),
            P(),
        ),
        out_specs=(P("dp", "shard", None, None), P(), P("dp", "shard", None)),
        check_vma=False,
    )
```

time: 67.7 us -> 58.9 us (0.87)
  Pallas kernels: 38.7 us -> 31.9 us
  waiting for transfers between devices: 3.06 us -> 0.5 us
  local copies, waits for them, and re-layouts: 6.37 us -> 7.14 us
    pallas_call x3 -> x9, Pallas kernels: 26.3 us -> 18.2 us  [the longest x3 11.6 us: chunk(): pl.pallas_call(functools.partial(chunk_kernel, blocks, len(moments)), in_...]
    ppermute x18 -> x15, waiting for transfers between devices: 3.06 us -> 0.5 us  [exchange(): return lax.ppermute(value, axis, [(i, i ^ bits) for i in range(size)])]
    pallas_call x1, Pallas kernels: 4.92 us -> 6 us  [prepare(): pl.pallas_call(prepare_kernel, in_specs=[SMEM] + [ANY] * 4, out_specs=[VM...]
    unnamed x24 -> x28, local copies, waits for them, and re-layouts: 5.62 us -> 6.38 us
    ppermute x18 -> x15, starting transfers between devices: 18.2 us -> 18 us  [exchange(): return lax.ppermute(value, axis, [(i, i ^ bits) for i in range(size)])]
  transfers between devices with their start and end apart: 18 -> 15, of which waited for: 1 -> 1; matrix products, arithmetic and copies ran while one was open for 0% -> 0% of each run, Pallas kernels for 40% -> 43%
where the time goes in v6:
time: 58.9 us; the launch traced here: 58.5 us
  Pallas kernels  31.9 us (54%)
  starting transfers between devices  18 us (31%)
  local copies, waits for them, and re-layouts  7.14 us (12%)
  between operations  0.94 us (2%)
    ppermute x15, starting transfers between devices, exchange(): return lax.ppermute(value, axis, [(i, i ^ bits) for i in range(size)])  18 us
    pallas_call x3, Pallas kernels, chunk(): pl.pallas_call(functools.partial(chunk_kernel, blocks, len(moments)), in_...  11.6 us
    unnamed x28, local copies, waits for them, and re-layouts  6.38 us
    pallas_call x1, Pallas kernels, chunk(): pl.pallas_call(functools.partial(last_kernel, blocks, len(moments), len(v...  6.38 us
    pallas_call x1, Pallas kernels, validation(): pl.pallas_call(validation_kernel, in_specs=[ANY] * 5 + [VMEM], out_specs=...  6.12 us
    pallas_call x1, Pallas kernels, prepare(): pl.pallas_call(prepare_kernel, in_specs=[SMEM] + [ANY] * 4, out_specs=[VM...  6 us
    pallas_call x1, Pallas kernels, cut_piece(): pl.pallas_call(cut_kernel, in_specs=[ANY, ANY], out_specs=VMEM, out_shape...  1.54 us
  transfers between devices with their start and end apart: 15, of which 1 were waited for; matrix products, arithmetic and copies ran while one was open for 0% of the time, Pallas kernels for 43%

profile of v6, /device:TPU:0, one launch (start us, length us, event | category | flops | bytes accessed | tf_op | source)
XLA Modules:
  0.0 58.5 jit_solution(12646710389625677566)
XLA Ops:
  0.6 0.5 collective-permute-start
  1.2 1.5 %cut_piece.1 = bf16[64,1024]{1,0:T(8,128)(2,1)} custom-call(bf16[4,32,1024]{2,1,0:T(8,128)(2,1)} %bitcast.8, bf16[4,32,1024]{2,1,0:T(8,128)(2,1)} %bitcast.11), custom_call_target="tpu_custom_call" | custom-call | tf_op jit(solution)/shard_map/cut_piece/pallas_call | solution.py:48
  2.8 3.1 %collective-permute-start.2 = (bf16[64,1024]{1,0:T(8,128)(2,1)}, bf16[64,1024]{1,0:T(8,128)(2,1)S(1)}, u32[]{:S(2)}, u32[]{:S(2)}) collective-permute-start(bf16[64,1024]{1,0:T(8,128)(2,1)} %cut_piece.1), channel_id=1, source_target_pairs={{0,2},{1,3},{2,0},{3,1},{4,6},{5,7},{6,4},{7,5},{8,10},{9,11},{10,... | collective-permute-start | bytes 393224 | tf_op jit(solution)/shard_map/ppermute | solution.py:397
  5.8 2.6 %collective-permute-start.3 = (bf16[64,1024]{1,0:T(8,128)(2,1)}, bf16[64,1024]{1,0:T(8,128)(2,1)S(1)}, u32[]{:S(2)}, u32[]{:S(2)}) collective-permute-start(bf16[64,1024]{1,0:T(8,128)(2,1)} %cut_piece.1), channel_id=1, source_target_pairs={{0,4},{1,5},{2,6},{3,7},{4,0},{5,1},{6,2},{7,3},{8,12},{9,13},{10,... | collective-permute-start | bytes 393224 | tf_op jit(solution)/shard_map/ppermute | solution.py:397
  8.4 6.1 %validation.1.val = f32[64,128]{1,0:T(8,128)} custom-call(bf16[32,8192]{1,0:T(8,128)(2,1)} %xv, bf16[32,8192]{1,0:T(8,128)(2,1)} %gv.1, bf16[64,8192]{1,0:T(8,128)(2,1)} %bitcast.15, bf16[64,8192]{1,0:T(8,128)(2,1)} %up.3, f32[8192,128]{1,0:T(8,128)} %refs_3_.5, f32[64,128]{1,0:T(8,128)} %bitcast.13), custom_call_target="tpu_custom_call" | custom-call | flops 1000000 | bytes 1000000 | tf_op jit(solution)/shard_map/validation/pallas_call | solution.py:205
  15.0 0.8 %copy-done.12 = f32[64,128]{1,0:T(8,128)S(1)} copy-done((f32[64,128]{1,0:T(8,128)S(1)}, f32[64,128]{1,0:T(8,128)}, u32[]{:S(2)}) %copy-start.12) | copy-done | bytes 32792
  15.9 1.6 %collective-permute-start.5 = (bf16[80,1024]{1,0:T(8,128)(2,1)S(1)}, bf16[80,1024]{1,0:T(8,128)(2,1)S(1)}, u32[]{:S(2)}, u32[]{:S(2)}) collective-permute-start(bf16[80,1024]{1,0:T(8,128)(2,1)S(1)} %pack.1.first), channel_id=1, source_target_pairs={{0,8},{8,0},{16,24},{24,16},{1,9},{9,1},{17,25},{25,17},{2,10},{10... | collective-permute-start | bytes 491528 | tf_op jit(solution)/shard_map/ppermute | solution.py:397
  17.4 1.5 %collective-permute-start.6 = (bf16[80,1024]{1,0:T(8,128)(2,1)S(1)}, bf16[80,1024]{1,0:T(8,128)(2,1)S(1)}, u32[]{:S(2)}, u32[]{:S(2)}) collective-permute-start(bf16[80,1024]{1,0:T(8,128)(2,1)S(1)} %pack.1.first), channel_id=1, source_target_pairs={{0,16},{8,24},{16,0},{24,8},{1,17},{9,25},{17,1},{25,9},{2,18},{10... | collective-permute-start | bytes 491528 | tf_op jit(solution)/shard_map/ppermute | solution.py:397
  18.9 0.5 collective-permute-start.7
  19.4 2.5 %collective-permute-start.4 = (bf16[64,1024]{1,0:T(8,128)(2,1)}, bf16[64,1024]{1,0:T(8,128)(2,1)S(1)}, u32[]{:S(2)}, u32[]{:S(2)}) collective-permute-start(bf16[64,1024]{1,0:T(8,128)(2,1)} %cut_piece.1), channel_id=1, source_target_pairs={{0,6},{1,7},{2,4},{3,5},{4,2},{5,3},{6,0},{7,1},{8,14},{9,15},{10,... | collective-permute-start | bytes 393224 | tf_op jit(solution)/shard_map/ppermute | solution.py:397
  21.9 6.0 %prepare.1 = (bf16[512,128]{1,0:T(8,128)(2,1)}, bf16[512,128]{1,0:T(8,128)(2,1)}) custom-call(s32[8]{0:T(128)} %bitcast.17, bf16[128,8192]{1,0:T(8,128)(2,1)} %refs_1_.3, bf16[128,8192]{1,0:T(8,128)(2,1)} %refs_2_.5, bf16[64,8192]{1,0:T(8,128)(2,1)} %bitcast.16, bf16[64,8192]{1,0:T(8,128)(2,1)} %up.3), custom_call_target="tpu_custom_call" | custom-call | flops 1000000 | bytes 1000000 | tf_op jit(solution)/shard_map/prepare/pallas_call | solution.py:222
  28.1 1.6 %collective-permute-start.10 = (bf16[128,1024]{1,0:T(8,128)(2,1)S(1)}, bf16[128,1024]{1,0:T(8,128)(2,1)S(1)}, u32[]{:S(2)}, u32[]{:S(2)}) collective-permute-start(bf16[128,1024]{1,0:T(8,128)(2,1)S(1)} %join.1.first), channel_id=1, source_target_pairs={{0,8},{8,0},{16,24},{24,16},{1,9},{9,1},{17,25},{25,17},{2,10},{10... | collective-permute-start | bytes 786440 | tf_op jit(solution)/shard_map/ppermute | solution.py:397
  29.6 1.5 %collective-permute-start.11 = (bf16[128,1024]{1,0:T(8,128)(2,1)S(1)}, bf16[128,1024]{1,0:T(8,128)(2,1)S(1)}, u32[]{:S(2)}, u32[]{:S(2)}) collective-permute-start(bf16[128,1024]{1,0:T(8,128)(2,1)S(1)} %join.1.first), channel_id=1, source_target_pairs={{0,16},{8,24},{16,0},{24,8},{1,17},{9,25},{17,1},{25,9},{2,18},{10... | collective-permute-start | bytes 786440 | tf_op jit(solution)/shard_map/ppermute | solution.py:397
  31.2 0.5 collective-permute-start.12
  31.7 2.2 %copy-done = f32[8192,128]{1,0:T(8,128)S(1)} copy-done((f32[8192,128]{1,0:T(8,128)S(1)}, f32[8192,128]{1,0:T(8,128)}, u32[]{:S(2)}) %copy-start) | copy-done | bytes 4194328
  33.8 1.6 %copy-done.3 = bf16[128,8192]{1,0:T(8,128)(2,1)S(1)} copy-done((bf16[128,8192]{1,0:T(8,128)(2,1)S(1)}, bf16[128,8192]{1,0:T(8,128)(2,1)}, u32[]{:S(2)}) %copy-start.3) | copy-done | bytes 2097176
  35.4 0.9 %copy-done.5 = bf16[512,128]{1,0:T(8,128)(2,1)S(1)} copy-done((bf16[512,128]{1,0:T(8,128)(2,1)S(1)}, bf16[512,128]{1,0:T(8,128)(2,1)}, u32[]{:S(2)}) %copy-start.5) | copy-done | bytes 131096
  36.3 0.9 %copy-done.7 = bf16[512,128]{1,0:T(8,128)(2,1)S(1)} copy-done((bf16[512,128]{1,0:T(8,128)(2,1)S(1)}, bf16[512,128]{1,0:T(8,128)(2,1)}, u32[]{:S(2)}) %copy-start.7) | copy-done | bytes 131096
  37.3 3.8 %chunk.3.refs_9_ = f32[2,576,128]{2,1,0:T(8,128)S(1)} custom-call(s32[8]{0:T(128)S(1)} %copy-done.13, bf16[4,32,1024]{2,1,0:T(8,128)(2,1)S(1)} %bitcast.9, bf16[4,32,1024]{2,1,0:T(8,128)(2,1)S(1)} %bitcast.12, bf16[4,32,1024]{2,1,0:T(8,128)(2,1)S(1)} %collective-permute-done.refs_2_, bf16[4,32,1024]{2,1,0:T(8,128)(2,1)S(1)} %collective-permute-done.1.refs_3_, ...), custom_call_target="tpu_custom_call" | custom-call | flops 1000000 | bytes 1000000 | tf_op jit(solution)/shard_map/chunk/pallas_call | solution.py:353
  41.2 3.8 %chunk.4.refs_10_ = f32[2,576,128]{2,1,0:T(8,128)S(1)} custom-call(s32[8]{0:T(128)S(1)} %copy-done.13, bf16[4,80,1024]{2,1,0:T(8,128)(2,1)S(1)} %order.2.own.refs_0_, bf16[4,80,1024]{2,1,0:T(8,128)(2,1)S(1)} %collective-permute-done.8.crossed.refs_1_, bf16[128,8192]{1,0:T(8,128)(2,1)S(1)} %copy-done.2, bf16[128,8192]{1,0:T(8,128)(2,1)S(1)} %copy-done.4, ...), custom_call_target="tpu_custom_call" | custom-call | flops 1000000 | bytes 1000000 | tf_op jit(solution)/shard_map/chunk/pallas_call | solution.py:353
  45.3 2.0 %collective-permute-start.14 = (f32[64,128]{1,0:T(8,128)S(1)}, f32[64,128]{1,0:T(8,128)S(1)}, u32[]{:S(2)}, u32[]{:S(2)}) collective-permute-start(f32[64,128]{1,0:T(8,128)S(1)} %add.3.refs_7_), channel_id=1, source_target_pairs={{0,4},{1,5},{2,6},{3,7},{4,0},{5,1},{6,2},{7,3},{8,12},{9,13},{10,... | collective-permute-start | bytes 98312 | tf_op jit(solution)/shard_map/ppermute | solution.py:397
  47.2 4.0 %chunk.5.refs_11_ = f32[2,576,128]{2,1,0:T(8,128)S(1)} custom-call(s32[8]{0:T(128)S(1)} %copy-done.13, bf16[4,128,1024]{2,1,0:T(8,128)(2,1)S(1)} %order.3.refs_0_, bf16[128,8192]{1,0:T(8,128)(2,1)S(1)} %copy-done.2, bf16[128,8192]{1,0:T(8,128)(2,1)S(1)} %copy-done.4, f32[8192,128]{1,0:T(8,128)S(1)} %copy-done.1, bf16[512,128]{1,0:T(8,128)(2,1)S(1)} %copy-done.6, ...), custom_call_target="tpu_custom_call" | custom-call | flops 1000000 | bytes 1000000 | tf_op jit(solution)/shard_map/chunk/pallas_call | solution.py:353
  51.3 6.4 %last_chunk.1 = (f32[8,64,128]{2,1,0:T(8,128)S(1)}, f32[64,128]{1,0:T(8,128)}, f32[8]{0:T(128)}) custom-call(s32[8]{0:T(128)S(1)} %copy-done.13, bf16[4,128,1024]{2,1,0:T(8,128)(2,1)S(1)} %collective-permute-done.13.refs_0_, bf16[128,8192]{1,0:T(8,128)(2,1)S(1)} %copy-done.2, bf16[128,8192]{1,0:T(8,128)(2,1)S(1)} %copy-done.4, f32[8192,128]{1,0:T(8,128)S(1)} %copy-done.1, ...), custom_call_target="tpu_custom_call" | custom-call | flops 1000000 | bytes 1000000 | tf_op jit(solution)/shard_map/last_chunk/pallas_call | solution.py:364
  57.7 0.8 %reshape.20 = f32[1,1,8,8192]{3,2,1,0:T(8,128)} reshape(f32[8,64,128]{2,1,0:T(8,128)S(1)} %get-tuple-element.72) | data formatting | bytes 524288 | tf_op jit(solution)/shard_map/reshape | solution.py:479
  (48 shorter events, 1.1 us)
Async XLA Ops:
  0.6 14.4 %collective-permute-start = (bf16[4,32,1024]{2,1,0:T(8,128)(2,1)}, bf16[4,32,1024]{2,1,0:T(8,128)(2,1)S(1)}, u32[]{:S(2)}, u32[]{:S(2)}) collective-permute-start(bf16[4,32,1024]{2,1,0:T(8,128)(2,1)} %bitcast.7), channel_id=1, source_target_pairs={{0,1},{1,0},{2,3},{3,2},{4,5},{5,4},{6,7},{7,6},{8,9},{9,8},{10,11... | collective-permute-start | bytes 786440 | tf_op jit(solution)/shard_map/ppermute | solution.py:397
  1.1 13.9 %collective-permute-start.1 = (bf16[4,32,1024]{2,1,0:T(8,128)(2,1)}, bf16[4,32,1024]{2,1,0:T(8,128)(2,1)S(1)}, u32[]{:S(2)}, u32[]{:S(2)}) collective-permute-start(bf16[4,32,1024]{2,1,0:T(8,128)(2,1)} %bitcast.10), channel_id=1, source_target_pairs={{0,1},{1,0},{2,3},{3,2},{4,5},{5,4},{6,7},{7,6},{8,9},{9,8},{10,11... | collective-permute-start | bytes 786440 | tf_op jit(solution)/shard_map/ppermute | solution.py:397
  2.8 11.8 %collective-permute-start.2 = (bf16[64,1024]{1,0:T(8,128)(2,1)}, bf16[64,1024]{1,0:T(8,128)(2,1)S(1)}, u32[]{:S(2)}, u32[]{:S(2)}) collective-permute-start(bf16[64,1024]{1,0:T(8,128)(2,1)} %cut_piece.1), channel_id=1, source_target_pairs={{0,2},{1,3},{2,0},{3,1},{4,6},{5,7},{6,4},{7,5},{8,10},{9,11},{10,... | collective-permute-start | bytes 393224 | tf_op jit(solution)/shard_map/ppermute | solution.py:397
  5.8 9.2 %collective-permute-start.3 = (bf16[64,1024]{1,0:T(8,128)(2,1)}, bf16[64,1024]{1,0:T(8,128)(2,1)S(1)}, u32[]{:S(2)}, u32[]{:S(2)}) collective-permute-start(bf16[64,1024]{1,0:T(8,128)(2,1)} %cut_piece.1), channel_id=1, source_target_pairs={{0,4},{1,5},{2,6},{3,7},{4,0},{5,1},{6,2},{7,3},{8,12},{9,13},{10,... | collective-permute-start | bytes 393224 | tf_op jit(solution)/shard_map/ppermute | solution.py:397
  15.8 15.8 %copy-start.9 = (bf16[1,128,1024]{2,1,0:T(8,128)(2,1)S(1)}, bf16[1,128,1024]{2,1,0:T(8,128)(2,1)}, u32[]{:S(2)}) copy-start(bf16[1,128,1024]{2,1,0:T(8,128)(2,1)} %param.18) | copy-start | bytes 786436
  15.8 15.8 %copy-start.10 = (bf16[1,128,1024]{2,1,0:T(8,128)(2,1)S(1)}, bf16[1,128,1024]{2,1,0:T(8,128)(2,1)}, u32[]{:S(2)}) copy-start(bf16[1,128,1024]{2,1,0:T(8,128)(2,1)} %param.19) | copy-start | bytes 786436
  15.8 15.8 %copy-start.13 = (s32[8]{0:T(128)S(1)}, s32[8]{0:T(128)}, u32[]{:S(2)}) copy-start(s32[8]{0:T(128)} %slots.7) | copy-start | bytes 100
  15.9 12.0 %collective-permute-start.5 = (bf16[80,1024]{1,0:T(8,128)(2,1)S(1)}, bf16[80,1024]{1,0:T(8,128)(2,1)S(1)}, u32[]{:S(2)}, u32[]{:S(2)}) collective-permute-start(bf16[80,1024]{1,0:T(8,128)(2,1)S(1)} %pack.1.first), channel_id=1, source_target_pairs={{0,8},{8,0},{16,24},{24,16},{1,9},{9,1},{17,25},{25,17},{2,10},{10... | collective-permute-start | bytes 491528 | tf_op jit(solution)/shard_map/ppermute | solution.py:397
  17.4 10.5 %collective-permute-start.6 = (bf16[80,1024]{1,0:T(8,128)(2,1)S(1)}, bf16[80,1024]{1,0:T(8,128)(2,1)S(1)}, u32[]{:S(2)}, u32[]{:S(2)}) collective-permute-start(bf16[80,1024]{1,0:T(8,128)(2,1)S(1)} %pack.1.first), channel_id=1, source_target_pairs={{0,16},{8,24},{16,0},{24,8},{1,17},{9,25},{17,1},{25,9},{2,18},{10... | collective-permute-start | bytes 491528 | tf_op jit(solution)/shard_map/ppermute | solution.py:397
  18.9 9.0 %collective-permute-start.7 = (bf16[80,1024]{1,0:T(8,128)(2,1)S(1)}, bf16[80,1024]{1,0:T(8,128)(2,1)S(1)}, u32[]{:S(2)}, u32[]{:S(2)}) collective-permute-start(bf16[80,1024]{1,0:T(8,128)(2,1)S(1)} %pack.1.first), channel_id=1, source_target_pairs={{0,24},{8,16},{16,8},{24,0},{1,25},{9,17},{17,9},{25,1},{2,26},{10... | collective-permute-start | bytes 491528 | tf_op jit(solution)/shard_map/ppermute | solution.py:397
  19.4 8.5 %collective-permute-start.4 = (bf16[64,1024]{1,0:T(8,128)(2,1)}, bf16[64,1024]{1,0:T(8,128)(2,1)S(1)}, u32[]{:S(2)}, u32[]{:S(2)}) collective-permute-start(bf16[64,1024]{1,0:T(8,128)(2,1)} %cut_piece.1), channel_id=1, source_target_pairs={{0,6},{1,7},{2,4},{3,5},{4,2},{5,3},{6,0},{7,1},{8,14},{9,15},{10,... | collective-permute-start | bytes 393224 | tf_op jit(solution)/shard_map/ppermute | solution.py:397
  21.9 9.8 %copy-start.2 = (bf16[128,8192]{1,0:T(8,128)(2,1)S(1)}, bf16[128,8192]{1,0:T(8,128)(2,1)}, u32[]{:S(2)}) copy-start(bf16[128,8192]{1,0:T(8,128)(2,1)} %refs_1_.3) | copy-start | bytes 6291460
  28.0 13.0 %collective-permute-start.8 = (bf16[4,80,1024]{2,1,0:T(8,128)(2,1)S(1)}, bf16[4,80,1024]{2,1,0:T(8,128)(2,1)S(1)}, u32[]{:S(2)}, u32[]{:S(2)}) collective-permute-start(bf16[4,80,1024]{2,1,0:T(8,128)(2,1)S(1)} %order.2.own.refs_0_), channel_id=1, source_target_pairs={{0,1},{1,0},{2,3},{3,2},{4,5},{5,4},{6,7},{7,6},{8,9},{9,8},{10,11... | collective-permute-start | bytes 1966088 | tf_op jit(solution)/shard_map/ppermute | solution.py:397
  28.1 16.9 %collective-permute-start.10 = (bf16[128,1024]{1,0:T(8,128)(2,1)S(1)}, bf16[128,1024]{1,0:T(8,128)(2,1)S(1)}, u32[]{:S(2)}, u32[]{:S(2)}) collective-permute-start(bf16[128,1024]{1,0:T(8,128)(2,1)S(1)} %join.1.first), channel_id=1, source_target_pairs={{0,8},{8,0},{16,24},{24,16},{1,9},{9,1},{17,25},{25,17},{2,10},{10... | collective-permute-start | bytes 786440 | tf_op jit(solution)/shard_map/ppermute | solution.py:397
  29.6 15.4 %collective-permute-start.11 = (bf16[128,1024]{1,0:T(8,128)(2,1)S(1)}, bf16[128,1024]{1,0:T(8,128)(2,1)S(1)}, u32[]{:S(2)}, u32[]{:S(2)}) collective-permute-start(bf16[128,1024]{1,0:T(8,128)(2,1)S(1)} %join.1.first), channel_id=1, source_target_pairs={{0,16},{8,24},{16,0},{24,8},{1,17},{9,25},{17,1},{25,9},{2,18},{10... | collective-permute-start | bytes 786440 | tf_op jit(solution)/shard_map/ppermute | solution.py:397
  31.2 13.9 %collective-permute-start.12 = (bf16[128,1024]{1,0:T(8,128)(2,1)S(1)}, bf16[128,1024]{1,0:T(8,128)(2,1)S(1)}, u32[]{:S(2)}, u32[]{:S(2)}) collective-permute-start(bf16[128,1024]{1,0:T(8,128)(2,1)S(1)} %join.1.first), channel_id=1, source_target_pairs={{0,24},{8,16},{16,8},{24,0},{1,25},{9,17},{17,9},{25,1},{2,26},{10... | collective-permute-start | bytes 786440 | tf_op jit(solution)/shard_map/ppermute | solution.py:397
  37.2 3.9 %copy-start.1 = (f32[8192,128]{1,0:T(8,128)S(1)}, f32[8192,128]{1,0:T(8,128)}, u32[]{:S(2)}) copy-start(f32[8192,128]{1,0:T(8,128)} %refs_3_.5) | copy-start | bytes 12582916
  37.2 3.9 %copy-start.4 = (bf16[128,8192]{1,0:T(8,128)(2,1)S(1)}, bf16[128,8192]{1,0:T(8,128)(2,1)}, u32[]{:S(2)}) copy-start(bf16[128,8192]{1,0:T(8,128)(2,1)} %refs_2_.5) | copy-start | bytes 6291460
  41.1 4.0 %collective-permute-start.9 = (f32[64,128]{1,0:T(8,128)S(1)}, f32[64,128]{1,0:T(8,128)S(1)}, u32[]{:S(2)}, u32[]{:S(2)}) collective-permute-start(f32[64,128]{1,0:T(8,128)S(1)} %plane_sum.1), channel_id=1, source_target_pairs={{0,2},{1,3},{2,0},{3,1},{4,6},{5,7},{6,4},{7,5},{8,10},{9,11},{10,... | collective-permute-start | bytes 98312 | tf_op jit(solution)/shard_map/ppermute | solution.py:397
  45.0 2.2 %copy-start.6 = (bf16[512,128]{1,0:T(8,128)(2,1)S(1)}, bf16[512,128]{1,0:T(8,128)(2,1)}, u32[]{:S(2)}) copy-start(bf16[512,128]{1,0:T(8,128)(2,1)} %get-tuple-element.56.refs_7_.refs_5_.refs_4_) | copy-start | bytes 393220
  45.2 6.1 %copy-start.8 = (bf16[512,128]{1,0:T(8,128)(2,1)S(1)}, bf16[512,128]{1,0:T(8,128)(2,1)}, u32[]{:S(2)}) copy-start(bf16[512,128]{1,0:T(8,128)(2,1)} %get-tuple-element.57.refs_8_.refs_6_.refs_5_) | copy-start | bytes 393220
  45.2 6.1 %copy-start.11 = (f32[128,64]{0,1:T(8,128)S(1)}, f32[128,64]{0,1:T(8,128)}, u32[]{:S(2)}) copy-start(f32[128,64]{0,1:T(8,128)} %param.22) | copy-start | bytes 98308
  45.2 6.1 %collective-permute-start.13 = (bf16[4,128,1024]{2,1,0:T(8,128)(2,1)S(1)}, bf16[4,128,1024]{2,1,0:T(8,128)(2,1)S(1)}, u32[]{:S(2)}, u32[]{:S(2)}) collective-permute-start(bf16[4,128,1024]{2,1,0:T(8,128)(2,1)S(1)} %order.3.refs_0_), channel_id=1, source_target_pairs={{0,1},{1,0},{2,3},{3,2},{4,5},{5,4},{6,7},{7,6},{8,9},{9,8},{10,11... | collective-permute-start | bytes 3145736 | tf_op jit(solution)/shard_map/ppermute | solution.py:397
  45.3 6.0 %collective-permute-start.14 = (f32[64,128]{1,0:T(8,128)S(1)}, f32[64,128]{1,0:T(8,128)S(1)}, u32[]{:S(2)}, u32[]{:S(2)}) collective-permute-start(f32[64,128]{1,0:T(8,128)S(1)} %add.3.refs_7_), channel_id=1, source_target_pairs={{0,4},{1,5},{2,6},{3,7},{4,0},{5,1},{6,2},{7,3},{8,12},{9,13},{10,... | collective-permute-start | bytes 98312 | tf_op jit(solution)/shard_map/ppermute | solution.py:397
  (5 other events, 6.4 us)

commit v7 on v6

--- a/solution.py
+++ b/solution.py
@@ -140,7 +140,6 @@
 
 
 PARTS = 4
-HALVES = 2
 
 
 def validation_kernel(xv, gv, down_t, up, columns, rows_t, proj_out, xvs, gvs, downs, ups, tables, sems):
@@ -171,30 +170,13 @@
     proj_out[...] = mm(rows_t[...], inner, NN, HIGHEST)
 
 
-def prepare_kernel(lengths, x, g, down_t, up, top_out, bottom_out, xs, gs, downs, ups, sems):
-    tokens, width = x.shape
-    examples, rank = lengths.shape[0], up.shape[0]
-    copies = []
-    for i, (source, target) in enumerate(((up, ups), (g, gs), (down_t, downs), (x, xs))):
-        copies.append(split_copies(source, target, 1, HALVES, sems, i * HALVES))
-    for i in range(HALVES):
-        for pair in copies[:2]:
-            pair[i].start()
-    for i in range(HALVES):
-        for pair in copies[2:]:
-            pair[i].start()
-    span = width // HALVES
+def prepare_kernel(lengths, x, g, down_t, up, top_out, bottom_out):
+    tokens, rank = x.shape[0], up.shape[0]
     position = lax.broadcasted_iota(jnp.int32, (rank, tokens), 1)
-    for first, (left, right, out) in enumerate(((gs, ups, top_out), (xs, downs, bottom_out))):
-        total = zeros(tokens, rank)
-        for i in range(HALVES):
-            copies[2 * first][i].wait()
-            copies[2 * first + 1][i].wait()
-            cols = pl.ds(i * span, span)
-            total = total + mm(left[:, cols], right[:, cols], NT)
-        turned = total.T
+    for left, right, out in ((g, up, top_out), (x, down_t, bottom_out)):
+        turned = mm(left[...], right[...], NT).T
         begin = jnp.int32(0)
-        for e in range(examples):
+        for e in range(lengths.shape[0]):
             finish = begin + lengths[e]
             member = (position >= begin) & (position < finish)
             out[pl.ds(e * rank, rank), :] = jnp.where(member, turned, 0.0).astype(jnp.bfloat16)
@@ -221,14 +203,10 @@
     shape = jax.ShapeDtypeStruct((lengths.shape[0] * up.shape[0], x.shape[0]), jnp.bfloat16)
     return pl.pallas_call(
         prepare_kernel,
-        in_specs=[SMEM] + [ANY] * 4,
+        in_specs=[SMEM] + [VMEM] * 4,
         out_specs=[VMEM] * 2,
         out_shape=[shape, shape],
-        scratch_shapes=[
-            *(pltpu.VMEM(a.shape, a.dtype) for a in (x, g, down_t, up)),
-            pltpu.SemaphoreType.DMA((4 * HALVES,)),
-        ],
-        compiler_params=pltpu.CompilerParams(vmem_limit_bytes=VMEM_LIMIT),
+        compiler_params=pltpu.CompilerParams(vmem_limit_bytes=CHUNK_LIMIT),
         cost_estimate=pl.CostEstimate(flops=10**6, bytes_accessed=10**6, transcendentals=0),
         name="prepare",
     )(lengths, x, g, down_t, up)
@@ -307,7 +285,7 @@
     x, g, columns, top, bottom, rows_t = refs[:6]
     val_parts, refs = refs[6 : 6 + n_val], refs[6 + n_val :]
     partials, refs = refs[:n_partial], refs[n_partial:]
-    dirs_out, val_out, scores_out, joined, update, inner = refs
+    dirs_out, val_out, scores_out, joined, directions, update, inner = refs
     accumulate(blocks, moments, slots, x, g, columns, top, bottom, update, inner)
     rank = (update.shape[1] - top.shape[0]) // 2
     examples = top.shape[0] // rank
@@ -327,11 +305,18 @@
             joined[pl.ds(half * rank, rank), pl.ds(e * k2, k2)] = total
     projected = mm(rows, joined[...], NN, HIGHEST)
     base = projected[:, examples * k2 :]
+    projs = [projected[:, e * k2 : (e + 1) * k2] + base for e in range(examples)]
+
+    def sums(products):
+        return jnp.sum(jnp.concatenate([jnp.sum(p, axis=0, keepdims=True) for p in products], axis=0), axis=1, keepdims=True)
+
+    scale = lax.rsqrt(sums([proj * proj for proj in projs]) / size + epsilon)
+    scores = sums([proj * val_dir for proj in projs]) * scale / math.sqrt(size)
     for e in range(examples):
-        proj = projected[:, e * k2 : (e + 1) * k2] + base
-        direction = proj * lax.rsqrt(jnp.sum(proj * proj) / size + epsilon)
-        dirs_out[e] = direction
-        scores_out[e] = jnp.sum(direction * val_dir) / math.sqrt(size)
+        directions[e] = projs[e] * scale[e : e + 1]
+        scores_out[e] = scores[e, 0]
+    for j in range(k1):
+        dirs_out[:, pl.ds(j * k2, k2)] = directions[:, j, :]
 
 
 def chunk(slots, blocks, moments, x, g, columns, top, bottom, rank, last=None):
@@ -366,11 +351,15 @@
         in_specs=common + [VMEM] * (1 + len(val_parts) + len(partials)),
         out_specs=[VMEM, VMEM, SMEM],
         out_shape=[
-            jax.ShapeDtypeStruct((examples, k1, k2), jnp.float32),
+            jax.ShapeDtypeStruct((examples, k1 * k2), jnp.float32),
             jax.ShapeDtypeStruct((k1, k2), jnp.float32),
             jax.ShapeDtypeStruct((examples,), jnp.float32),
         ],
-        scratch_shapes=[pltpu.VMEM((2 * rank, (examples + 1) * k2), jnp.float32), *scratch],
+        scratch_shapes=[
+            pltpu.VMEM((2 * rank, (examples + 1) * k2), jnp.float32),
+            pltpu.VMEM((examples, k1, k2), jnp.float32),
+            *scratch,
+        ],
         name="last_chunk",
         **options,
     )(*operands, rows_t, *val_parts, *partials)

time: 58.9 us -> 53.8 us (0.913)
  Pallas kernels: 31.9 us -> 27.2 us
  waiting for transfers between devices: 0.5 us -> 4.88 us
  local copies, waits for them, and re-layouts: 7.14 us -> 3.6 us
  starting transfers between devices: 18 us -> 16.8 us
    ppermute x15, waiting for transfers between devices: 0.5 us -> 4.88 us  [exchange(): return lax.ppermute(value, axis, [(i, i ^ bits) for i in range(size)])]
    pallas_call x1, Pallas kernels: 6 us -> 1.84 us  [prepare(): pl.pallas_call(prepare_kernel, in_specs=[SMEM] + [VMEM] * 4, out_specs=[V...]
    unnamed x28 -> x26, local copies, waits for them, and re-layouts: 6.38 us -> 3.6 us
    ppermute x15, starting transfers between devices: 18 us -> 16.8 us  [exchange(): return lax.ppermute(value, axis, [(i, i ^ bits) for i in range(size)])]
    pallas_call x1, Pallas kernels: 6.38 us -> 5.39 us  [chunk(): pl.pallas_call(functools.partial(last_kernel, blocks, len(moments), len(v...]
    reshape x1 -> x0, local copies, waits for them, and re-layouts: 0.75 us -> none  [body(): dirs.reshape(1, 1, dirs.shape[0], -1)]
  transfers between devices with their start and end apart: 15 -> 15, of which waited for: 1 -> 2; matrix products, arithmetic and copies ran while one was open for 0% -> 0% of each run, Pallas kernels for 43% -> 40%
where the time goes in v7:
time: 53.8 us; the launch traced here: 53.5 us
  Pallas kernels  27.2 us (51%)
  starting transfers between devices  16.8 us (31%)
  waiting for transfers between devices  4.88 us (9%)
  local copies, waits for them, and re-layouts  3.6 us (7%)
  between operations  1.03 us (2%)
    ppermute x15, starting transfers between devices, exchange(): return lax.ppermute(value, axis, [(i, i ^ bits) for i in range(size)])  16.8 us
    pallas_call x3, Pallas kernels, chunk(): pl.pallas_call(functools.partial(chunk_kernel, blocks, len(moments)), in_...  11.6 us
    pallas_call x1, Pallas kernels, validation(): pl.pallas_call(validation_kernel, in_specs=[ANY] * 5 + [VMEM], out_specs=...  6.59 us
    pallas_call x1, Pallas kernels, chunk(): pl.pallas_call(functools.partial(last_kernel, blocks, len(moments), len(v...  5.39 us
    ppermute x15, waiting for transfers between devices, exchange(): return lax.ppermute(value, axis, [(i, i ^ bits) for i in range(size)])  4.88 us
    unnamed x26, local copies, waits for them, and re-layouts  3.6 us
    pallas_call x1, Pallas kernels, prepare(): pl.pallas_call(prepare_kernel, in_specs=[SMEM] + [VMEM] * 4, out_specs=[V...  1.84 us
    pallas_call x1, Pallas kernels, cut_piece(): pl.pallas_call(cut_kernel, in_specs=[ANY, ANY], out_specs=VMEM, out_shape...  1.54 us
  transfers between devices with their start and end apart: 15, of which 2 were waited for; matrix products, arithmetic and copies ran while one was open for 0% of the time, Pallas kernels for 40%

profile of v7, /device:TPU:0, one launch (start us, length us, event | category | flops | bytes accessed | tf_op | source)
XLA Modules:
  0.0 53.5 jit_solution(10793813091692860850)
XLA Ops:
  0.6 0.5 collective-permute-start
  1.1 0.1 collective-permute-start.1
  1.2 1.5 %cut_piece.1 = bf16[64,1024]{1,0:T(8,128)(2,1)} custom-call(bf16[4,32,1024]{2,1,0:T(8,128)(2,1)} %bitcast.11, bf16[4,32,1024]{2,1,0:T(8,128)(2,1)} %bitcast.14), custom_call_target="tpu_custom_call" | custom-call | tf_op jit(solution)/shard_map/cut_piece/pallas_call | solution.py:48
  2.8 3.1 %collective-permute-start.2 = (bf16[64,1024]{1,0:T(8,128)(2,1)}, bf16[64,1024]{1,0:T(8,128)(2,1)S(1)}, u32[]{:S(2)}, u32[]{:S(2)}) collective-permute-start(bf16[64,1024]{1,0:T(8,128)(2,1)} %cut_piece.1), channel_id=1, source_target_pairs={{0,2},{1,3},{2,0},{3,1},{4,6},{5,7},{6,4},{7,5},{8,10},{9,11},{10,... | collective-permute-start | bytes 393224 | tf_op jit(solution)/shard_map/ppermute | solution.py:386
  5.8 2.6 %collective-permute-start.3 = (bf16[64,1024]{1,0:T(8,128)(2,1)}, bf16[64,1024]{1,0:T(8,128)(2,1)S(1)}, u32[]{:S(2)}, u32[]{:S(2)}) collective-permute-start(bf16[64,1024]{1,0:T(8,128)(2,1)} %cut_piece.1), channel_id=1, source_target_pairs={{0,4},{1,5},{2,6},{3,7},{4,0},{5,1},{6,2},{7,3},{8,12},{9,13},{10,... | collective-permute-start | bytes 393224 | tf_op jit(solution)/shard_map/ppermute | solution.py:386
  8.4 6.6 %validation.1.val = f32[64,128]{1,0:T(8,128)} custom-call(bf16[32,8192]{1,0:T(8,128)(2,1)} %xv, bf16[32,8192]{1,0:T(8,128)(2,1)} %gv.1, bf16[64,8192]{1,0:T(8,128)(2,1)} %bitcast.8, bf16[64,8192]{1,0:T(8,128)(2,1)} %up.3, f32[8192,128]{1,0:T(8,128)} %refs_3_.5, f32[64,128]{1,0:T(8,128)} %bitcast.16), custom_call_target="tpu_custom_call" | custom-call | flops 1000000 | bytes 1000000 | tf_op jit(solution)/shard_map/validation/pallas_call | solution.py:187
  15.1 0.7 %copy-done.9 = f32[64,128]{1,0:T(8,128)S(1)} copy-done((f32[64,128]{1,0:T(8,128)S(1)}, f32[64,128]{1,0:T(8,128)}, u32[]{:S(2)}) %copy-start.9) | copy-done | bytes 32792
  15.9 1.6 %collective-permute-start.5 = (bf16[80,1024]{1,0:T(8,128)(2,1)S(1)}, bf16[80,1024]{1,0:T(8,128)(2,1)S(1)}, u32[]{:S(2)}, u32[]{:S(2)}) collective-permute-start(bf16[80,1024]{1,0:T(8,128)(2,1)S(1)} %pack.1.first), channel_id=1, source_target_pairs={{0,8},{8,0},{16,24},{24,16},{1,9},{9,1},{17,25},{25,17},{2,10},{10... | collective-permute-start | bytes 491528 | tf_op jit(solution)/shard_map/ppermute | solution.py:386
  17.4 1.5 %collective-permute-start.6 = (bf16[80,1024]{1,0:T(8,128)(2,1)S(1)}, bf16[80,1024]{1,0:T(8,128)(2,1)S(1)}, u32[]{:S(2)}, u32[]{:S(2)}) collective-permute-start(bf16[80,1024]{1,0:T(8,128)(2,1)S(1)} %pack.1.first), channel_id=1, source_target_pairs={{0,16},{8,24},{16,0},{24,8},{1,17},{9,25},{17,1},{25,9},{2,18},{10... | collective-permute-start | bytes 491528 | tf_op jit(solution)/shard_map/ppermute | solution.py:386
  18.9 0.5 collective-permute-start.7
  19.4 2.4 %collective-permute-start.4 = (bf16[64,1024]{1,0:T(8,128)(2,1)S(1)}, bf16[64,1024]{1,0:T(8,128)(2,1)S(1)}, u32[]{:S(2)}, u32[]{:S(2)}) collective-permute-start(bf16[64,1024]{1,0:T(8,128)(2,1)S(1)} %copy-done.12), channel_id=1, source_target_pairs={{0,6},{1,7},{2,4},{3,5},{4,2},{5,3},{6,0},{7,1},{8,14},{9,15},{10,... | collective-permute-start | bytes 393224 | tf_op jit(solution)/shard_map/ppermute | solution.py:386
  21.8 1.6 %copy-done.2 = bf16[128,8192]{1,0:T(8,128)(2,1)S(1)} copy-done((bf16[128,8192]{1,0:T(8,128)(2,1)S(1)}, bf16[128,8192]{1,0:T(8,128)(2,1)}, u32[]{:S(2)}) %copy-start.2) | copy-done | bytes 2097176
  23.4 1.2 %copy-done.5 = bf16[64,8192]{1,0:T(8,128)(2,1)S(1)} copy-done((bf16[64,8192]{1,0:T(8,128)(2,1)S(1)}, bf16[64,8192]{1,0:T(8,128)(2,1)}, u32[]{:S(2)}) %copy-start.5) | copy-done | bytes 1048600
  24.7 1.8 %prepare.1 = (bf16[512,128]{1,0:T(8,128)(2,1)S(1)}, bf16[512,128]{1,0:T(8,128)(2,1)S(1)}) custom-call(s32[8]{0:T(128)S(1)} %bitcast.18, bf16[128,8192]{1,0:T(8,128)(2,1)S(1)} %copy-done.1, bf16[128,8192]{1,0:T(8,128)(2,1)S(1)} %copy-done.2, bf16[64,8192]{1,0:T(8,128)(2,1)S(1)} %bitcast.9, bf16[64,8192]{1,0:T(8,128)(2,1)S(1)} %copy-done.5), custom_call_target="tpu_custom_call" | custom-call | flops 1000000 | bytes 1000000 | tf_op jit(solution)/shard_map/prepare/pallas_call | solution.py:204
  26.7 1.6 %collective-permute-start.10 = (bf16[128,1024]{1,0:T(8,128)(2,1)S(1)}, bf16[128,1024]{1,0:T(8,128)(2,1)S(1)}, u32[]{:S(2)}, u32[]{:S(2)}) collective-permute-start(bf16[128,1024]{1,0:T(8,128)(2,1)S(1)} %join.1.first), channel_id=1, source_target_pairs={{0,8},{8,0},{16,24},{24,16},{1,9},{9,1},{17,25},{25,17},{2,10},{10... | collective-permute-start | bytes 786440 | tf_op jit(solution)/shard_map/ppermute | solution.py:386
  28.3 1.5 %collective-permute-start.11 = (bf16[128,1024]{1,0:T(8,128)(2,1)S(1)}, bf16[128,1024]{1,0:T(8,128)(2,1)S(1)}, u32[]{:S(2)}, u32[]{:S(2)}) collective-permute-start(bf16[128,1024]{1,0:T(8,128)(2,1)S(1)} %join.1.first), channel_id=1, source_target_pairs={{0,16},{8,24},{16,0},{24,8},{1,17},{9,25},{17,1},{25,9},{2,18},{10... | collective-permute-start | bytes 786440 | tf_op jit(solution)/shard_map/ppermute | solution.py:386
  29.8 0.5 collective-permute-start.12
  30.3 3.8 %chunk.3.refs_9_ = f32[2,576,128]{2,1,0:T(8,128)S(1)} custom-call(s32[8]{0:T(128)S(1)} %copy-done.10, bf16[4,32,1024]{2,1,0:T(8,128)(2,1)S(1)} %bitcast.12, bf16[4,32,1024]{2,1,0:T(8,128)(2,1)S(1)} %bitcast.15, bf16[4,32,1024]{2,1,0:T(8,128)(2,1)S(1)} %collective-permute-done.refs_2_, bf16[4,32,1024]{2,1,0:T(8,128)(2,1)S(1)} %collective-permute-done.1.refs_3_, ...), custom_call_target="tpu_custom_call" | custom-call | flops 1000000 | bytes 1000000 | tf_op jit(solution)/shard_map/chunk/pallas_call | solution.py:338
  34.2 0.8 %collective-permute-start.9 = (f32[64,128]{1,0:T(8,128)S(1)}, f32[64,128]{1,0:T(8,128)S(1)}, u32[]{:S(2)}, u32[]{:S(2)}) collective-permute-start(f32[64,128]{1,0:T(8,128)S(1)} %plane_sum.1), channel_id=1, source_target_pairs={{0,2},{1,3},{2,0},{3,1},{4,6},{5,7},{6,4},{7,5},{8,10},{9,11},{10,... | collective-permute-start | bytes 98312 | tf_op jit(solution)/shard_map/ppermute | solution.py:386
  35.0 3.8 %chunk.4.refs_10_ = f32[2,576,128]{2,1,0:T(8,128)S(1)} custom-call(s32[8]{0:T(128)S(1)} %copy-done.10, bf16[4,80,1024]{2,1,0:T(8,128)(2,1)S(1)} %order.2.own.refs_0_, bf16[4,80,1024]{2,1,0:T(8,128)(2,1)S(1)} %collective-permute-done.8.crossed.refs_1_, bf16[128,8192]{1,0:T(8,128)(2,1)S(1)} %copy-done.1, bf16[128,8192]{1,0:T(8,128)(2,1)S(1)} %copy-done.3, ...), custom_call_target="tpu_custom_call" | custom-call | flops 1000000 | bytes 1000000 | tf_op jit(solution)/shard_map/chunk/pallas_call | solution.py:338
  38.8 3.5 %collective-permute-done.11.third = bf16[128,1024]{1,0:T(8,128)(2,1)S(1)} collective-permute-done((bf16[128,1024]{1,0:T(8,128)(2,1)S(1)}, bf16[128,1024]{1,0:T(8,128)(2,1)S(1)}, u32[]{:S(2)}, u32[]{:S(2)}) %collective-permute-start.11) | collective-permute-done | bytes 262176 | tf_op jit(solution)/shard_map/ppermute | solution.py:386
  42.6 4.0 %chunk.5.refs_11_ = f32[2,576,128]{2,1,0:T(8,128)S(1)} custom-call(s32[8]{0:T(128)S(1)} %copy-done.10, bf16[4,128,1024]{2,1,0:T(8,128)(2,1)S(1)} %order.3.refs_0_, bf16[128,8192]{1,0:T(8,128)(2,1)S(1)} %copy-done.1, bf16[128,8192]{1,0:T(8,128)(2,1)S(1)} %copy-done.3, f32[8192,128]{1,0:T(8,128)S(1)} %copy-done, ...), custom_call_target="tpu_custom_call" | custom-call | flops 1000000 | bytes 1000000 | tf_op jit(solution)/shard_map/chunk/pallas_call | solution.py:338
  46.6 1.3 %collective-permute-done.14.refs_8_ = f32[64,128]{1,0:T(8,128)S(1)} collective-permute-done((f32[64,128]{1,0:T(8,128)S(1)}, f32[64,128]{1,0:T(8,128)S(1)}, u32[]{:S(2)}, u32[]{:S(2)}) %collective-permute-start.14) | collective-permute-done | bytes 32800 | tf_op jit(solution)/shard_map/ppermute | solution.py:386
  47.9 5.4 %last_chunk.1 = (f32[8,8192]{1,0:T(8,128)}, f32[64,128]{1,0:T(8,128)}, f32[8]{0:T(128)}) custom-call(s32[8]{0:T(128)S(1)} %copy-done.10, bf16[4,128,1024]{2,1,0:T(8,128)(2,1)S(1)} %collective-permute-done.13.refs_0_, bf16[128,8192]{1,0:T(8,128)(2,1)S(1)} %copy-done.1, bf16[128,8192]{1,0:T(8,128)(2,1)S(1)} %copy-done.3, f32[8192,128]{1,0:T(8,128)S(1)} %copy-done, ...), custom_call_target="tpu_custom_call" | custom-call | flops 1000000 | bytes 1000000 | tf_op jit(solution)/shard_map/last_chunk/pallas_call | solution.py:349
  (45 shorter events, 0.5 us)
Async XLA Ops:
  0.6 14.4 %collective-permute-start = (bf16[4,32,1024]{2,1,0:T(8,128)(2,1)}, bf16[4,32,1024]{2,1,0:T(8,128)(2,1)S(1)}, u32[]{:S(2)}, u32[]{:S(2)}) collective-permute-start(bf16[4,32,1024]{2,1,0:T(8,128)(2,1)} %bitcast.10), channel_id=1, source_target_pairs={{0,1},{1,0},{2,3},{3,2},{4,5},{5,4},{6,7},{7,6},{8,9},{9,8},{10,11... | collective-permute-start | bytes 786440 | tf_op jit(solution)/shard_map/ppermute | solution.py:386
  1.1 13.9 %collective-permute-start.1 = (bf16[4,32,1024]{2,1,0:T(8,128)(2,1)}, bf16[4,32,1024]{2,1,0:T(8,128)(2,1)S(1)}, u32[]{:S(2)}, u32[]{:S(2)}) collective-permute-start(bf16[4,32,1024]{2,1,0:T(8,128)(2,1)} %bitcast.13), channel_id=1, source_target_pairs={{0,1},{1,0},{2,3},{3,2},{4,5},{5,4},{6,7},{7,6},{8,9},{9,8},{10,11... | collective-permute-start | bytes 786440 | tf_op jit(solution)/shard_map/ppermute | solution.py:386
  2.8 12.3 %collective-permute-start.2 = (bf16[64,1024]{1,0:T(8,128)(2,1)}, bf16[64,1024]{1,0:T(8,128)(2,1)S(1)}, u32[]{:S(2)}, u32[]{:S(2)}) collective-permute-start(bf16[64,1024]{1,0:T(8,128)(2,1)} %cut_piece.1), channel_id=1, source_target_pairs={{0,2},{1,3},{2,0},{3,1},{4,6},{5,7},{6,4},{7,5},{8,10},{9,11},{10,... | collective-permute-start | bytes 393224 | tf_op jit(solution)/shard_map/ppermute | solution.py:386
  5.8 9.2 %collective-permute-start.3 = (bf16[64,1024]{1,0:T(8,128)(2,1)}, bf16[64,1024]{1,0:T(8,128)(2,1)S(1)}, u32[]{:S(2)}, u32[]{:S(2)}) collective-permute-start(bf16[64,1024]{1,0:T(8,128)(2,1)} %cut_piece.1), channel_id=1, source_target_pairs={{0,4},{1,5},{2,6},{3,7},{4,0},{5,1},{6,2},{7,3},{8,12},{9,13},{10,... | collective-permute-start | bytes 393224 | tf_op jit(solution)/shard_map/ppermute | solution.py:386
  8.4 11.0 %copy-start.12 = (bf16[64,1024]{1,0:T(8,128)(2,1)S(1)}, bf16[64,1024]{1,0:T(8,128)(2,1)}, u32[]{:S(2)}) copy-start(bf16[64,1024]{1,0:T(8,128)(2,1)} %cut_piece.1) | copy-start | bytes 393220
  8.4 13.4 %copy-start.1 = (bf16[128,8192]{1,0:T(8,128)(2,1)S(1)}, bf16[128,8192]{1,0:T(8,128)(2,1)}, u32[]{:S(2)}) copy-start(bf16[128,8192]{1,0:T(8,128)(2,1)} %refs_1_.3) | copy-start | bytes 6291460
  8.4 13.4 %copy-start.4 = (bf16[8192,64]{0,1:T(8,128)(2,1)S(1)}, bf16[8192,64]{0,1:T(8,128)(2,1)}, u32[]{:S(2)}) copy-start(bf16[8192,64]{0,1:T(8,128)(2,1)} %param.16) | copy-start | bytes 3145732
  8.4 13.4 %copy-start.11 = (s32[1,1,8]{2,1,0:T(1,128)S(1)}, s32[1,1,8]{2,1,0:T(1,128)}, u32[]{:S(2)}) copy-start(s32[1,1,8]{2,1,0:T(1,128)} %param.21) | copy-start | bytes 100
  15.8 14.4 %copy-start.6 = (bf16[1,128,1024]{2,1,0:T(8,128)(2,1)S(1)}, bf16[1,128,1024]{2,1,0:T(8,128)(2,1)}, u32[]{:S(2)}) copy-start(bf16[1,128,1024]{2,1,0:T(8,128)(2,1)} %param.18) | copy-start | bytes 786436
  15.9 14.4 %copy-start.10 = (s32[8]{0:T(128)S(1)}, s32[8]{0:T(128)}, u32[]{:S(2)}) copy-start(s32[8]{0:T(128)} %slots.7) | copy-start | bytes 100
  15.9 10.7 %collective-permute-start.5 = (bf16[80,1024]{1,0:T(8,128)(2,1)S(1)}, bf16[80,1024]{1,0:T(8,128)(2,1)S(1)}, u32[]{:S(2)}, u32[]{:S(2)}) collective-permute-start(bf16[80,1024]{1,0:T(8,128)(2,1)S(1)} %pack.1.first), channel_id=1, source_target_pairs={{0,8},{8,0},{16,24},{24,16},{1,9},{9,1},{17,25},{25,17},{2,10},{10... | collective-permute-start | bytes 491528 | tf_op jit(solution)/shard_map/ppermute | solution.py:386
  17.4 9.1 %collective-permute-start.6 = (bf16[80,1024]{1,0:T(8,128)(2,1)S(1)}, bf16[80,1024]{1,0:T(8,128)(2,1)S(1)}, u32[]{:S(2)}, u32[]{:S(2)}) collective-permute-start(bf16[80,1024]{1,0:T(8,128)(2,1)S(1)} %pack.1.first), channel_id=1, source_target_pairs={{0,16},{8,24},{16,0},{24,8},{1,17},{9,25},{17,1},{25,9},{2,18},{10... | collective-permute-start | bytes 491528 | tf_op jit(solution)/shard_map/ppermute | solution.py:386
  18.9 7.6 %collective-permute-start.7 = (bf16[80,1024]{1,0:T(8,128)(2,1)S(1)}, bf16[80,1024]{1,0:T(8,128)(2,1)S(1)}, u32[]{:S(2)}, u32[]{:S(2)}) collective-permute-start(bf16[80,1024]{1,0:T(8,128)(2,1)S(1)} %pack.1.first), channel_id=1, source_target_pairs={{0,24},{8,16},{16,8},{24,0},{1,25},{9,17},{17,9},{25,1},{2,26},{10... | collective-permute-start | bytes 491528 | tf_op jit(solution)/shard_map/ppermute | solution.py:386
  19.4 7.1 %collective-permute-start.4 = (bf16[64,1024]{1,0:T(8,128)(2,1)S(1)}, bf16[64,1024]{1,0:T(8,128)(2,1)S(1)}, u32[]{:S(2)}, u32[]{:S(2)}) collective-permute-start(bf16[64,1024]{1,0:T(8,128)(2,1)S(1)} %copy-done.12), channel_id=1, source_target_pairs={{0,6},{1,7},{2,4},{3,5},{4,2},{5,3},{6,0},{7,1},{8,14},{9,15},{10,... | collective-permute-start | bytes 393224 | tf_op jit(solution)/shard_map/ppermute | solution.py:386
  24.7 5.6 %copy-start = (f32[8192,128]{1,0:T(8,128)S(1)}, f32[8192,128]{1,0:T(8,128)}, u32[]{:S(2)}) copy-start(f32[8192,128]{1,0:T(8,128)} %refs_3_.5) | copy-start | bytes 12582916
  24.7 5.6 %copy-start.3 = (bf16[128,8192]{1,0:T(8,128)(2,1)S(1)}, bf16[128,8192]{1,0:T(8,128)(2,1)}, u32[]{:S(2)}) copy-start(bf16[128,8192]{1,0:T(8,128)(2,1)} %refs_2_.5) | copy-start | bytes 6291460
  24.7 5.6 %copy-start.7 = (bf16[1,128,1024]{2,1,0:T(8,128)(2,1)S(1)}, bf16[1,128,1024]{2,1,0:T(8,128)(2,1)}, u32[]{:S(2)}) copy-start(bf16[1,128,1024]{2,1,0:T(8,128)(2,1)} %param.19) | copy-start | bytes 786436
  26.6 7.5 %collective-permute-start.8 = (bf16[4,80,1024]{2,1,0:T(8,128)(2,1)S(1)}, bf16[4,80,1024]{2,1,0:T(8,128)(2,1)S(1)}, u32[]{:S(2)}, u32[]{:S(2)}) collective-permute-start(bf16[4,80,1024]{2,1,0:T(8,128)(2,1)S(1)} %order.2.own.refs_0_), channel_id=1, source_target_pairs={{0,1},{1,0},{2,3},{3,2},{4,5},{5,4},{6,7},{7,6},{8,9},{9,8},{10,11... | collective-permute-start | bytes 1966088 | tf_op jit(solution)/shard_map/ppermute | solution.py:386
  26.7 12.1 %collective-permute-start.10 = (bf16[128,1024]{1,0:T(8,128)(2,1)S(1)}, bf16[128,1024]{1,0:T(8,128)(2,1)S(1)}, u32[]{:S(2)}, u32[]{:S(2)}) collective-permute-start(bf16[128,1024]{1,0:T(8,128)(2,1)S(1)} %join.1.first), channel_id=1, source_target_pairs={{0,8},{8,0},{16,24},{24,16},{1,9},{9,1},{17,25},{25,17},{2,10},{10... | collective-permute-start | bytes 786440 | tf_op jit(solution)/shard_map/ppermute | solution.py:386
  28.3 14.0 %collective-permute-start.11 = (bf16[128,1024]{1,0:T(8,128)(2,1)S(1)}, bf16[128,1024]{1,0:T(8,128)(2,1)S(1)}, u32[]{:S(2)}, u32[]{:S(2)}) collective-permute-start(bf16[128,1024]{1,0:T(8,128)(2,1)S(1)} %join.1.first), channel_id=1, source_target_pairs={{0,16},{8,24},{16,0},{24,8},{1,17},{9,25},{17,1},{25,9},{2,18},{10... | collective-permute-start | bytes 786440 | tf_op jit(solution)/shard_map/ppermute | solution.py:386
  29.8 12.5 %collective-permute-start.12 = (bf16[128,1024]{1,0:T(8,128)(2,1)S(1)}, bf16[128,1024]{1,0:T(8,128)(2,1)S(1)}, u32[]{:S(2)}, u32[]{:S(2)}) collective-permute-start(bf16[128,1024]{1,0:T(8,128)(2,1)S(1)} %join.1.first), channel_id=1, source_target_pairs={{0,24},{8,16},{16,8},{24,0},{1,25},{9,17},{17,9},{25,1},{2,26},{10... | collective-permute-start | bytes 786440 | tf_op jit(solution)/shard_map/ppermute | solution.py:386
  34.2 8.2 %collective-permute-start.9 = (f32[64,128]{1,0:T(8,128)S(1)}, f32[64,128]{1,0:T(8,128)S(1)}, u32[]{:S(2)}, u32[]{:S(2)}) collective-permute-start(f32[64,128]{1,0:T(8,128)S(1)} %plane_sum.1), channel_id=1, source_target_pairs={{0,2},{1,3},{2,0},{3,1},{4,6},{5,7},{6,4},{7,5},{8,10},{9,11},{10,... | collective-permute-start | bytes 98312 | tf_op jit(solution)/shard_map/ppermute | solution.py:386
  42.4 5.5 %collective-permute-start.13 = (bf16[4,128,1024]{2,1,0:T(8,128)(2,1)S(1)}, bf16[4,128,1024]{2,1,0:T(8,128)(2,1)S(1)}, u32[]{:S(2)}, u32[]{:S(2)}) collective-permute-start(bf16[4,128,1024]{2,1,0:T(8,128)(2,1)S(1)} %order.3.refs_0_), channel_id=1, source_target_pairs={{0,1},{1,0},{2,3},{3,2},{4,5},{5,4},{6,7},{7,6},{8,9},{9,8},{10,11... | collective-permute-start | bytes 3145736 | tf_op jit(solution)/shard_map/ppermute | solution.py:386
  42.5 5.4 %collective-permute-start.14 = (f32[64,128]{1,0:T(8,128)S(1)}, f32[64,128]{1,0:T(8,128)S(1)}, u32[]{:S(2)}, u32[]{:S(2)}) collective-permute-start(f32[64,128]{1,0:T(8,128)S(1)} %add.3.refs_7_), channel_id=1, source_target_pairs={{0,4},{1,5},{2,6},{3,7},{4,0},{5,1},{6,2},{7,3},{8,12},{9,13},{10,... | collective-permute-start | bytes 98312 | tf_op jit(solution)/shard_map/ppermute | solution.py:386
  (4 other events, 9.1 us)

commit v8 on v7

--- a/solution.py
+++ b/solution.py
@@ -77,29 +77,19 @@
     )(*operands)
 
 
-def pack_kernel(piece, val, out):
-    rows = piece.shape[0]
-    out[pl.ds(0, rows), :] = piece[...]
+def pack_kernel(first, second, val, out):
+    rows = first.shape[0]
+    out[pl.ds(0, rows), :] = first[...]
+    out[pl.ds(rows, rows), :] = second[...]
     wide = fold(val[...], out.shape[1] // val.shape[1])
     coarse = wide.astype(jnp.bfloat16).astype(jnp.float32)
     terms = jnp.concatenate([coarse, wide - coarse], axis=0)
-    out[pl.ds(rows, terms.shape[0]), :] = terms.astype(jnp.bfloat16)
-
-
-def pack(piece, val):
-    rows, span = piece.shape
-    return on_vmem(pack_kernel, (rows + 2 * val.size // span, span), piece.dtype, "pack", piece, val)
-
-
-def join_kernel(first, second, out):
-    rows = first.shape[0]
-    out[pl.ds(0, rows), :] = first[...]
-    out[pl.ds(rows, rows), :] = second[...]
-
-
-def join(first, second):
+    out[pl.ds(2 * rows, terms.shape[0]), :] = terms.astype(jnp.bfloat16)
+
+
+def pack(first, second, val):
     rows, span = first.shape
-    return on_vmem(join_kernel, (2 * rows, span), first.dtype, "join", first, second)
+    return on_vmem(pack_kernel, (2 * rows + 2 * val.size // span, span), first.dtype, "pack", first, second, val)
 
 
 def order_kernel(first, second, third, fourth, out):
@@ -421,37 +411,32 @@
     top, bottom = prepare(lengths, *train, down_t, adapter_up)
     if stepwise:
         val_part, *sibling, far[0], far[1] = lax.optimization_barrier((val_part, *sibling, far[0], far[1]))
-        packed = pack(far[0], val_part)
+        packed = pack(far[0], far[1], val_part)
         near = [packed] + [exchange(packed, "dp", bits) for bits in (1, 2, 3)]
-        *arrived, top, bottom = lax.optimization_barrier((*far[1:], *near, top, bottom))
-        rest = join(*arrived[:2])
-        four = [rest] + [exchange(rest, "dp", bits) for bits in (1, 2, 3)]
-        one = order(arrived[2:])
-        one, top, bottom = lax.optimization_barrier((one, top, bottom))
-        one_crossed = exchange(one, "shard", 1)
         operands = (*train, projection_columns, top, bottom, rank)
         slots = slot_block_index
-        partials = [chunk(slots, [paired_block(quarter, i, i) for i in (0, 1)], own + sibling, *operands)]
-        partials[0], one_crossed = lax.optimization_barrier((partials[0], one_crossed))
-        total = plane_sum(2 * quarter, val_part.shape, one, one_crossed)
-        total, one_crossed = lax.optimization_barrier((total, one_crossed))
+        first = chunk(slots, [paired_block(quarter, i, i) for i in (0, 1)], own + sibling, *operands)
+        first, last_far, *near = lax.optimization_barrier((first, far[2], *near))
+        four = [last_far] + [exchange(last_far, "dp", bits) for bits in (1, 2, 3)]
+        one = order(near)
+        one_crossed = exchange(one, "shard", 1)
+        second = chunk(slots, [ordered_block(quarter, 0, 1 + i, 0, i) for i in (0, 1)], [one], *operands)
+        second, one_crossed, *four = lax.optimization_barrier((second, one_crossed, *four))
+        total = plane_sum(4 * quarter, val_part.shape, one, one_crossed)
+        both = order(four)
+        total, both, one_crossed = lax.optimization_barrier((total, both, one_crossed))
         other = exchange(total, "shard", 2)
-        partials.append(
-            chunk(slots, [ordered_block(quarter, i, 1, i, 0) for i in (0, 1)], [one, one_crossed], *operands)
-        )
-        partials[1], other, *four = lax.optimization_barrier((partials[1], other, *four))
+        both_crossed = exchange(both, "shard", 1)
+        third = chunk(slots, [ordered_block(quarter, 1, 1 + i, 0, i) for i in (0, 1)], [one_crossed], *operands)
+        third, other = lax.optimization_barrier((third, other))
         total = total + other
-        both = order(four)
-        total, both = lax.optimization_barrier((total, both))
         val_parts = [total, exchange(total, "shard", 4)]
-        both_crossed = exchange(both, "shard", 1)
-        partials.append(chunk(slots, [ordered_block(quarter, 0, 2 + i, 0, i) for i in (0, 1)], [both], *operands))
         dirs, val_dir, scores = chunk(
             slots,
-            [ordered_block(quarter, 1, 2 + i, 0, i) for i in (0, 1)],
-            [both_crossed],
+            [ordered_block(quarter, i, 3, i, 0) for i in (0, 1)],
+            [both, both_crossed],
             *operands,
-            last=(rows_t, val_parts, partials),
+            last=(rows_t, val_parts, [first, second, third]),
         )
     else:
         operands = (*train, projection_columns, top, bottom, rank)

time: 53.8 us -> 57.4 us (1.067)
  starting transfers between devices: 16.8 us -> 18.9 us
  waiting for transfers between devices: 4.88 us -> 6.3 us
    ppermute x15, starting transfers between devices: 16.8 us -> 18.9 us  [exchange(): return lax.ppermute(value, axis, [(i, i ^ bits) for i in range(size)])]
    ppermute x15, waiting for transfers between devices: 4.88 us -> 6.3 us  [exchange(): return lax.ppermute(value, axis, [(i, i ^ bits) for i in range(size)])]
  transfers between devices with their start and end apart: 15 -> 15, of which waited for: 2 -> 4; matrix products, arithmetic and copies ran while one was open for 0% -> 0% of each run, Pallas kernels for 40% -> 38%
where the time goes in v8:
time: 57.4 us; the launch traced here: 57.1 us
  Pallas kernels  27.3 us (48%)
  starting transfers between devices  18.9 us (33%)
  waiting for transfers between devices  6.3 us (11%)
  local copies, waits for them, and re-layouts  3.61 us (6%)
  between operations  1.03 us (2%)
    ppermute x15, starting transfers between devices, exchange(): return lax.ppermute(value, axis, [(i, i ^ bits) for i in range(size)])  18.9 us
    pallas_call x3, Pallas kernels, chunk(): pl.pallas_call(functools.partial(chunk_kernel, blocks, len(moments)), in_...  11.7 us
    pallas_call x1, Pallas kernels, validation(): pl.pallas_call(validation_kernel, in_specs=[ANY] * 5 + [VMEM], out_specs=...  6.59 us
    ppermute x15, waiting for transfers between devices, exchange(): return lax.ppermute(value, axis, [(i, i ^ bits) for i in range(size)])  6.3 us
    pallas_call x1, Pallas kernels, chunk(): pl.pallas_call(functools.partial(last_kernel, blocks, len(moments), len(v...  5.46 us
    unnamed x26, local copies, waits for them, and re-layouts  3.61 us
    pallas_call x1, Pallas kernels, prepare(): pl.pallas_call(prepare_kernel, in_specs=[SMEM] + [VMEM] * 4, out_specs=[V...  1.84 us
    pallas_call x1, Pallas kernels, cut_piece(): pl.pallas_call(cut_kernel, in_specs=[ANY, ANY], out_specs=VMEM, out_shape...  1.54 us
  transfers between devices with their start and end apart: 15, of which 4 were waited for; matrix products, arithmetic and copies ran while one was open for 0% of the time, Pallas kernels for 38%

profile of v8, /device:TPU:0, one launch (start us, length us, event | category | flops | bytes accessed | tf_op | source)
XLA Modules:
  0.0 57.1 jit_solution(1820022156366389811)
XLA Ops:
  0.6 0.5 collective-permute-start
  1.2 1.5 %cut_piece.1 = bf16[64,1024]{1,0:T(8,128)(2,1)} custom-call(bf16[4,32,1024]{2,1,0:T(8,128)(2,1)} %bitcast.11, bf16[4,32,1024]{2,1,0:T(8,128)(2,1)} %bitcast.14), custom_call_target="tpu_custom_call" | custom-call | tf_op jit(solution)/shard_map/cut_piece/pallas_call | solution.py:48
  2.8 4.1 %collective-permute-start.3 = (bf16[64,1024]{1,0:T(8,128)(2,1)}, bf16[64,1024]{1,0:T(8,128)(2,1)S(1)}, u32[]{:S(2)}, u32[]{:S(2)}) collective-permute-start(bf16[64,1024]{1,0:T(8,128)(2,1)} %cut_piece.1), channel_id=1, source_target_pairs={{0,4},{1,5},{2,6},{3,7},{4,0},{5,1},{6,2},{7,3},{8,12},{9,13},{10,... | collective-permute-start | bytes 393224 | tf_op jit(solution)/shard_map/ppermute | solution.py:376
  6.9 1.6 %collective-permute-start.2 = (bf16[64,1024]{1,0:T(8,128)(2,1)}, bf16[64,1024]{1,0:T(8,128)(2,1)S(1)}, u32[]{:S(2)}, u32[]{:S(2)}) collective-permute-start(bf16[64,1024]{1,0:T(8,128)(2,1)} %cut_piece.1), channel_id=1, source_target_pairs={{0,2},{1,3},{2,0},{3,1},{4,6},{5,7},{6,4},{7,5},{8,10},{9,11},{10,... | collective-permute-start | bytes 393224 | tf_op jit(solution)/shard_map/ppermute | solution.py:376
  8.4 6.6 %validation.1.val = f32[64,128]{1,0:T(8,128)} custom-call(bf16[32,8192]{1,0:T(8,128)(2,1)} %xv, bf16[32,8192]{1,0:T(8,128)(2,1)} %gv.1, bf16[64,8192]{1,0:T(8,128)(2,1)} %bitcast.8, bf16[64,8192]{1,0:T(8,128)(2,1)} %up.3, f32[8192,128]{1,0:T(8,128)} %refs_4_.3, f32[64,128]{1,0:T(8,128)} %bitcast.16), custom_call_target="tpu_custom_call" | custom-call | flops 1000000 | bytes 1000000 | tf_op jit(solution)/shard_map/validation/pallas_call | solution.py:177
  15.1 0.7 %copy-done.9 = f32[64,128]{1,0:T(8,128)S(1)} copy-done((f32[64,128]{1,0:T(8,128)S(1)}, f32[64,128]{1,0:T(8,128)}, u32[]{:S(2)}) %copy-start.9) | copy-done | bytes 32792
  15.9 2.5 %collective-permute-start.7 = (bf16[144,1024]{1,0:T(8,128)(2,1)S(1)}, bf16[144,1024]{1,0:T(8,128)(2,1)S(1)}, u32[]{:S(2)}, u32[]{:S(2)}) collective-permute-start(bf16[144,1024]{1,0:T(8,128)(2,1)S(1)} %pack.1.first), channel_id=1, source_target_pairs={{0,24},{8,16},{16,8},{24,0},{1,25},{9,17},{17,9},{25,1},{2,26},{10... | collective-permute-start | bytes 884744 | tf_op jit(solution)/shard_map/ppermute | solution.py:376
  18.4 0.5 collective-permute-start.6
  18.9 0.5 collective-permute-start.5
  19.5 2.1 %collective-permute-start.4 = (bf16[64,1024]{1,0:T(8,128)(2,1)S(1)}, bf16[64,1024]{1,0:T(8,128)(2,1)S(1)}, u32[]{:S(2)}, u32[]{:S(2)}) collective-permute-start(bf16[64,1024]{1,0:T(8,128)(2,1)S(1)} %copy-done.12), channel_id=1, source_target_pairs={{0,6},{1,7},{2,4},{3,5},{4,2},{5,3},{6,0},{7,1},{8,14},{9,15},{10,... | collective-permute-start | bytes 393224 | tf_op jit(solution)/shard_map/ppermute | solution.py:376
  21.6 1.6 %copy-done.2 = bf16[128,8192]{1,0:T(8,128)(2,1)S(1)} copy-done((bf16[128,8192]{1,0:T(8,128)(2,1)S(1)}, bf16[128,8192]{1,0:T(8,128)(2,1)}, u32[]{:S(2)}) %copy-start.2) | copy-done | bytes 2097176
  23.1 1.2 %copy-done.5 = bf16[64,8192]{1,0:T(8,128)(2,1)S(1)} copy-done((bf16[64,8192]{1,0:T(8,128)(2,1)S(1)}, bf16[64,8192]{1,0:T(8,128)(2,1)}, u32[]{:S(2)}) %copy-start.5) | copy-done | bytes 1048600
  24.4 1.8 %prepare.1 = (bf16[512,128]{1,0:T(8,128)(2,1)S(1)}, bf16[512,128]{1,0:T(8,128)(2,1)S(1)}) custom-call(s32[8]{0:T(128)S(1)} %bitcast.18, bf16[128,8192]{1,0:T(8,128)(2,1)S(1)} %copy-done.1, bf16[128,8192]{1,0:T(8,128)(2,1)S(1)} %copy-done.2, bf16[64,8192]{1,0:T(8,128)(2,1)S(1)} %bitcast.9, bf16[64,8192]{1,0:T(8,128)(2,1)S(1)} %copy-done.5), custom_call_target="tpu_custom_call" | custom-call | flops 1000000 | bytes 1000000 | tf_op jit(solution)/shard_map/prepare/pallas_call | solution.py:194
  26.3 3.8 %chunk.3.refs_10_ = f32[2,576,128]{2,1,0:T(8,128)S(1)} custom-call(s32[8]{0:T(128)S(1)} %copy-done.10, bf16[4,32,1024]{2,1,0:T(8,128)(2,1)S(1)} %bitcast.12, bf16[4,32,1024]{2,1,0:T(8,128)(2,1)S(1)} %bitcast.15, bf16[4,32,1024]{2,1,0:T(8,128)(2,1)S(1)} %collective-permute-done.refs_2_, bf16[4,32,1024]{2,1,0:T(8,128)(2,1)S(1)} %collective-permute-done.1.refs_3_, ...), custom_call_target="tpu_custom_call" | custom-call | flops 1000000 | bytes 1000000 | tf_op jit(solution)/shard_map/chunk/pallas_call | solution.py:328
  30.1 1.5 %collective-permute-done.6.third = bf16[144,1024]{1,0:T(8,128)(2,1)S(1)} collective-permute-done((bf16[144,1024]{1,0:T(8,128)(2,1)S(1)}, bf16[144,1024]{1,0:T(8,128)(2,1)S(1)}, u32[]{:S(2)}, u32[]{:S(2)}) %collective-permute-start.6) | collective-permute-done | bytes 294944 | tf_op jit(solution)/shard_map/ppermute | solution.py:376
  31.9 1.7 %collective-permute-start.11 = (bf16[64,1024]{1,0:T(8,128)(2,1)S(1)}, bf16[64,1024]{1,0:T(8,128)(2,1)S(1)}, u32[]{:S(2)}, u32[]{:S(2)}) collective-permute-start(bf16[64,1024]{1,0:T(8,128)(2,1)S(1)} %collective-permute-done.4.first), channel_id=1, source_target_pairs={{0,24},{8,16},{16,8},{24,0},{1,25},{9,17},{17,9},{25,1},{2,26},{10... | collective-permute-start | bytes 393224 | tf_op jit(solution)/shard_map/ppermute | solution.py:376
  33.6 1.3 %collective-permute-start.10 = (bf16[64,1024]{1,0:T(8,128)(2,1)S(1)}, bf16[64,1024]{1,0:T(8,128)(2,1)S(1)}, u32[]{:S(2)}, u32[]{:S(2)}) collective-permute-start(bf16[64,1024]{1,0:T(8,128)(2,1)S(1)} %collective-permute-done.4.first), channel_id=1, source_target_pairs={{0,16},{8,24},{16,0},{24,8},{1,17},{9,25},{17,1},{25,9},{2,18},{10... | collective-permute-start | bytes 393224 | tf_op jit(solution)/shard_map/ppermute | solution.py:376
  34.9 0.5 collective-permute-start.9
  35.4 3.8 %chunk.4.refs_11_ = f32[2,576,128]{2,1,0:T(8,128)S(1)} custom-call(s32[8]{0:T(128)S(1)} %copy-done.10, bf16[4,144,1024]{2,1,0:T(8,128)(2,1)S(1)} %order.2.refs_0_.own, bf16[128,8192]{1,0:T(8,128)(2,1)S(1)} %copy-done.1, bf16[128,8192]{1,0:T(8,128)(2,1)S(1)} %copy-done.3, f32[8192,128]{1,0:T(8,128)S(1)} %copy-done, ...), custom_call_target="tpu_custom_call" | custom-call | flops 1000000 | bytes 1000000 | tf_op jit(solution)/shard_map/chunk/pallas_call | solution.py:328
  39.3 2.2 %collective-permute-done.10.third = bf16[64,1024]{1,0:T(8,128)(2,1)S(1)} collective-permute-done((bf16[64,1024]{1,0:T(8,128)(2,1)S(1)}, bf16[64,1024]{1,0:T(8,128)(2,1)S(1)}, u32[]{:S(2)}, u32[]{:S(2)}) %collective-permute-start.10) | collective-permute-done | bytes 131104 | tf_op jit(solution)/shard_map/ppermute | solution.py:376
  42.2 4.0 %chunk.5.refs_12_ = f32[2,576,128]{2,1,0:T(8,128)S(1)} custom-call(s32[8]{0:T(128)S(1)} %copy-done.10, bf16[4,144,1024]{2,1,0:T(8,128)(2,1)S(1)} %collective-permute-done.8.crossed.refs_0_, bf16[128,8192]{1,0:T(8,128)(2,1)S(1)} %copy-done.1, bf16[128,8192]{1,0:T(8,128)(2,1)S(1)} %copy-done.3, f32[8192,128]{1,0:T(8,128)S(1)} %copy-done, ...), custom_call_target="tpu_custom_call" | custom-call | flops 1000000 | bytes 1000000 | tf_op jit(solution)/shard_map/chunk/pallas_call | solution.py:328
  46.3 2.8 %collective-permute-start.14 = (f32[64,128]{1,0:T(8,128)S(1)}, f32[64,128]{1,0:T(8,128)S(1)}, u32[]{:S(2)}, u32[]{:S(2)}) collective-permute-start(f32[64,128]{1,0:T(8,128)S(1)} %add.3.refs_8_), channel_id=1, source_target_pairs={{0,4},{1,5},{2,6},{3,7},{4,0},{5,1},{6,2},{7,3},{8,12},{9,13},{10,... | collective-permute-start | bytes 98312 | tf_op jit(solution)/shard_map/ppermute | solution.py:376
  49.1 2.5 %collective-permute-done.14.refs_9_ = f32[64,128]{1,0:T(8,128)S(1)} collective-permute-done((f32[64,128]{1,0:T(8,128)S(1)}, f32[64,128]{1,0:T(8,128)S(1)}, u32[]{:S(2)}, u32[]{:S(2)}) %collective-permute-start.14) | collective-permute-done | bytes 32800 | tf_op jit(solution)/shard_map/ppermute | solution.py:376
  51.5 5.5 %last_chunk.1 = (f32[8,8192]{1,0:T(8,128)}, f32[64,128]{1,0:T(8,128)}, f32[8]{0:T(128)}) custom-call(s32[8]{0:T(128)S(1)} %copy-done.10, bf16[4,64,1024]{2,1,0:T(8,128)(2,1)S(1)} %order.3.refs_0_, bf16[4,64,1024]{2,1,0:T(8,128)(2,1)S(1)} %collective-permute-done.12.refs_1_, bf16[128,8192]{1,0:T(8,128)(2,1)S(1)} %copy-done.1, ...), custom_call_target="tpu_custom_call" | custom-call | flops 1000000 | bytes 1000000 | tf_op jit(solution)/shard_map/last_chunk/pallas_call | solution.py:339
  (44 shorter events, 1.1 us)
Async XLA Ops:
  0.6 14.4 %collective-permute-start = (bf16[4,32,1024]{2,1,0:T(8,128)(2,1)}, bf16[4,32,1024]{2,1,0:T(8,128)(2,1)S(1)}, u32[]{:S(2)}, u32[]{:S(2)}) collective-permute-start(bf16[4,32,1024]{2,1,0:T(8,128)(2,1)} %bitcast.10), channel_id=1, source_target_pairs={{0,1},{1,0},{2,3},{3,2},{4,5},{5,4},{6,7},{7,6},{8,9},{9,8},{10,11... | collective-permute-start | bytes 786440 | tf_op jit(solution)/shard_map/ppermute | solution.py:376
  1.1 13.9 %collective-permute-start.1 = (bf16[4,32,1024]{2,1,0:T(8,128)(2,1)}, bf16[4,32,1024]{2,1,0:T(8,128)(2,1)S(1)}, u32[]{:S(2)}, u32[]{:S(2)}) collective-permute-start(bf16[4,32,1024]{2,1,0:T(8,128)(2,1)} %bitcast.13), channel_id=1, source_target_pairs={{0,1},{1,0},{2,3},{3,2},{4,5},{5,4},{6,7},{7,6},{8,9},{9,8},{10,11... | collective-permute-start | bytes 786440 | tf_op jit(solution)/shard_map/ppermute | solution.py:376
  2.8 12.3 %collective-permute-start.3 = (bf16[64,1024]{1,0:T(8,128)(2,1)}, bf16[64,1024]{1,0:T(8,128)(2,1)S(1)}, u32[]{:S(2)}, u32[]{:S(2)}) collective-permute-start(bf16[64,1024]{1,0:T(8,128)(2,1)} %cut_piece.1), channel_id=1, source_target_pairs={{0,4},{1,5},{2,6},{3,7},{4,0},{5,1},{6,2},{7,3},{8,12},{9,13},{10,... | collective-permute-start | bytes 393224 | tf_op jit(solution)/shard_map/ppermute | solution.py:376
  6.9 8.2 %collective-permute-start.2 = (bf16[64,1024]{1,0:T(8,128)(2,1)}, bf16[64,1024]{1,0:T(8,128)(2,1)S(1)}, u32[]{:S(2)}, u32[]{:S(2)}) collective-permute-start(bf16[64,1024]{1,0:T(8,128)(2,1)} %cut_piece.1), channel_id=1, source_target_pairs={{0,2},{1,3},{2,0},{3,1},{4,6},{5,7},{6,4},{7,5},{8,10},{9,11},{10,... | collective-permute-start | bytes 393224 | tf_op jit(solution)/shard_map/ppermute | solution.py:376
  8.4 11.0 %copy-start.12 = (bf16[64,1024]{1,0:T(8,128)(2,1)S(1)}, bf16[64,1024]{1,0:T(8,128)(2,1)}, u32[]{:S(2)}) copy-start(bf16[64,1024]{1,0:T(8,128)(2,1)} %cut_piece.1) | copy-start | bytes 393220
  8.4 13.1 %copy-start.1 = (bf16[128,8192]{1,0:T(8,128)(2,1)S(1)}, bf16[128,8192]{1,0:T(8,128)(2,1)}, u32[]{:S(2)}) copy-start(bf16[128,8192]{1,0:T(8,128)(2,1)} %refs_2_.5) | copy-start | bytes 6291460
  8.4 13.1 %copy-start.4 = (bf16[8192,64]{0,1:T(8,128)(2,1)S(1)}, bf16[8192,64]{0,1:T(8,128)(2,1)}, u32[]{:S(2)}) copy-start(bf16[8192,64]{0,1:T(8,128)(2,1)} %param.16) | copy-start | bytes 3145732
  8.4 13.1 %copy-start.11 = (s32[1,1,8]{2,1,0:T(1,128)S(1)}, s32[1,1,8]{2,1,0:T(1,128)}, u32[]{:S(2)}) copy-start(s32[1,1,8]{2,1,0:T(1,128)} %param.21) | copy-start | bytes 100
  15.8 10.4 %copy-start.6 = (bf16[1,128,1024]{2,1,0:T(8,128)(2,1)S(1)}, bf16[1,128,1024]{2,1,0:T(8,128)(2,1)}, u32[]{:S(2)}) copy-start(bf16[1,128,1024]{2,1,0:T(8,128)(2,1)} %param.18) | copy-start | bytes 786436
  15.9 10.4 %copy-start.7 = (bf16[1,128,1024]{2,1,0:T(8,128)(2,1)S(1)}, bf16[1,128,1024]{2,1,0:T(8,128)(2,1)}, u32[]{:S(2)}) copy-start(bf16[1,128,1024]{2,1,0:T(8,128)(2,1)} %param.19) | copy-start | bytes 786436
  15.9 10.4 %copy-start.10 = (s32[8]{0:T(128)S(1)}, s32[8]{0:T(128)}, u32[]{:S(2)}) copy-start(s32[8]{0:T(128)} %slots.7) | copy-start | bytes 100
  15.9 10.4 %copy-start = (f32[8192,128]{1,0:T(8,128)S(1)}, f32[8192,128]{1,0:T(8,128)}, u32[]{:S(2)}) copy-start(f32[8192,128]{1,0:T(8,128)} %refs_4_.3) | copy-start | bytes 12582916
  15.9 14.2 %collective-permute-start.7 = (bf16[144,1024]{1,0:T(8,128)(2,1)S(1)}, bf16[144,1024]{1,0:T(8,128)(2,1)S(1)}, u32[]{:S(2)}, u32[]{:S(2)}) collective-permute-start(bf16[144,1024]{1,0:T(8,128)(2,1)S(1)} %pack.1.first), channel_id=1, source_target_pairs={{0,24},{8,16},{16,8},{24,0},{1,25},{9,17},{17,9},{25,1},{2,26},{10... | collective-permute-start | bytes 884744 | tf_op jit(solution)/shard_map/ppermute | solution.py:376
  18.4 13.2 %collective-permute-start.6 = (bf16[144,1024]{1,0:T(8,128)(2,1)S(1)}, bf16[144,1024]{1,0:T(8,128)(2,1)S(1)}, u32[]{:S(2)}, u32[]{:S(2)}) collective-permute-start(bf16[144,1024]{1,0:T(8,128)(2,1)S(1)} %pack.1.first), channel_id=1, source_target_pairs={{0,16},{8,24},{16,0},{24,8},{1,17},{9,25},{17,1},{25,9},{2,18},{10... | collective-permute-start | bytes 884744 | tf_op jit(solution)/shard_map/ppermute | solution.py:376
  18.9 12.8 %collective-permute-start.5 = (bf16[144,1024]{1,0:T(8,128)(2,1)S(1)}, bf16[144,1024]{1,0:T(8,128)(2,1)S(1)}, u32[]{:S(2)}, u32[]{:S(2)}) collective-permute-start(bf16[144,1024]{1,0:T(8,128)(2,1)S(1)} %pack.1.first), channel_id=1, source_target_pairs={{0,8},{8,0},{16,24},{24,16},{1,9},{9,1},{17,25},{25,17},{2,10},{10... | collective-permute-start | bytes 884744 | tf_op jit(solution)/shard_map/ppermute | solution.py:376
  19.5 10.6 %collective-permute-start.4 = (bf16[64,1024]{1,0:T(8,128)(2,1)S(1)}, bf16[64,1024]{1,0:T(8,128)(2,1)S(1)}, u32[]{:S(2)}, u32[]{:S(2)}) collective-permute-start(bf16[64,1024]{1,0:T(8,128)(2,1)S(1)} %copy-done.12), channel_id=1, source_target_pairs={{0,6},{1,7},{2,4},{3,5},{4,2},{5,3},{6,0},{7,1},{8,14},{9,15},{10,... | collective-permute-start | bytes 393224 | tf_op jit(solution)/shard_map/ppermute | solution.py:376
  31.8 9.7 %collective-permute-start.8 = (bf16[4,144,1024]{2,1,0:T(8,128)(2,1)S(1)}, bf16[4,144,1024]{2,1,0:T(8,128)(2,1)S(1)}, u32[]{:S(2)}, u32[]{:S(2)}) collective-permute-start(bf16[4,144,1024]{2,1,0:T(8,128)(2,1)S(1)} %order.2.refs_0_.own), channel_id=1, source_target_pairs={{0,1},{1,0},{2,3},{3,2},{4,5},{5,4},{6,7},{7,6},{8,9},{9,8},{10,11... | collective-permute-start | bytes 3538952 | tf_op jit(solution)/shard_map/ppermute | solution.py:376
  31.9 7.4 %collective-permute-start.11 = (bf16[64,1024]{1,0:T(8,128)(2,1)S(1)}, bf16[64,1024]{1,0:T(8,128)(2,1)S(1)}, u32[]{:S(2)}, u32[]{:S(2)}) collective-permute-start(bf16[64,1024]{1,0:T(8,128)(2,1)S(1)} %collective-permute-done.4.first), channel_id=1, source_target_pairs={{0,24},{8,16},{16,8},{24,0},{1,25},{9,17},{17,9},{25,1},{2,26},{10... | collective-permute-start | bytes 393224 | tf_op jit(solution)/shard_map/ppermute | solution.py:376
  33.6 7.9 %collective-permute-start.10 = (bf16[64,1024]{1,0:T(8,128)(2,1)S(1)}, bf16[64,1024]{1,0:T(8,128)(2,1)S(1)}, u32[]{:S(2)}, u32[]{:S(2)}) collective-permute-start(bf16[64,1024]{1,0:T(8,128)(2,1)S(1)} %collective-permute-done.4.first), channel_id=1, source_target_pairs={{0,16},{8,24},{16,0},{24,8},{1,17},{9,25},{17,1},{25,9},{2,18},{10... | collective-permute-start | bytes 393224 | tf_op jit(solution)/shard_map/ppermute | solution.py:376
  34.9 6.6 %collective-permute-start.9 = (bf16[64,1024]{1,0:T(8,128)(2,1)S(1)}, bf16[64,1024]{1,0:T(8,128)(2,1)S(1)}, u32[]{:S(2)}, u32[]{:S(2)}) collective-permute-start(bf16[64,1024]{1,0:T(8,128)(2,1)S(1)} %collective-permute-done.4.first), channel_id=1, source_target_pairs={{0,8},{8,0},{16,24},{24,16},{1,9},{9,1},{17,25},{25,17},{2,10},{10... | collective-permute-start | bytes 393224 | tf_op jit(solution)/shard_map/ppermute | solution.py:376
  41.6 9.9 %copy-start.8 = (f32[128,64]{0,1:T(8,128)S(1)}, f32[128,64]{0,1:T(8,128)}, u32[]{:S(2)}) copy-start(f32[128,64]{0,1:T(8,128)} %param.22) | copy-start | bytes 98308
  41.6 9.9 %collective-permute-start.12 = (bf16[4,64,1024]{2,1,0:T(8,128)(2,1)S(1)}, bf16[4,64,1024]{2,1,0:T(8,128)(2,1)S(1)}, u32[]{:S(2)}, u32[]{:S(2)}) collective-permute-start(bf16[4,64,1024]{2,1,0:T(8,128)(2,1)S(1)} %order.3.refs_0_), channel_id=1, source_target_pairs={{0,1},{1,0},{2,3},{3,2},{4,5},{5,4},{6,7},{7,6},{8,9},{9,8},{10,11... | collective-permute-start | bytes 1572872 | tf_op jit(solution)/shard_map/ppermute | solution.py:376
  41.7 4.5 %collective-permute-start.13 = (f32[64,128]{1,0:T(8,128)S(1)}, f32[64,128]{1,0:T(8,128)S(1)}, u32[]{:S(2)}, u32[]{:S(2)}) collective-permute-start(f32[64,128]{1,0:T(8,128)S(1)} %plane_sum.1), channel_id=1, source_target_pairs={{0,2},{1,3},{2,0},{3,1},{4,6},{5,7},{6,4},{7,5},{8,10},{9,11},{10,... | collective-permute-start | bytes 98312 | tf_op jit(solution)/shard_map/ppermute | solution.py:376
  46.3 5.2 %collective-permute-start.14 = (f32[64,128]{1,0:T(8,128)S(1)}, f32[64,128]{1,0:T(8,128)S(1)}, u32[]{:S(2)}, u32[]{:S(2)}) collective-permute-start(f32[64,128]{1,0:T(8,128)S(1)} %add.3.refs_8_), channel_id=1, source_target_pairs={{0,4},{1,5},{2,6},{3,7},{4,0},{5,1},{6,2},{7,3},{8,12},{9,13},{10,... | collective-permute-start | bytes 98312 | tf_op jit(solution)/shard_map/ppermute | solution.py:376
  (4 other events, 5.5 us)

commit v9 on v7

--- a/solution.py
+++ b/solution.py
@@ -15,6 +15,7 @@
 TN = (((0,), (0,)), ((), ()))
 NT = (((1,), (1,)), ((), ()))
 VMEM_LIMIT = 60 * 1024 * 1024
+VALIDATION_LIMIT = 57 * 1024 * 1024
 CHUNK_LIMIT = 24 * 1024 * 1024
 ANY = pl.BlockSpec(memory_space=pl.ANY)
 SMEM = pl.BlockSpec(memory_space=pltpu.SMEM)
@@ -193,7 +194,7 @@
             *(pltpu.VMEM(a.shape, a.dtype) for a in (xv, gv, down_t, up, columns)),
             pltpu.SemaphoreType.DMA((4 + PARTS,)),
         ],
-        compiler_params=pltpu.CompilerParams(vmem_limit_bytes=VMEM_LIMIT),
+        compiler_params=pltpu.CompilerParams(vmem_limit_bytes=VALIDATION_LIMIT),
         cost_estimate=pl.CostEstimate(flops=10**6, bytes_accessed=10**6, transcendentals=0),
         name="validation",
     )(xv, gv, down_t, up, columns, rows_t)

time: 53.8 us -> 53.8 us (level)
  local copies, waits for them, and re-layouts: 3.6 us -> 0.81 us
  waiting for transfers between devices: 4.88 us -> 7.52 us
    unnamed x26 -> x24, local copies, waits for them, and re-layouts: 3.6 us -> 0.81 us
    ppermute x15, waiting for transfers between devices: 4.88 us -> 7.52 us  [exchange(): return lax.ppermute(value, axis, [(i, i ^ bits) for i in range(size)])]
  transfers between devices with their start and end apart: 15 -> 15, of which waited for: 2 -> 3; matrix products, arithmetic and copies ran while one was open for 0% -> 0% of each run, Pallas kernels for 40% -> 41%
where the time goes in v9:
time: 53.8 us; the launch traced here: 53.6 us
  Pallas kernels  27.4 us (51%)
  starting transfers between devices  16.8 us (31%)
  waiting for transfers between devices  7.52 us (14%)
  between operations  1.04 us (2%)
  local copies, waits for them, and re-layouts  0.81 us (2%)
    ppermute x15, starting transfers between devices, exchange(): return lax.ppermute(value, axis, [(i, i ^ bits) for i in range(size)])  16.8 us
    pallas_call x3, Pallas kernels, chunk(): pl.pallas_call(functools.partial(chunk_kernel, blocks, len(moments)), in_...  11.6 us
    ppermute x15, waiting for transfers between devices, exchange(): return lax.ppermute(value, axis, [(i, i ^ bits) for i in range(size)])  7.52 us
    pallas_call x1, Pallas kernels, validation(): pl.pallas_call(validation_kernel, in_specs=[ANY] * 5 + [VMEM], out_specs=...  6.79 us
    pallas_call x1, Pallas kernels, chunk(): pl.pallas_call(functools.partial(last_kernel, blocks, len(moments), len(v...  5.39 us
    pallas_call x1, Pallas kernels, prepare(): pl.pallas_call(prepare_kernel, in_specs=[SMEM] + [VMEM] * 4, out_specs=[V...  1.84 us
    pallas_call x1, Pallas kernels, cut_piece(): pl.pallas_call(cut_kernel, in_specs=[ANY, ANY], out_specs=VMEM, out_shape...  1.54 us
  transfers between devices with their start and end apart: 15, of which 3 were waited for; matrix products, arithmetic and copies ran while one was open for 0% of the time, Pallas kernels for 41%

profile of v9, /device:TPU:0, one launch (start us, length us, event | category | flops | bytes accessed | tf_op | source)
XLA Modules:
  0.0 53.6 jit_solution(15940270875598133711)
XLA Ops:
  0.6 0.5 collective-permute-start
  1.2 1.5 %cut_piece.1 = bf16[64,1024]{1,0:T(8,128)(2,1)} custom-call(bf16[4,32,1024]{2,1,0:T(8,128)(2,1)} %bitcast.11, bf16[4,32,1024]{2,1,0:T(8,128)(2,1)} %bitcast.14), custom_call_target="tpu_custom_call" | custom-call | tf_op jit(solution)/shard_map/cut_piece/pallas_call | solution.py:49
  2.8 3.1 %collective-permute-start.2 = (bf16[64,1024]{1,0:T(8,128)(2,1)}, bf16[64,1024]{1,0:T(8,128)(2,1)S(1)}, u32[]{:S(2)}, u32[]{:S(2)}) collective-permute-start(bf16[64,1024]{1,0:T(8,128)(2,1)} %cut_piece.1), channel_id=1, source_target_pairs={{0,2},{1,3},{2,0},{3,1},{4,6},{5,7},{6,4},{7,5},{8,10},{9,11},{10,... | collective-permute-start | bytes 393224 | tf_op jit(solution)/shard_map/ppermute | solution.py:387
  5.8 2.6 %collective-permute-start.3 = (bf16[64,1024]{1,0:T(8,128)(2,1)}, bf16[64,1024]{1,0:T(8,128)(2,1)S(1)}, u32[]{:S(2)}, u32[]{:S(2)}) collective-permute-start(bf16[64,1024]{1,0:T(8,128)(2,1)} %cut_piece.1), channel_id=1, source_target_pairs={{0,4},{1,5},{2,6},{3,7},{4,0},{5,1},{6,2},{7,3},{8,12},{9,13},{10,... | collective-permute-start | bytes 393224 | tf_op jit(solution)/shard_map/ppermute | solution.py:387
  8.5 6.8 %validation.1.val = f32[64,128]{1,0:T(8,128)} custom-call(bf16[32,8192]{1,0:T(8,128)(2,1)} %xv, bf16[32,8192]{1,0:T(8,128)(2,1)} %gv.1, bf16[64,8192]{1,0:T(8,128)(2,1)} %bitcast.8, bf16[64,8192]{1,0:T(8,128)(2,1)} %up.3, f32[8192,128]{1,0:T(8,128)} %refs_3_.5, f32[64,128]{1,0:T(8,128)} %bitcast.16), custom_call_target="tpu_custom_call" | custom-call | flops 1000000 | bytes 1000000 | tf_op jit(solution)/shard_map/validation/pallas_call | solution.py:188
  15.3 0.7 %copy-done.8 = f32[64,128]{1,0:T(8,128)S(1)} copy-done((f32[64,128]{1,0:T(8,128)S(1)}, f32[64,128]{1,0:T(8,128)}, u32[]{:S(2)}) %copy-start.8) | copy-done | bytes 32792
  16.1 1.6 %collective-permute-start.5 = (bf16[80,1024]{1,0:T(8,128)(2,1)S(1)}, bf16[80,1024]{1,0:T(8,128)(2,1)S(1)}, u32[]{:S(2)}, u32[]{:S(2)}) collective-permute-start(bf16[80,1024]{1,0:T(8,128)(2,1)S(1)} %pack.1.first), channel_id=1, source_target_pairs={{0,8},{8,0},{16,24},{24,16},{1,9},{9,1},{17,25},{25,17},{2,10},{10... | collective-permute-start | bytes 491528 | tf_op jit(solution)/shard_map/ppermute | solution.py:387
  17.7 1.5 %collective-permute-start.6 = (bf16[80,1024]{1,0:T(8,128)(2,1)S(1)}, bf16[80,1024]{1,0:T(8,128)(2,1)S(1)}, u32[]{:S(2)}, u32[]{:S(2)}) collective-permute-start(bf16[80,1024]{1,0:T(8,128)(2,1)S(1)} %pack.1.first), channel_id=1, source_target_pairs={{0,16},{8,24},{16,0},{24,8},{1,17},{9,25},{17,1},{25,9},{2,18},{10... | collective-permute-start | bytes 491528 | tf_op jit(solution)/shard_map/ppermute | solution.py:387
  19.2 0.5 collective-permute-start.7
  19.7 2.2 %collective-permute-start.4 = (bf16[64,1024]{1,0:T(8,128)(2,1)S(1)}, bf16[64,1024]{1,0:T(8,128)(2,1)S(1)}, u32[]{:S(2)}, u32[]{:S(2)}) collective-permute-start(bf16[64,1024]{1,0:T(8,128)(2,1)S(1)} %copy-done.11), channel_id=1, source_target_pairs={{0,6},{1,7},{2,4},{3,5},{4,2},{5,3},{6,0},{7,1},{8,14},{9,15},{10,... | collective-permute-start | bytes 393224 | tf_op jit(solution)/shard_map/ppermute | solution.py:387
  21.9 1.8 %prepare.1 = (bf16[512,128]{1,0:T(8,128)(2,1)S(1)}, bf16[512,128]{1,0:T(8,128)(2,1)S(1)}) custom-call(s32[8]{0:T(128)S(1)} %bitcast.18, bf16[128,8192]{1,0:T(8,128)(2,1)S(1)} %copy-done.1, bf16[128,8192]{1,0:T(8,128)(2,1)S(1)} %copy-done.2, bf16[64,8192]{1,0:T(8,128)(2,1)S(1)} %bitcast.9, bf16[64,8192]{1,0:T(8,128)(2,1)S(1)} %copy-done.4), custom_call_target="tpu_custom_call" | custom-call | flops 1000000 | bytes 1000000 | tf_op jit(solution)/shard_map/prepare/pallas_call | solution.py:205
  23.7 2.8 %collective-permute-done.4.second = bf16[64,1024]{1,0:T(8,128)(2,1)S(1)} collective-permute-done((bf16[64,1024]{1,0:T(8,128)(2,1)S(1)}, bf16[64,1024]{1,0:T(8,128)(2,1)S(1)}, u32[]{:S(2)}, u32[]{:S(2)}) %collective-permute-start.4) | collective-permute-done | bytes 131104 | tf_op jit(solution)/shard_map/ppermute | solution.py:387
  26.7 1.6 %collective-permute-start.10 = (bf16[128,1024]{1,0:T(8,128)(2,1)S(1)}, bf16[128,1024]{1,0:T(8,128)(2,1)S(1)}, u32[]{:S(2)}, u32[]{:S(2)}) collective-permute-start(bf16[128,1024]{1,0:T(8,128)(2,1)S(1)} %join.1.first), channel_id=1, source_target_pairs={{0,8},{8,0},{16,24},{24,16},{1,9},{9,1},{17,25},{25,17},{2,10},{10... | collective-permute-start | bytes 786440 | tf_op jit(solution)/shard_map/ppermute | solution.py:387
  28.3 1.5 %collective-permute-start.11 = (bf16[128,1024]{1,0:T(8,128)(2,1)S(1)}, bf16[128,1024]{1,0:T(8,128)(2,1)S(1)}, u32[]{:S(2)}, u32[]{:S(2)}) collective-permute-start(bf16[128,1024]{1,0:T(8,128)(2,1)S(1)} %join.1.first), channel_id=1, source_target_pairs={{0,16},{8,24},{16,0},{24,8},{1,17},{9,25},{17,1},{25,9},{2,18},{10... | collective-permute-start | bytes 786440 | tf_op jit(solution)/shard_map/ppermute | solution.py:387
  29.8 0.5 collective-permute-start.12
  30.3 3.8 %chunk.3.refs_9_ = f32[2,576,128]{2,1,0:T(8,128)S(1)} custom-call(s32[8]{0:T(128)S(1)} %copy-done.9, bf16[4,32,1024]{2,1,0:T(8,128)(2,1)S(1)} %bitcast.12, bf16[4,32,1024]{2,1,0:T(8,128)(2,1)S(1)} %bitcast.15, bf16[4,32,1024]{2,1,0:T(8,128)(2,1)S(1)} %collective-permute-done.refs_2_, bf16[4,32,1024]{2,1,0:T(8,128)(2,1)S(1)} %collective-permute-done.1.refs_3_, ...), custom_call_target="tpu_custom_call" | custom-call | flops 1000000 | bytes 1000000 | tf_op jit(solution)/shard_map/chunk/pallas_call | solution.py:339
  34.2 1.0 %collective-permute-start.9 = (f32[64,128]{1,0:T(8,128)S(1)}, f32[64,128]{1,0:T(8,128)S(1)}, u32[]{:S(2)}, u32[]{:S(2)}) collective-permute-start(f32[64,128]{1,0:T(8,128)S(1)} %plane_sum.1), channel_id=1, source_target_pairs={{0,2},{1,3},{2,0},{3,1},{4,6},{5,7},{6,4},{7,5},{8,10},{9,11},{10,... | collective-permute-start | bytes 98312 | tf_op jit(solution)/shard_map/ppermute | solution.py:387
  35.2 3.8 %chunk.4.refs_10_ = f32[2,576,128]{2,1,0:T(8,128)S(1)} custom-call(s32[8]{0:T(128)S(1)} %copy-done.9, bf16[4,80,1024]{2,1,0:T(8,128)(2,1)S(1)} %order.2.own.refs_0_, bf16[4,80,1024]{2,1,0:T(8,128)(2,1)S(1)} %collective-permute-done.8.crossed.refs_1_, bf16[128,8192]{1,0:T(8,128)(2,1)S(1)} %copy-done.1, bf16[128,8192]{1,0:T(8,128)(2,1)S(1)} %copy-done.2, ...), custom_call_target="tpu_custom_call" | custom-call | flops 1000000 | bytes 1000000 | tf_op jit(solution)/shard_map/chunk/pallas_call | solution.py:339
  39.0 3.3 %collective-permute-done.11.third = bf16[128,1024]{1,0:T(8,128)(2,1)S(1)} collective-permute-done((bf16[128,1024]{1,0:T(8,128)(2,1)S(1)}, bf16[128,1024]{1,0:T(8,128)(2,1)S(1)}, u32[]{:S(2)}, u32[]{:S(2)}) %collective-permute-start.11) | collective-permute-done | bytes 262176 | tf_op jit(solution)/shard_map/ppermute | solution.py:387
  42.4 0.1 order.3.refs_0_
  42.5 0.1 collective-permute-start.14
  42.6 4.0 %chunk.5.refs_11_ = f32[2,576,128]{2,1,0:T(8,128)S(1)} custom-call(s32[8]{0:T(128)S(1)} %copy-done.9, bf16[4,128,1024]{2,1,0:T(8,128)(2,1)S(1)} %order.3.refs_0_, bf16[128,8192]{1,0:T(8,128)(2,1)S(1)} %copy-done.1, bf16[128,8192]{1,0:T(8,128)(2,1)S(1)} %copy-done.2, f32[8192,128]{1,0:T(8,128)S(1)} %copy-done, ...), custom_call_target="tpu_custom_call" | custom-call | flops 1000000 | bytes 1000000 | tf_op jit(solution)/shard_map/chunk/pallas_call | solution.py:339
  46.7 1.3 %collective-permute-done.14.refs_8_ = f32[64,128]{1,0:T(8,128)S(1)} collective-permute-done((f32[64,128]{1,0:T(8,128)S(1)}, f32[64,128]{1,0:T(8,128)S(1)}, u32[]{:S(2)}, u32[]{:S(2)}) %collective-permute-start.14) | collective-permute-done | bytes 32800 | tf_op jit(solution)/shard_map/ppermute | solution.py:387
  48.0 5.4 %last_chunk.1 = (f32[8,8192]{1,0:T(8,128)}, f32[64,128]{1,0:T(8,128)}, f32[8]{0:T(128)}) custom-call(s32[8]{0:T(128)S(1)} %copy-done.9, bf16[4,128,1024]{2,1,0:T(8,128)(2,1)S(1)} %collective-permute-done.13.refs_0_, bf16[128,8192]{1,0:T(8,128)(2,1)S(1)} %copy-done.1, bf16[128,8192]{1,0:T(8,128)(2,1)S(1)} %copy-done.2, f32[8192,128]{1,0:T(8,128)S(1)} %copy-done, ...), custom_call_target="tpu_custom_call" | custom-call | flops 1000000 | bytes 1000000 | tf_op jit(solution)/shard_map/last_chunk/pallas_call | solution.py:350
  (43 shorter events, 0.5 us)
Async XLA Ops:
  0.6 14.7 %collective-permute-start = (bf16[4,32,1024]{2,1,0:T(8,128)(2,1)}, bf16[4,32,1024]{2,1,0:T(8,128)(2,1)S(1)}, u32[]{:S(2)}, u32[]{:S(2)}) collective-permute-start(bf16[4,32,1024]{2,1,0:T(8,128)(2,1)} %bitcast.10), channel_id=1, source_target_pairs={{0,1},{1,0},{2,3},{3,2},{4,5},{5,4},{6,7},{7,6},{8,9},{9,8},{10,11... | collective-permute-start | bytes 786440 | tf_op jit(solution)/shard_map/ppermute | solution.py:387
  1.1 14.2 %collective-permute-start.1 = (bf16[4,32,1024]{2,1,0:T(8,128)(2,1)}, bf16[4,32,1024]{2,1,0:T(8,128)(2,1)S(1)}, u32[]{:S(2)}, u32[]{:S(2)}) collective-permute-start(bf16[4,32,1024]{2,1,0:T(8,128)(2,1)} %bitcast.13), channel_id=1, source_target_pairs={{0,1},{1,0},{2,3},{3,2},{4,5},{5,4},{6,7},{7,6},{8,9},{9,8},{10,11... | collective-permute-start | bytes 786440 | tf_op jit(solution)/shard_map/ppermute | solution.py:387
  2.8 12.5 %collective-permute-start.2 = (bf16[64,1024]{1,0:T(8,128)(2,1)}, bf16[64,1024]{1,0:T(8,128)(2,1)S(1)}, u32[]{:S(2)}, u32[]{:S(2)}) collective-permute-start(bf16[64,1024]{1,0:T(8,128)(2,1)} %cut_piece.1), channel_id=1, source_target_pairs={{0,2},{1,3},{2,0},{3,1},{4,6},{5,7},{6,4},{7,5},{8,10},{9,11},{10,... | collective-permute-start | bytes 393224 | tf_op jit(solution)/shard_map/ppermute | solution.py:387
  5.8 9.4 %collective-permute-start.3 = (bf16[64,1024]{1,0:T(8,128)(2,1)}, bf16[64,1024]{1,0:T(8,128)(2,1)S(1)}, u32[]{:S(2)}, u32[]{:S(2)}) collective-permute-start(bf16[64,1024]{1,0:T(8,128)(2,1)} %cut_piece.1), channel_id=1, source_target_pairs={{0,4},{1,5},{2,6},{3,7},{4,0},{5,1},{6,2},{7,3},{8,12},{9,13},{10,... | collective-permute-start | bytes 393224 | tf_op jit(solution)/shard_map/ppermute | solution.py:387
  8.4 11.2 %copy-start.11 = (bf16[64,1024]{1,0:T(8,128)(2,1)S(1)}, bf16[64,1024]{1,0:T(8,128)(2,1)}, u32[]{:S(2)}) copy-start(bf16[64,1024]{1,0:T(8,128)(2,1)} %cut_piece.1) | copy-start | bytes 393220
  8.4 13.4 %copy-start.1 = (bf16[128,8192]{1,0:T(8,128)(2,1)S(1)}, bf16[128,8192]{1,0:T(8,128)(2,1)}, u32[]{:S(2)}) copy-start(bf16[128,8192]{1,0:T(8,128)(2,1)} %refs_1_.3) | copy-start | bytes 6291460
  8.4 13.4 %copy-start.2 = (bf16[128,8192]{1,0:T(8,128)(2,1)S(1)}, bf16[128,8192]{1,0:T(8,128)(2,1)}, u32[]{:S(2)}) copy-start(bf16[128,8192]{1,0:T(8,128)(2,1)} %refs_2_.5) | copy-start | bytes 6291460
  8.4 13.4 %copy-start.3 = (bf16[8192,64]{0,1:T(8,128)(2,1)S(1)}, bf16[8192,64]{0,1:T(8,128)(2,1)}, u32[]{:S(2)}) copy-start(bf16[8192,64]{0,1:T(8,128)(2,1)} %param.16) | copy-start | bytes 3145732
  8.4 13.4 %copy-start.4 = (bf16[64,8192]{1,0:T(8,128)(2,1)S(1)}, bf16[64,8192]{1,0:T(8,128)(2,1)}, u32[]{:S(2)}) copy-start(bf16[64,8192]{1,0:T(8,128)(2,1)} %up.3) | copy-start | bytes 3145732
  8.5 13.4 %copy-start.10 = (s32[1,1,8]{2,1,0:T(1,128)S(1)}, s32[1,1,8]{2,1,0:T(1,128)}, u32[]{:S(2)}) copy-start(s32[1,1,8]{2,1,0:T(1,128)} %param.21) | copy-start | bytes 100
  16.1 14.2 %copy-start.5 = (bf16[1,128,1024]{2,1,0:T(8,128)(2,1)S(1)}, bf16[1,128,1024]{2,1,0:T(8,128)(2,1)}, u32[]{:S(2)}) copy-start(bf16[1,128,1024]{2,1,0:T(8,128)(2,1)} %param.18) | copy-start | bytes 786436
  16.1 14.2 %copy-start.6 = (bf16[1,128,1024]{2,1,0:T(8,128)(2,1)S(1)}, bf16[1,128,1024]{2,1,0:T(8,128)(2,1)}, u32[]{:S(2)}) copy-start(bf16[1,128,1024]{2,1,0:T(8,128)(2,1)} %param.19) | copy-start | bytes 786436
  16.1 14.2 %copy-start.9 = (s32[8]{0:T(128)S(1)}, s32[8]{0:T(128)}, u32[]{:S(2)}) copy-start(s32[8]{0:T(128)} %slots.7) | copy-start | bytes 100
  16.1 10.4 %collective-permute-start.5 = (bf16[80,1024]{1,0:T(8,128)(2,1)S(1)}, bf16[80,1024]{1,0:T(8,128)(2,1)S(1)}, u32[]{:S(2)}, u32[]{:S(2)}) collective-permute-start(bf16[80,1024]{1,0:T(8,128)(2,1)S(1)} %pack.1.first), channel_id=1, source_target_pairs={{0,8},{8,0},{16,24},{24,16},{1,9},{9,1},{17,25},{25,17},{2,10},{10... | collective-permute-start | bytes 491528 | tf_op jit(solution)/shard_map/ppermute | solution.py:387
  17.7 8.9 %collective-permute-start.6 = (bf16[80,1024]{1,0:T(8,128)(2,1)S(1)}, bf16[80,1024]{1,0:T(8,128)(2,1)S(1)}, u32[]{:S(2)}, u32[]{:S(2)}) collective-permute-start(bf16[80,1024]{1,0:T(8,128)(2,1)S(1)} %pack.1.first), channel_id=1, source_target_pairs={{0,16},{8,24},{16,0},{24,8},{1,17},{9,25},{17,1},{25,9},{2,18},{10... | collective-permute-start | bytes 491528 | tf_op jit(solution)/shard_map/ppermute | solution.py:387
  19.2 7.4 %collective-permute-start.7 = (bf16[80,1024]{1,0:T(8,128)(2,1)S(1)}, bf16[80,1024]{1,0:T(8,128)(2,1)S(1)}, u32[]{:S(2)}, u32[]{:S(2)}) collective-permute-start(bf16[80,1024]{1,0:T(8,128)(2,1)S(1)} %pack.1.first), channel_id=1, source_target_pairs={{0,24},{8,16},{16,8},{24,0},{1,25},{9,17},{17,9},{25,1},{2,26},{10... | collective-permute-start | bytes 491528 | tf_op jit(solution)/shard_map/ppermute | solution.py:387
  19.7 6.9 %collective-permute-start.4 = (bf16[64,1024]{1,0:T(8,128)(2,1)S(1)}, bf16[64,1024]{1,0:T(8,128)(2,1)S(1)}, u32[]{:S(2)}, u32[]{:S(2)}) collective-permute-start(bf16[64,1024]{1,0:T(8,128)(2,1)S(1)} %copy-done.11), channel_id=1, source_target_pairs={{0,6},{1,7},{2,4},{3,5},{4,2},{5,3},{6,0},{7,1},{8,14},{9,15},{10,... | collective-permute-start | bytes 393224 | tf_op jit(solution)/shard_map/ppermute | solution.py:387
  26.6 7.5 %collective-permute-start.8 = (bf16[4,80,1024]{2,1,0:T(8,128)(2,1)S(1)}, bf16[4,80,1024]{2,1,0:T(8,128)(2,1)S(1)}, u32[]{:S(2)}, u32[]{:S(2)}) collective-permute-start(bf16[4,80,1024]{2,1,0:T(8,128)(2,1)S(1)} %order.2.own.refs_0_), channel_id=1, source_target_pairs={{0,1},{1,0},{2,3},{3,2},{4,5},{5,4},{6,7},{7,6},{8,9},{9,8},{10,11... | collective-permute-start | bytes 1966088 | tf_op jit(solution)/shard_map/ppermute | solution.py:387
  26.7 12.3 %collective-permute-start.10 = (bf16[128,1024]{1,0:T(8,128)(2,1)S(1)}, bf16[128,1024]{1,0:T(8,128)(2,1)S(1)}, u32[]{:S(2)}, u32[]{:S(2)}) collective-permute-start(bf16[128,1024]{1,0:T(8,128)(2,1)S(1)} %join.1.first), channel_id=1, source_target_pairs={{0,8},{8,0},{16,24},{24,16},{1,9},{9,1},{17,25},{25,17},{2,10},{10... | collective-permute-start | bytes 786440 | tf_op jit(solution)/shard_map/ppermute | solution.py:387
  28.3 14.0 %collective-permute-start.11 = (bf16[128,1024]{1,0:T(8,128)(2,1)S(1)}, bf16[128,1024]{1,0:T(8,128)(2,1)S(1)}, u32[]{:S(2)}, u32[]{:S(2)}) collective-permute-start(bf16[128,1024]{1,0:T(8,128)(2,1)S(1)} %join.1.first), channel_id=1, source_target_pairs={{0,16},{8,24},{16,0},{24,8},{1,17},{9,25},{17,1},{25,9},{2,18},{10... | collective-permute-start | bytes 786440 | tf_op jit(solution)/shard_map/ppermute | solution.py:387
  29.8 12.5 %collective-permute-start.12 = (bf16[128,1024]{1,0:T(8,128)(2,1)S(1)}, bf16[128,1024]{1,0:T(8,128)(2,1)S(1)}, u32[]{:S(2)}, u32[]{:S(2)}) collective-permute-start(bf16[128,1024]{1,0:T(8,128)(2,1)S(1)} %join.1.first), channel_id=1, source_target_pairs={{0,24},{8,16},{16,8},{24,0},{1,25},{9,17},{17,9},{25,1},{2,26},{10... | collective-permute-start | bytes 786440 | tf_op jit(solution)/shard_map/ppermute | solution.py:387
  34.2 8.2 %collective-permute-start.9 = (f32[64,128]{1,0:T(8,128)S(1)}, f32[64,128]{1,0:T(8,128)S(1)}, u32[]{:S(2)}, u32[]{:S(2)}) collective-permute-start(f32[64,128]{1,0:T(8,128)S(1)} %plane_sum.1), channel_id=1, source_target_pairs={{0,2},{1,3},{2,0},{3,1},{4,6},{5,7},{6,4},{7,5},{8,10},{9,11},{10,... | collective-permute-start | bytes 98312 | tf_op jit(solution)/shard_map/ppermute | solution.py:387
  42.5 5.6 %collective-permute-start.13 = (bf16[4,128,1024]{2,1,0:T(8,128)(2,1)S(1)}, bf16[4,128,1024]{2,1,0:T(8,128)(2,1)S(1)}, u32[]{:S(2)}, u32[]{:S(2)}) collective-permute-start(bf16[4,128,1024]{2,1,0:T(8,128)(2,1)S(1)} %order.3.refs_0_), channel_id=1, source_target_pairs={{0,1},{1,0},{2,3},{3,2},{4,5},{5,4},{6,7},{7,6},{8,9},{9,8},{10,11... | collective-permute-start | bytes 3145736 | tf_op jit(solution)/shard_map/ppermute | solution.py:387
  42.5 5.5 %collective-permute-start.14 = (f32[64,128]{1,0:T(8,128)S(1)}, f32[64,128]{1,0:T(8,128)S(1)}, u32[]{:S(2)}, u32[]{:S(2)}) collective-permute-start(f32[64,128]{1,0:T(8,128)S(1)} %add.3.refs_7_), channel_id=1, source_target_pairs={{0,4},{1,5},{2,6},{3,7},{4,0},{5,1},{6,2},{7,3},{8,12},{9,13},{10,... | collective-permute-start | bytes 98312 | tf_op jit(solution)/shard_map/ppermute | solution.py:387
  (3 other events, 14.7 us)
